TPU v7x, 512 devices: a whole 4x4x16 slice. The times are simulated.
512 devices in a mesh: row: 16 (over y, x_lo, core), col: 32 (over x_hi, z).
Axes of the slice: x: 4 (x_hi: 2, x_lo: 2; x = x_hi * 2 + x_lo), y: 4, z: 16, core: 2. Of those that a mesh axis runs over, the one named last changes fastest.
Arguments:
- image_embed: bfloat16 [163840, 1152], P(('row', 'col')), as said below
- text_embed: bfloat16 [163840, 1152], P(('row', 'col')), as said below
Outputs:
- row_loss: float32 [163840], P(('row', 'col'))
- image_grad: float32 [163840, 1152], P(('row', 'col'))
- text_grad: float32 [163840, 1152], P(('row', 'col'))
Inputs may be any that keep to these rules, and one draw needn't show every extreme that they name: `image_embed`: no row is zero. `text_embed`: no row is zero.
All inputs are finite; a program needn't handle non-finite values.
Results may differ from a plain program's by a relative error of at most 0.0048.
Values may be sent and summed in bfloat16 or wider, within the bound.
No kernel may reach another device: no remote copies, remote signals or barrier semaphores. Data moves between devices by JAX's collectives and lax.ppermute only.
A program may use at most 64 MiB of HBM per device.

v0:
```python
import jax
import jax.numpy as jnp
from jax import lax
from jax.sharding import PartitionSpec as P

LOGIT_SCALE = 8.0
LOGIT_BIAS = -4.0
EPSILON = 1e-06
CONTRACT_ROWS = (((0,), (0,)), ((), ()))


def partner(value, axis, bit):
    mask = 2**bit
    pairs = [(source, source ^ mask) for source in range(lax.axis_size(axis))]
    return lax.ppermute(value, axis, pairs)


def normalize_rows(raw_rows):
    widened = raw_rows.astype(jnp.float32)
    inverse = lax.rsqrt(jnp.sum(widened * widened, axis=1, keepdims=True) + EPSILON)
    return (widened * inverse, inverse)


def logit_block(left_rows, right_rows):
    product = lax.dot_general(
        left_rows, right_rows, (((1,), (1,)), ((), ())), preferred_element_type=jnp.float32
    )
    return LOGIT_SCALE * product + LOGIT_BIAS


def raw_gradient(normed, inverse, gradient):
    return inverse * (gradient - normed * jnp.sum(normed * gradient, axis=1, keepdims=True))


def move_text(held_text, axis_name, bit_index):
    if axis_name == "col":
        return partner(held_text, "col", bit_index)
    return partner(held_text, "row", bit_index)


def send_home(text_share, path_bits):
    col_steps = [step_bit for step_bit in path_bits if step_bit[0] == "col"]
    row_steps = [step_bit for step_bit in path_bits if step_bit[0] == "row"]
    ordered = col_steps + row_steps
    for axis_name, bit_index in ordered:
        if axis_name == "col":
            text_share = partner(text_share, "col", bit_index)
        else:
            text_share = partner(text_share, "row", bit_index)
    return text_share


def toggle_step(path_bits, step_bit):
    if step_bit in path_bits:
        return [entry for entry in path_bits if entry != step_bit]
    return path_bits + [step_bit]


def shards(image_embed, text_embed):
    row_count = image_embed.shape[0]
    image_unit, image_inverse = normalize_rows(image_embed)
    text_unit, text_inverse = normalize_rows(text_embed)
    own_image = image_unit.astype(jnp.bfloat16)
    own_text = text_unit.astype(jnp.bfloat16)
    row_index = lax.broadcasted_iota(jnp.int32, (row_count, row_count), 0)
    column_index = lax.broadcasted_iota(jnp.int32, (row_count, row_count), 1)
    identity = (row_index == column_index).astype(jnp.float32)
    top_bit = lax.axis_size("col").bit_length() - 2
    walk_steps = (("col", 0), ("row", 0), ("col", 0), ("col", top_bit), ("col", 0), ("row", 0))
    forward = logit_block(own_image, own_text)
    row_losses = jnp.sum(jnp.log1p(jnp.exp(forward)) - identity * forward, axis=1)
    weights = (jax.nn.sigmoid(forward) - identity).astype(jnp.bfloat16)
    image_total = LOGIT_SCALE * jnp.dot(weights, own_text, preferred_element_type=jnp.float32)
    text_share = (
        LOGIT_SCALE
        * lax.dot_general(weights, own_image, CONTRACT_ROWS, preferred_element_type=jnp.float32)
    ).astype(jnp.bfloat16)
    text_total = lax.optimization_barrier(text_share).astype(jnp.float32)
    held_text = own_text
    path_bits = []
    for axis_name, bit_index in walk_steps:
        held_text = move_text(held_text, axis_name, bit_index)
        path_bits = toggle_step(path_bits, (axis_name, bit_index))
        forward = logit_block(own_image, held_text)
        row_losses = row_losses + jnp.sum(jnp.log1p(jnp.exp(forward)), axis=1)
        weights = jax.nn.sigmoid(forward).astype(jnp.bfloat16)
        image_total = image_total + LOGIT_SCALE * jnp.dot(
            weights, held_text, preferred_element_type=jnp.float32
        )
        text_share = (
            LOGIT_SCALE
            * lax.dot_general(weights, own_image, CONTRACT_ROWS, preferred_element_type=jnp.float32)
        ).astype(jnp.bfloat16)
        text_total = text_total + send_home(text_share, list(path_bits)).astype(jnp.float32)
    image_grad = raw_gradient(image_unit, image_inverse, image_total)
    text_grad = raw_gradient(text_unit, text_inverse, text_total)
    return (row_losses / row_count, image_grad, text_grad)


def solution(mesh):
    return jax.shard_map(
        shards,
        mesh=mesh,
        in_specs=(P(("row", "col"), None), P(("row", "col"), None)),
        out_specs=(P(("row", "col")), P(("row", "col"), None), P(("row", "col"), None)),
        check_vma=False,
    )
```

profile of v0, /device:TPU:1, one launch (start us, length us, event | category | flops | bytes accessed | tf_op | source)
XLA Modules:
  0.0 175.4 jit_solution(2456563246605264187)
XLA Ops:
  3.4 4.4 %collective-permute-start = (bf16[320,1152]{1,0:T(8,128)(2,1)S(1)}, bf16[320,1152]{1,0:T(8,128)(2,1)S(1)}, u32[]{:S(2)}, u32[]{:S(2)}) collective-permute-start(bf16[320,1152]{1,0:T(8,128)(2,1)S(1)} %fusion.10), channel_id=1, source_target_pairs={{0,1},{1,0},{2,3},{3,2},{4,5},{5,4},{6,7},{7,6},{8,9},{9,8},{10,11... | collective-permute-start | bytes 2211848 | tf_op jit(solution)/shard_map/ppermute | solution.py:15
  8.9 10.5 %collective-permute-done = bf16[320,1152]{1,0:T(8,128)(2,1)S(1)} collective-permute-done((bf16[320,1152]{1,0:T(8,128)(2,1)S(1)}, bf16[320,1152]{1,0:T(8,128)(2,1)S(1)}, u32[]{:S(2)}, u32[]{:S(2)}) %collective-permute-start) | collective-permute-done | bytes 737312 | tf_op jit(solution)/shard_map/ppermute | solution.py:15
  19.4 7.7 %collective-permute-start.1 = (bf16[320,1152]{1,0:T(8,128)(2,1)S(1)}, bf16[320,1152]{1,0:T(8,128)(2,1)S(1)}, u32[]{:S(2)}, u32[]{:S(2)}) collective-permute-start(bf16[320,1152]{1,0:T(8,128)(2,1)S(1)} %collective-permute-done), channel_id=1, source_target_pairs={{0,32},{32,0},{64,96},{96,64},{128,160},{160,128},{192,224},{224,1... | collective-permute-start | bytes 2211848 | tf_op jit(solution)/shard_map/ppermute | solution.py:15
  29.2 3.4 %collective-permute-start.2 = (bf16[320,1152]{1,0:T(8,128)(2,1)S(1)}, bf16[320,1152]{1,0:T(8,128)(2,1)S(1)}, u32[]{:S(2)}, u32[]{:S(2)}) collective-permute-start(bf16[320,1152]{1,0:T(8,128)(2,1)S(1)} %collective-permute-done.1), channel_id=1, source_target_pairs={{0,1},{1,0},{2,3},{3,2},{4,5},{5,4},{6,7},{7,6},{8,9},{9,8},{10,11... | collective-permute-start | bytes 2211848 | tf_op jit(solution)/shard_map/ppermute | solution.py:15
  33.3 1.9 %collective-permute-start.6 = (bf16[320,1152]{1,0:T(8,128)(2,1)S(1)}, bf16[320,1152]{1,0:T(8,128)(2,1)S(1)}, u32[]{:S(2)}, u32[]{:S(2)}) collective-permute-start(bf16[320,1152]{1,0:T(8,128)(2,1)S(1)} %fusion.2), channel_id=1, source_target_pairs={{0,1},{1,0},{2,3},{3,2},{4,5},{5,4},{6,7},{7,6},{8,9},{9,8},{10,11... | collective-permute-start | bytes 2211848 | tf_op jit(solution)/shard_map/ppermute | solution.py:15
  36.7 12.5 %collective-permute-done.2 = bf16[320,1152]{1,0:T(8,128)(2,1)S(1)} collective-permute-done((bf16[320,1152]{1,0:T(8,128)(2,1)S(1)}, bf16[320,1152]{1,0:T(8,128)(2,1)S(1)}, u32[]{:S(2)}, u32[]{:S(2)}) %collective-permute-start.2) | collective-permute-done | bytes 737312 | tf_op jit(solution)/shard_map/ppermute | solution.py:15
  49.2 4.6 %collective-permute-start.3 = (bf16[320,1152]{1,0:T(8,128)(2,1)S(1)}, bf16[320,1152]{1,0:T(8,128)(2,1)S(1)}, u32[]{:S(2)}, u32[]{:S(2)}) collective-permute-start(bf16[320,1152]{1,0:T(8,128)(2,1)S(1)} %collective-permute-done.2), channel_id=1, source_target_pairs={{0,16},{1,17},{2,18},{3,19},{4,20},{5,21},{6,22},{7,23},{8,24},{9,... | collective-permute-start | bytes 2211848 | tf_op jit(solution)/shard_map/ppermute | solution.py:15
  54.5 3.4 %collective-permute-start.7 = (bf16[320,1152]{1,0:T(8,128)(2,1)S(1)}, bf16[320,1152]{1,0:T(8,128)(2,1)S(1)}, u32[]{:S(2)}, u32[]{:S(2)}) collective-permute-start(bf16[320,1152]{1,0:T(8,128)(2,1)S(1)} %fusion.3), channel_id=1, source_target_pairs={{0,1},{1,0},{2,3},{3,2},{4,5},{5,4},{6,7},{7,6},{8,9},{9,8},{10,11... | collective-permute-start | bytes 2211848 | tf_op jit(solution)/shard_map/ppermute | solution.py:15
  59.3 10.0 %collective-permute-done.3 = bf16[320,1152]{1,0:T(8,128)(2,1)S(1)} collective-permute-done((bf16[320,1152]{1,0:T(8,128)(2,1)S(1)}, bf16[320,1152]{1,0:T(8,128)(2,1)S(1)}, u32[]{:S(2)}, u32[]{:S(2)}) %collective-permute-start.3) | collective-permute-done | bytes 737312 | tf_op jit(solution)/shard_map/ppermute | solution.py:15
  69.3 3.4 %collective-permute-start.4 = (bf16[320,1152]{1,0:T(8,128)(2,1)S(1)}, bf16[320,1152]{1,0:T(8,128)(2,1)S(1)}, u32[]{:S(2)}, u32[]{:S(2)}) collective-permute-start(bf16[320,1152]{1,0:T(8,128)(2,1)S(1)} %collective-permute-done.3), channel_id=1, source_target_pairs={{0,1},{1,0},{2,3},{3,2},{4,5},{5,4},{6,7},{7,6},{8,9},{9,8},{10,11... | collective-permute-start | bytes 2211848 | tf_op jit(solution)/shard_map/ppermute | solution.py:15
  74.8 21.8 %collective-permute-done.4 = bf16[320,1152]{1,0:T(8,128)(2,1)S(1)} collective-permute-done((bf16[320,1152]{1,0:T(8,128)(2,1)S(1)}, bf16[320,1152]{1,0:T(8,128)(2,1)S(1)}, u32[]{:S(2)}, u32[]{:S(2)}) %collective-permute-start.4) | collective-permute-done | bytes 737312 | tf_op jit(solution)/shard_map/ppermute | solution.py:15
  96.6 2.7 %collective-permute-start.5 = (bf16[320,1152]{1,0:T(8,128)(2,1)S(1)}, bf16[320,1152]{1,0:T(8,128)(2,1)S(1)}, u32[]{:S(2)}, u32[]{:S(2)}) collective-permute-start(bf16[320,1152]{1,0:T(8,128)(2,1)S(1)} %collective-permute-done.4), channel_id=1, source_target_pairs={{0,32},{32,0},{64,96},{96,64},{128,160},{160,128},{192,224},{224,1... | collective-permute-start | bytes 2211848 | tf_op jit(solution)/shard_map/ppermute | solution.py:15
  100.8 4.7 %collective-permute-start.12 = (bf16[320,1152]{1,0:T(8,128)(2,1)S(1)}, bf16[320,1152]{1,0:T(8,128)(2,1)S(1)}, u32[]{:S(2)}, u32[]{:S(2)}) collective-permute-start(bf16[320,1152]{1,0:T(8,128)(2,1)S(1)} %fusion.6), channel_id=1, source_target_pairs={{0,16},{1,17},{2,18},{3,19},{4,20},{5,21},{6,22},{7,23},{8,24},{9,... | collective-permute-start | bytes 2211848 | tf_op jit(solution)/shard_map/ppermute | solution.py:15
  106.2 2.3 %collective-permute-start.10 = (bf16[320,1152]{1,0:T(8,128)(2,1)S(1)}, bf16[320,1152]{1,0:T(8,128)(2,1)S(1)}, u32[]{:S(2)}, u32[]{:S(2)}) collective-permute-start(bf16[320,1152]{1,0:T(8,128)(2,1)S(1)} %fusion.5), channel_id=1, source_target_pairs={{0,16},{1,17},{2,18},{3,19},{4,20},{5,21},{6,22},{7,23},{8,24},{9,... | collective-permute-start | bytes 2211848 | tf_op jit(solution)/shard_map/ppermute | solution.py:15
  110.0 4.7 %collective-permute-start.15 = (bf16[320,1152]{1,0:T(8,128)(2,1)S(1)}, bf16[320,1152]{1,0:T(8,128)(2,1)S(1)}, u32[]{:S(2)}, u32[]{:S(2)}) collective-permute-start(bf16[320,1152]{1,0:T(8,128)(2,1)S(1)} %fusion.7), channel_id=1, source_target_pairs={{0,16},{1,17},{2,18},{3,19},{4,20},{5,21},{6,22},{7,23},{8,24},{9,... | collective-permute-start | bytes 2211848 | tf_op jit(solution)/shard_map/ppermute | solution.py:15
  114.7 7.7 %collective-permute-done.12 = bf16[320,1152]{1,0:T(8,128)(2,1)S(1)} collective-permute-done((bf16[320,1152]{1,0:T(8,128)(2,1)S(1)}, bf16[320,1152]{1,0:T(8,128)(2,1)S(1)}, u32[]{:S(2)}, u32[]{:S(2)}) %collective-permute-start.12) | collective-permute-done | bytes 737312 | tf_op jit(solution)/shard_map/ppermute | solution.py:15
  122.3 3.4 %collective-permute-start.13 = (bf16[320,1152]{1,0:T(8,128)(2,1)S(1)}, bf16[320,1152]{1,0:T(8,128)(2,1)S(1)}, u32[]{:S(2)}, u32[]{:S(2)}) collective-permute-start(bf16[320,1152]{1,0:T(8,128)(2,1)S(1)} %collective-permute-done.12), channel_id=1, source_target_pairs={{0,1},{1,0},{2,3},{3,2},{4,5},{5,4},{6,7},{7,6},{8,9},{9,8},{10,11... | collective-permute-start | bytes 2211848 | tf_op jit(solution)/shard_map/ppermute | solution.py:15
  127.9 3.4 %collective-permute-start.9 = (bf16[320,1152]{1,0:T(8,128)(2,1)S(1)}, bf16[320,1152]{1,0:T(8,128)(2,1)S(1)}, u32[]{:S(2)}, u32[]{:S(2)}) collective-permute-start(bf16[320,1152]{1,0:T(8,128)(2,1)S(1)} %fusion.4), channel_id=1, source_target_pairs={{0,32},{32,0},{64,96},{96,64},{128,160},{160,128},{192,224},{224,1... | collective-permute-start | bytes 2211848 | tf_op jit(solution)/shard_map/ppermute | solution.py:15
  133.2 5.0 %collective-permute-done.10 = bf16[320,1152]{1,0:T(8,128)(2,1)S(1)} collective-permute-done((bf16[320,1152]{1,0:T(8,128)(2,1)S(1)}, bf16[320,1152]{1,0:T(8,128)(2,1)S(1)}, u32[]{:S(2)}, u32[]{:S(2)}) %collective-permute-start.10) | collective-permute-done | bytes 737312 | tf_op jit(solution)/shard_map/ppermute | solution.py:15
  138.1 3.1 %collective-permute-start.11 = (bf16[320,1152]{1,0:T(8,128)(2,1)S(1)}, bf16[320,1152]{1,0:T(8,128)(2,1)S(1)}, u32[]{:S(2)}, u32[]{:S(2)}) collective-permute-start(bf16[320,1152]{1,0:T(8,128)(2,1)S(1)} %collective-permute-done.10), channel_id=1, source_target_pairs={{0,32},{32,0},{64,96},{96,64},{128,160},{160,128},{192,224},{224,1... | collective-permute-start | bytes 2211848 | tf_op jit(solution)/shard_map/ppermute | solution.py:15
  141.2 12.7 %collective-permute-done.15 = bf16[320,1152]{1,0:T(8,128)(2,1)S(1)} collective-permute-done((bf16[320,1152]{1,0:T(8,128)(2,1)S(1)}, bf16[320,1152]{1,0:T(8,128)(2,1)S(1)}, u32[]{:S(2)}, u32[]{:S(2)}) %collective-permute-start.15) | collective-permute-done | bytes 737312 | tf_op jit(solution)/shard_map/ppermute | solution.py:15
  153.9 3.4 %collective-permute-start.16 = (bf16[320,1152]{1,0:T(8,128)(2,1)S(1)}, bf16[320,1152]{1,0:T(8,128)(2,1)S(1)}, u32[]{:S(2)}, u32[]{:S(2)}) collective-permute-start(bf16[320,1152]{1,0:T(8,128)(2,1)S(1)} %collective-permute-done.15), channel_id=1, source_target_pairs={{0,1},{1,0},{2,3},{3,2},{4,5},{5,4},{6,7},{7,6},{8,9},{9,8},{10,11... | collective-permute-start | bytes 2211848 | tf_op jit(solution)/shard_map/ppermute | solution.py:15
  157.3 3.0 %collective-permute-start.14 = (bf16[320,1152]{1,0:T(8,128)(2,1)S(1)}, bf16[320,1152]{1,0:T(8,128)(2,1)S(1)}, u32[]{:S(2)}, u32[]{:S(2)}) collective-permute-start(bf16[320,1152]{1,0:T(8,128)(2,1)S(1)} %collective-permute-done.13), channel_id=1, source_target_pairs={{0,32},{32,0},{64,96},{96,64},{128,160},{160,128},{192,224},{224,1... | collective-permute-start | bytes 2211848 | tf_op jit(solution)/shard_map/ppermute | solution.py:15
  162.3 10.7 %collective-permute-done.16 = bf16[320,1152]{1,0:T(8,128)(2,1)S(1)} collective-permute-done((bf16[320,1152]{1,0:T(8,128)(2,1)S(1)}, bf16[320,1152]{1,0:T(8,128)(2,1)S(1)}, u32[]{:S(2)}, u32[]{:S(2)}) %collective-permute-start.16) | collective-permute-done | bytes 737312 | tf_op jit(solution)/shard_map/ppermute | solution.py:15
  (44 shorter events, 24.4 us)
Async XLA Ops:
  0.6 7.1 %copy-start.1 = (bf16[320,1152]{1,0:T(8,128)(2,1)S(1)}, bf16[320,1152]{1,0:T(8,128)(2,1)}, u32[]{:S(2)}) copy-start(bf16[320,1152]{1,0:T(8,128)(2,1)} %param.2) | copy-start | bytes 2211844
  3.4 16.0 %collective-permute-start = (bf16[320,1152]{1,0:T(8,128)(2,1)S(1)}, bf16[320,1152]{1,0:T(8,128)(2,1)S(1)}, u32[]{:S(2)}, u32[]{:S(2)}) collective-permute-start(bf16[320,1152]{1,0:T(8,128)(2,1)S(1)} %fusion.10), channel_id=1, source_target_pairs={{0,1},{1,0},{2,3},{3,2},{4,5},{5,4},{6,7},{7,6},{8,9},{9,8},{10,11... | collective-permute-start | bytes 2211848 | tf_op jit(solution)/shard_map/ppermute | solution.py:15
  19.4 9.8 %collective-permute-start.1 = (bf16[320,1152]{1,0:T(8,128)(2,1)S(1)}, bf16[320,1152]{1,0:T(8,128)(2,1)S(1)}, u32[]{:S(2)}, u32[]{:S(2)}) collective-permute-start(bf16[320,1152]{1,0:T(8,128)(2,1)S(1)} %collective-permute-done), channel_id=1, source_target_pairs={{0,32},{32,0},{64,96},{96,64},{128,160},{160,128},{192,224},{224,1... | collective-permute-start | bytes 2211848 | tf_op jit(solution)/shard_map/ppermute | solution.py:15
  29.2 20.0 %collective-permute-start.2 = (bf16[320,1152]{1,0:T(8,128)(2,1)S(1)}, bf16[320,1152]{1,0:T(8,128)(2,1)S(1)}, u32[]{:S(2)}, u32[]{:S(2)}) collective-permute-start(bf16[320,1152]{1,0:T(8,128)(2,1)S(1)} %collective-permute-done.1), channel_id=1, source_target_pairs={{0,1},{1,0},{2,3},{3,2},{4,5},{5,4},{6,7},{7,6},{8,9},{9,8},{10,11... | collective-permute-start | bytes 2211848 | tf_op jit(solution)/shard_map/ppermute | solution.py:15
  33.3 94.6 %collective-permute-start.6 = (bf16[320,1152]{1,0:T(8,128)(2,1)S(1)}, bf16[320,1152]{1,0:T(8,128)(2,1)S(1)}, u32[]{:S(2)}, u32[]{:S(2)}) collective-permute-start(bf16[320,1152]{1,0:T(8,128)(2,1)S(1)} %fusion.2), channel_id=1, source_target_pairs={{0,1},{1,0},{2,3},{3,2},{4,5},{5,4},{6,7},{7,6},{8,9},{9,8},{10,11... | collective-permute-start | bytes 2211848 | tf_op jit(solution)/shard_map/ppermute | solution.py:15
  49.2 20.1 %collective-permute-start.3 = (bf16[320,1152]{1,0:T(8,128)(2,1)S(1)}, bf16[320,1152]{1,0:T(8,128)(2,1)S(1)}, u32[]{:S(2)}, u32[]{:S(2)}) collective-permute-start(bf16[320,1152]{1,0:T(8,128)(2,1)S(1)} %collective-permute-done.2), channel_id=1, source_target_pairs={{0,16},{1,17},{2,18},{3,19},{4,20},{5,21},{6,22},{7,23},{8,24},{9,... | collective-permute-start | bytes 2211848 | tf_op jit(solution)/shard_map/ppermute | solution.py:15
  54.5 76.8 %collective-permute-start.7 = (bf16[320,1152]{1,0:T(8,128)(2,1)S(1)}, bf16[320,1152]{1,0:T(8,128)(2,1)S(1)}, u32[]{:S(2)}, u32[]{:S(2)}) collective-permute-start(bf16[320,1152]{1,0:T(8,128)(2,1)S(1)} %fusion.3), channel_id=1, source_target_pairs={{0,1},{1,0},{2,3},{3,2},{4,5},{5,4},{6,7},{7,6},{8,9},{9,8},{10,11... | collective-permute-start | bytes 2211848 | tf_op jit(solution)/shard_map/ppermute | solution.py:15
  69.3 27.3 %collective-permute-start.4 = (bf16[320,1152]{1,0:T(8,128)(2,1)S(1)}, bf16[320,1152]{1,0:T(8,128)(2,1)S(1)}, u32[]{:S(2)}, u32[]{:S(2)}) collective-permute-start(bf16[320,1152]{1,0:T(8,128)(2,1)S(1)} %collective-permute-done.3), channel_id=1, source_target_pairs={{0,1},{1,0},{2,3},{3,2},{4,5},{5,4},{6,7},{7,6},{8,9},{9,8},{10,11... | collective-permute-start | bytes 2211848 | tf_op jit(solution)/shard_map/ppermute | solution.py:15
  96.6 11.9 %collective-permute-start.5 = (bf16[320,1152]{1,0:T(8,128)(2,1)S(1)}, bf16[320,1152]{1,0:T(8,128)(2,1)S(1)}, u32[]{:S(2)}, u32[]{:S(2)}) collective-permute-start(bf16[320,1152]{1,0:T(8,128)(2,1)S(1)} %collective-permute-done.4), channel_id=1, source_target_pairs={{0,32},{32,0},{64,96},{96,64},{128,160},{160,128},{192,224},{224,1... | collective-permute-start | bytes 2211848 | tf_op jit(solution)/shard_map/ppermute | solution.py:15
  100.8 21.5 %collective-permute-start.12 = (bf16[320,1152]{1,0:T(8,128)(2,1)S(1)}, bf16[320,1152]{1,0:T(8,128)(2,1)S(1)}, u32[]{:S(2)}, u32[]{:S(2)}) collective-permute-start(bf16[320,1152]{1,0:T(8,128)(2,1)S(1)} %fusion.6), channel_id=1, source_target_pairs={{0,16},{1,17},{2,18},{3,19},{4,20},{5,21},{6,22},{7,23},{8,24},{9,... | collective-permute-start | bytes 2211848 | tf_op jit(solution)/shard_map/ppermute | solution.py:15
  106.2 32.0 %collective-permute-start.10 = (bf16[320,1152]{1,0:T(8,128)(2,1)S(1)}, bf16[320,1152]{1,0:T(8,128)(2,1)S(1)}, u32[]{:S(2)}, u32[]{:S(2)}) collective-permute-start(bf16[320,1152]{1,0:T(8,128)(2,1)S(1)} %fusion.5), channel_id=1, source_target_pairs={{0,16},{1,17},{2,18},{3,19},{4,20},{5,21},{6,22},{7,23},{8,24},{9,... | collective-permute-start | bytes 2211848 | tf_op jit(solution)/shard_map/ppermute | solution.py:15
  110.0 44.0 %collective-permute-start.15 = (bf16[320,1152]{1,0:T(8,128)(2,1)S(1)}, bf16[320,1152]{1,0:T(8,128)(2,1)S(1)}, u32[]{:S(2)}, u32[]{:S(2)}) collective-permute-start(bf16[320,1152]{1,0:T(8,128)(2,1)S(1)} %fusion.7), channel_id=1, source_target_pairs={{0,16},{1,17},{2,18},{3,19},{4,20},{5,21},{6,22},{7,23},{8,24},{9,... | collective-permute-start | bytes 2211848 | tf_op jit(solution)/shard_map/ppermute | solution.py:15
  122.3 35.0 %collective-permute-start.13 = (bf16[320,1152]{1,0:T(8,128)(2,1)S(1)}, bf16[320,1152]{1,0:T(8,128)(2,1)S(1)}, u32[]{:S(2)}, u32[]{:S(2)}) collective-permute-start(bf16[320,1152]{1,0:T(8,128)(2,1)S(1)} %collective-permute-done.12), channel_id=1, source_target_pairs={{0,1},{1,0},{2,3},{3,2},{4,5},{5,4},{6,7},{7,6},{8,9},{9,8},{10,11... | collective-permute-start | bytes 2211848 | tf_op jit(solution)/shard_map/ppermute | solution.py:15
  127.9 34.5 %collective-permute-start.9 = (bf16[320,1152]{1,0:T(8,128)(2,1)S(1)}, bf16[320,1152]{1,0:T(8,128)(2,1)S(1)}, u32[]{:S(2)}, u32[]{:S(2)}) collective-permute-start(bf16[320,1152]{1,0:T(8,128)(2,1)S(1)} %fusion.4), channel_id=1, source_target_pairs={{0,32},{32,0},{64,96},{96,64},{128,160},{160,128},{192,224},{224,1... | collective-permute-start | bytes 2211848 | tf_op jit(solution)/shard_map/ppermute | solution.py:15
  131.3 31.1 %collective-permute-start.8 = (bf16[320,1152]{1,0:T(8,128)(2,1)S(1)}, bf16[320,1152]{1,0:T(8,128)(2,1)S(1)}, u32[]{:S(2)}, u32[]{:S(2)}) collective-permute-start(bf16[320,1152]{1,0:T(8,128)(2,1)S(1)} %collective-permute-done.7), channel_id=1, source_target_pairs={{0,32},{32,0},{64,96},{96,64},{128,160},{160,128},{192,224},{224,1... | collective-permute-start | bytes 2211848 | tf_op jit(solution)/shard_map/ppermute | solution.py:15
  138.1 24.2 %collective-permute-start.11 = (bf16[320,1152]{1,0:T(8,128)(2,1)S(1)}, bf16[320,1152]{1,0:T(8,128)(2,1)S(1)}, u32[]{:S(2)}, u32[]{:S(2)}) collective-permute-start(bf16[320,1152]{1,0:T(8,128)(2,1)S(1)} %collective-permute-done.10), channel_id=1, source_target_pairs={{0,32},{32,0},{64,96},{96,64},{128,160},{160,128},{192,224},{224,1... | collective-permute-start | bytes 2211848 | tf_op jit(solution)/shard_map/ppermute | solution.py:15
  153.9 19.1 %collective-permute-start.16 = (bf16[320,1152]{1,0:T(8,128)(2,1)S(1)}, bf16[320,1152]{1,0:T(8,128)(2,1)S(1)}, u32[]{:S(2)}, u32[]{:S(2)}) collective-permute-start(bf16[320,1152]{1,0:T(8,128)(2,1)S(1)} %collective-permute-done.15), channel_id=1, source_target_pairs={{0,1},{1,0},{2,3},{3,2},{4,5},{5,4},{6,7},{7,6},{8,9},{9,8},{10,11... | collective-permute-start | bytes 2211848 | tf_op jit(solution)/shard_map/ppermute | solution.py:15
  157.3 15.7 %collective-permute-start.14 = (bf16[320,1152]{1,0:T(8,128)(2,1)S(1)}, bf16[320,1152]{1,0:T(8,128)(2,1)S(1)}, u32[]{:S(2)}, u32[]{:S(2)}) collective-permute-start(bf16[320,1152]{1,0:T(8,128)(2,1)S(1)} %collective-permute-done.13), channel_id=1, source_target_pairs={{0,32},{32,0},{64,96},{96,64},{128,160},{160,128},{192,224},{224,1... | collective-permute-start | bytes 2211848 | tf_op jit(solution)/shard_map/ppermute | solution.py:15
  160.9 12.2 %copy-start = (bf16[320,1152]{1,0:T(8,128)(2,1)S(1)}, bf16[320,1152]{1,0:T(8,128)(2,1)}, u32[]{:S(2)}) copy-start(bf16[320,1152]{1,0:T(8,128)(2,1)} %param.3) | copy-start | bytes 2211844
where the time goes:
time: 176 us; the launch traced here: 175 us
  waiting for transfers between devices  90.9 us (52%)
  starting transfers between devices  61.1 us (35%)
  matrix products  15.1 us (9%)
  other arithmetic  7.33 us (4%)
    ppermute x17, waiting for transfers between devices, partner(): return lax.ppermute(value, axis, pairs)  90.9 us
    ppermute x17, starting transfers between devices, partner(): return lax.ppermute(value, axis, pairs)  61.1 us
    dot_general x7, matrix products, logit_block(): lax.dot_general(left_rows, right_rows, (((1,), (1,)), ((), ())), preferre...  5.97 us
    dot_general x7, matrix products, shards(): lax.dot_general(weights, own_image, CONTRACT_ROWS, preferred_element_type...  4.5 us
    dot_general x6, matrix products, shards(): jnp.dot(weights, held_text, preferred_element_type=jnp.float32)  4 us
  transfers between devices with their start and end apart: 17, of which 8 were waited for; matrix products, arithmetic and copies ran while one was open for 10% of the time, Pallas kernels for 0%

commit v1 on v0

v1 whole, which is shorter than its diff:
```python
import jax
import jax.numpy as jnp
from jax import lax
from jax.sharding import Mesh
from jax.sharding import PartitionSpec as P

LOGIT_SCALE = 8.0
LOGIT_BIAS = -4.0
EPSILON = 1e-06
ROW_COL = (((1,), (1,)), ((), ()))
SWAP = ((0, 1), (1, 0))
AXES = ("outer", "core", "x_hi", "z_hi", "z_lo")


def swap(value, axis):
    return lax.ppermute(value, axis, SWAP)


def normalize_rows(raw_rows):
    widened = raw_rows.astype(jnp.float32)
    inverse = lax.rsqrt(jnp.sum(widened * widened, axis=1, keepdims=True) + EPSILON)
    return (widened * inverse, inverse)


def logit_block(left_rows, right_rows):
    product = lax.dot_general(left_rows, right_rows, ROW_COL, preferred_element_type=jnp.float32)
    return LOGIT_SCALE * product + LOGIT_BIAS


def raw_gradient(normed, inverse, gradient):
    return inverse * (gradient - normed * jnp.sum(normed * gradient, axis=1, keepdims=True))


def shards(image, text):
    rows = image.shape[0]
    z_text = swap(text, "z_lo")
    x_image = swap(image, "x_hi")
    mate = swap(jnp.concatenate([image, text], axis=0), "core")
    far = swap(jnp.concatenate([x_image, z_text], axis=0), "core")

    def unit(raw):
        return normalize_rows(raw)[0].astype(jnp.bfloat16)

    mate, far = unit(mate), unit(far)
    own_image, own_text, x_image, z_text = unit(image), unit(text), unit(x_image), unit(z_text)
    mate_image, mate_text = mate[:rows], mate[rows:]
    far_image, far_text = far[:rows], far[rows:]
    r = lax.broadcasted_iota(jnp.int32, (rows, rows), 0)
    c = lax.broadcasted_iota(jnp.int32, (rows, rows), 1)
    identity = (r == c).astype(jnp.float32)

    def group(left, rights, positive, losses):
        total, loss = 0.0, 0.0
        for n, right in enumerate(rights):
            logits = logit_block(left, right)
            weights = jax.nn.sigmoid(logits)
            if losses:
                soft = jnp.log1p(jnp.exp(logits))
                if positive and n == 0:
                    soft = soft - identity * logits
                loss = loss + jnp.sum(soft, axis=1)
            if positive and n == 0:
                weights = weights - identity
            weights = weights.astype(jnp.bfloat16)
            total = total + jnp.dot(weights, right, preferred_element_type=jnp.float32)
        return LOGIT_SCALE * total, loss

    x_total, x_loss = group(x_image, [mate_text, z_text, far_text], False, True)
    x_back = swap(x_total.astype(jnp.bfloat16), "x_hi")
    z_total, _ = group(z_text, [own_image, mate_image, x_image, far_image], False, False)
    z_back = swap(z_total.astype(jnp.bfloat16), "z_lo")
    l_back = swap(x_loss, "x_hi")
    i_total, i_loss = group(own_image, [own_text, mate_text, z_text, far_text], True, True)
    t_total, _ = group(own_text, [own_image, mate_image, far_image], True, False)

    i_total = i_total + x_back.astype(jnp.float32)
    t_total = t_total + z_back.astype(jnp.float32)
    image_unit, image_inverse = normalize_rows(image)
    text_unit, text_inverse = normalize_rows(text)
    image_grad = raw_gradient(image_unit, image_inverse, i_total)
    text_grad = raw_gradient(text_unit, text_inverse, t_total)
    return ((i_loss + l_back) / rows, image_grad, text_grad)


def solution(mesh):
    n_row, n_col = mesh.devices.shape
    fine = Mesh(mesh.devices.reshape(n_row // 2, 2, 2, n_col // 4, 2), AXES)
    return jax.shard_map(
        shards,
        mesh=fine,
        in_specs=(P(AXES, None), P(AXES, None)),
        out_specs=(P(AXES), P(AXES, None), P(AXES, None)),
        check_vma=False,
    )
```

time: 176 us -> 109 us (0.62)
  waiting for transfers between devices: 90.9 us -> 14.5 us
  starting transfers between devices: 61.1 us -> 27.1 us
  matrix products: 15.1 us -> 45.9 us
  other arithmetic: 7.33 us -> 17.7 us
  local copies, waits for them, and re-layouts: 0.01 us -> 2.18 us
    ppermute x17 -> x7, waiting for transfers between devices: 90.9 us -> 14.5 us  [swap(): return lax.ppermute(value, axis, SWAP)]
    ppermute x17 -> x7, starting transfers between devices: 61.1 us -> 27.1 us  [swap(): return lax.ppermute(value, axis, SWAP)]
    dot_general x21, matrix products: 15.1 us -> 45.9 us  [the longest x14 38 us: group(): total = total + jnp.dot(weights, right, preferred_element_type=jnp.float32)]
    concatenate x0 -> x2, other arithmetic: none -> 3.78 us  [the longest x1 2.56 us: shards(): mate = swap(jnp.concatenate([image, text], axis=0), 'core')]
    convert_element_type x1 -> x2, other arithmetic: 1.31 us -> 4.48 us  [unit(): return normalize_rows(raw)[0].astype(jnp.bfloat16)]
    reduce_sum x2 -> x6, other arithmetic: 1.67 us -> 4.42 us  [normalize_rows(): jnp.sum(widened * widened, axis=1, keepdims=True) + EPSILON]
    unnamed x4 -> x22, local copies, waits for them, and re-layouts: 0.01 us -> 2.18 us
  transfers between devices with their start and end apart: 17 -> 7, of which waited for: 8 -> 2; matrix products, arithmetic and copies ran while one was open for 10% -> 44% of each run, Pallas kernels for 0% -> 0%
where the time goes in v1:
time: 109 us; the launch traced here: 108 us
  matrix products  45.9 us (42%)
  starting transfers between devices  27.1 us (25%)
  other arithmetic  17.7 us (16%)
  waiting for transfers between devices  14.5 us (13%)
  local copies, waits for them, and re-layouts  2.18 us (2%)
    dot_general x14, matrix products, group(): total = total + jnp.dot(weights, right, preferred_element_type=jnp.float32)  38 us
    ppermute x7, starting transfers between devices, swap(): return lax.ppermute(value, axis, SWAP)  27.1 us
    ppermute x7, waiting for transfers between devices, swap(): return lax.ppermute(value, axis, SWAP)  14.5 us
    dot_general x7, matrix products, logit_block(): lax.dot_general(left_rows, right_rows, ROW_COL, preferred_element_type=jn...  7.85 us
    convert_element_type x2, other arithmetic, unit(): return normalize_rows(raw)[0].astype(jnp.bfloat16)  4.48 us
    reduce_sum x6, other arithmetic, normalize_rows(): jnp.sum(widened * widened, axis=1, keepdims=True) + EPSILON  4.42 us
    mul x2, other arithmetic, raw_gradient(): inverse * (gradient - normed * jnp.sum(normed * gradient, axis=1, keepdim...  4.37 us
    concatenate x1, other arithmetic, shards(): mate = swap(jnp.concatenate([image, text], axis=0), 'core')  2.56 us
  transfers between devices with their start and end apart: 7, of which 2 were waited for; matrix products, arithmetic and copies ran while one was open for 44% of the time, Pallas kernels for 0%

profile of v1, /device:TPU:1, one launch (start us, length us, event | category | flops | bytes accessed | tf_op | source)
XLA Modules:
  0.0 108.1 jit_solution(8071858755172723320)
XLA Ops:
  0.6 4.5 %collective-permute-start.1 = (bf16[320,1152]{1,0:T(8,128)(2,1)}, bf16[320,1152]{1,0:T(8,128)(2,1)S(1)}, u32[]{:S(2)}, u32[]{:S(2)}) collective-permute-start(bf16[320,1152]{1,0:T(8,128)(2,1)} %param.3), channel_id=1, source_target_pairs={{0,1},{1,0},{2,3},{3,2},{4,5},{5,4},{6,7},{7,6},{8,9},{9,8},{10,11... | collective-permute-start | bytes 2211848 | tf_op jit(solution)/shard_map/ppermute | solution.py:16
  5.2 4.7 %collective-permute-start.2 = (bf16[320,1152]{1,0:T(8,128)(2,1)}, bf16[320,1152]{1,0:T(8,128)(2,1)S(1)}, u32[]{:S(2)}, u32[]{:S(2)}) collective-permute-start(bf16[320,1152]{1,0:T(8,128)(2,1)} %param.2), channel_id=1, source_target_pairs={{0,16},{16,0},{1,17},{17,1},{2,18},{18,2},{3,19},{19,3},{4,20},{20... | collective-permute-start | bytes 2211848 | tf_op jit(solution)/shard_map/ppermute | solution.py:16
  9.8 2.6 %pad_maximum_fusion = bf16[640,1152]{1,0:T(8,128)(2,1)} fusion(bf16[320,1152]{1,0:T(8,128)(2,1)} %param.3, bf16[320,1152]{1,0:T(8,128)(2,1)} %param.2), kind=kLoop, calls=%fused_computation.52 | loop fusion | flops 2949120 | bytes 2949120 | tf_op jit(solution)/shard_map/concatenate | solution.py:38
  12.4 3.6 %collective-permute-start = (bf16[640,1152]{1,0:T(8,128)(2,1)}, bf16[640,1152]{1,0:T(8,128)(2,1)}, u32[]{:S(2)}, u32[]{:S(2)}) collective-permute-start(bf16[640,1152]{1,0:T(8,128)(2,1)} %pad_maximum_fusion), channel_id=1, source_target_pairs={{0,32},{32,0},{1,33},{33,1},{2,34},{34,2},{3,35},{35,3},{4,36},{36... | collective-permute-start | bytes 4423688 | tf_op jit(solution)/shard_map/ppermute | solution.py:16
  17.4 1.9 %fusion.106 = f32[320,1152]{1,0:T(8,128)} fusion(f32[320,320]{0,1:T(8,128)S(1)} %get-tuple-element.14, bf16[320,1152]{1,0:T(8,128)(2,1)S(1)} %copy-done.1, f32[320]{0:T(512)S(1)} %add_rsqrt_fusion.4), kind=kOutput, calls=%fused_computation.152 | convolution fusion | flops 237752320 | bytes 2622720 | tf_op jit(solution)/shard_map/dot_general | solution.py:65
  19.2 2.6 %fusion.85 = f32[320,1152]{1,0:T(8,128)} fusion(bf16[320,1152]{1,0:T(8,128)(2,1)S(1)} %copy-done.1, f32[320]{0:T(512)S(1)} %add_rsqrt_fusion.4, bf16[320,1152]{1,0:T(8,128)(2,1)S(1)} %copy-done, f32[320]{0:T(512)S(1)} %add_rsqrt_fusion.5), kind=kOutput, calls=%fused_computation.120 | convolution fusion | flops 476098560 | bytes 2951680 | tf_op jit(solution)/shard_map/dot_general | solution.py:65
  22.1 2.4 %collective-permute-done.2 = bf16[320,1152]{1,0:T(8,128)(2,1)S(1)} collective-permute-done((bf16[320,1152]{1,0:T(8,128)(2,1)}, bf16[320,1152]{1,0:T(8,128)(2,1)S(1)}, u32[]{:S(2)}, u32[]{:S(2)}) %collective-permute-start.2) | collective-permute-done | bytes 737312 | tf_op jit(solution)/shard_map/ppermute | solution.py:16
  25.7 5.3 %collective-permute-start.3 = (bf16[640,1152]{1,0:T(8,128)(2,1)}, bf16[640,1152]{1,0:T(8,128)(2,1)}, u32[]{:S(2)}, u32[]{:S(2)}) collective-permute-start(bf16[640,1152]{1,0:T(8,128)(2,1)} %pad_maximum_fusion.1), channel_id=1, source_target_pairs={{0,32},{32,0},{1,33},{33,1},{2,34},{34,2},{3,35},{35,3},{4,36},{36... | collective-permute-start | bytes 4423688 | tf_op jit(solution)/shard_map/ppermute | solution.py:16
  32.9 1.8 %fusion.108 = f32[320,1152]{1,0:T(8,128)} fusion(f32[320,320]{0,1:T(8,128)S(1)} %get-tuple-element.8, bf16[320,1152]{1,0:T(8,128)(2,1)S(1)} %collective-permute-done.1, f32[320]{0:T(512)S(1)} %add_rsqrt_fusion.3), kind=kOutput, calls=%fused_computation.153 | convolution fusion | flops 237445120 | bytes 2622720 | tf_op jit(solution)/shard_map/dot_general | solution.py:65
  34.8 2.6 %fusion.84 = f32[320,1152]{1,0:T(8,128)} fusion(bf16[320,1152]{1,0:T(8,128)(2,1)S(1)} %copy-done, f32[320]{0:T(512)S(1)} %add_rsqrt_fusion.5, bf16[320,1152]{1,0:T(8,128)(2,1)S(1)} %collective-permute-done.1, f32[320]{0:T(512)S(1)} %add_rsqrt_fusion.3), kind=kOutput, calls=%fused_computation.119 | convolution fusion | flops 475791360 | bytes 2951680 | tf_op jit(solution)/shard_map/dot_general | solution.py:65
  43.3 1.8 %convolution_add_fusion.6 = f32[320,1152]{1,0:T(8,128)} fusion(f32[320,1152]{1,0:T(8,128)S(1)} %copy-done.8, bf16[640,1152]{1,0:T(8,128)(2,1)S(1)} %fusion.10, f32[320,320]{0,1:T(8,128)S(1)} %get-tuple-element.16), kind=kOutput, calls=%fused_computation.14 | convolution fusion | flops 236707840 | bytes 4177920 | tf_op jit(solution)/shard_map/dot_general | solution.py:65
  45.0 4.4 %convolution_add_fusion.3 = f32[320,1152]{1,0:T(8,128)} fusion(f32[320,1152]{1,0:T(8,128)} %fusion.85, bf16[640,1152]{1,0:T(8,128)(2,1)} %copy-done.3, bf16[320,1152]{1,0:T(8,128)(2,1)S(1)} %copy-done.1, f32[320]{0:T(512)S(1)} %add_rsqrt_fusion.4), kind=kOutput, calls=%fused_computation.9 | convolution fusion | flops 473948160 | bytes 5162240 | tf_op jit(solution)/shard_map/dot_general | solution.py:65
  49.4 4.4 %convolution_add_fusion.1 = f32[320,1152]{1,0:T(8,128)} fusion(f32[320,1152]{1,0:T(8,128)} %fusion.84, bf16[640,1152]{1,0:T(8,128)(2,1)} %copy-done.3, bf16[320,1152]{1,0:T(8,128)(2,1)S(1)} %collective-permute-done.1, f32[320]{0:T(512)S(1)} %add_rsqrt_fusion.3), kind=kOutput, calls=%fused_computation.6 | convolution fusion | flops 473948160 | bytes 5162240 | tf_op jit(solution)/shard_map/dot_general | solution.py:65
  55.5 2.8 %fusion.12 = bf16[640,1152]{1,0:T(8,128)(2,1)} fusion(bf16[640,1152]{1,0:T(8,128)(2,1)} %collective-permute-done.3, f32[640]{0:T(1024)S(1)} %add_rsqrt_fusion), kind=kLoop, calls=%fused_computation.23 | loop fusion | flops 2211840 | bytes 2951680 | tf_op jit(solution)/shard_map/convert_element_type | solution.py:42
  58.3 3.8 %fusion.83 = f32[320,1152]{1,0:T(8,128)} fusion(bf16[640,1152]{1,0:T(8,128)(2,1)} %fusion.12, bf16[320,1152]{1,0:T(8,128)(2,1)S(1)} %collective-permute-done.1, f32[320]{0:T(512)S(1)} %add_rsqrt_fusion.3), kind=kOutput, calls=%fused_computation.118 | convolution fusion | flops 473579520 | bytes 3687680 | tf_op jit(solution)/shard_map/dot_general | solution.py:65
  62.2 4.1 %fusion.13 = bf16[320,1152]{1,0:T(8,128)(2,1)} fusion(f32[320,1152]{1,0:T(8,128)} %fusion.83, f32[320,1152]{1,0:T(8,128)} %convolution_add_fusion.1, bf16[320,1152]{1,0:T(8,128)(2,1)S(1)} %collective-permute-done.2, f32[320]{0:T(512)S(1)} %add_rsqrt_fusion.2, bf16[320,1152]{1,0:T(8,128)(2,1)S(1)} %collective-permute-done.1, f32[320]{0:T(512)S(1)} %add_rsqrt_fusion.3), kind=kOutput, calls=%fused_computation.24 | convolution fusion | flops 477265920 | bytes 5163520 | tf_op jit(solution)/shard_map/dot_general | solution.py:65
  66.3 2.3 %collective-permute-start.6 = (bf16[320,1152]{1,0:T(8,128)(2,1)}, bf16[320,1152]{1,0:T(8,128)(2,1)}, u32[]{:S(2)}, u32[]{:S(2)}) collective-permute-start(bf16[320,1152]{1,0:T(8,128)(2,1)} %fusion.13), channel_id=1, source_target_pairs={{0,1},{1,0},{2,3},{3,2},{4,5},{5,4},{6,7},{7,6},{8,9},{9,8},{10,11... | collective-permute-start | bytes 2211848 | tf_op jit(solution)/shard_map/ppermute | solution.py:16
  68.5 2.0 %log-plus-one_reduce_fusion = (f32[320]{0:T(512)S(1)}, f32[320,320]{0,1:T(8,128)S(1)}) fusion(bf16[640,1152]{1,0:T(8,128)(2,1)} %fusion.12, bf16[320,1152]{1,0:T(8,128)(2,1)S(1)} %collective-permute-done.2, f32[320]{0:T(512)S(1)} %add_rsqrt_fusion.2), kind=kOutput, calls=%fused_computation.134 | convolution fusion | flops 237342400 | bytes 1886720 | tf_op jit(solution)/shard_map/dot_general | solution.py:26
  73.9 4.6 %collective-permute-start.5 = (bf16[320,1152]{1,0:T(8,128)(2,1)}, bf16[320,1152]{1,0:T(8,128)(2,1)S(1)}, u32[]{:S(2)}, u32[]{:S(2)}) collective-permute-start(bf16[320,1152]{1,0:T(8,128)(2,1)} %fusion.14), channel_id=1, source_target_pairs={{0,16},{16,0},{1,17},{17,1},{2,18},{18,2},{3,19},{19,3},{4,20},{20... | collective-permute-start | bytes 2211848 | tf_op jit(solution)/shard_map/ppermute | solution.py:16
  78.6 2.1 %collective-permute-start.4 = (f32[320]{0:T(512)S(1)}, f32[320]{0:T(512)S(1)}, u32[]{:S(2)}, u32[]{:S(2)}) collective-permute-start(f32[320]{0:T(512)S(1)} %add_add_fusion), channel_id=1, source_target_pairs={{0,16},{16,0},{1,17},{17,1},{2,18},{18,2},{3,19},{19,3},{4,20},{20... | collective-permute-start | bytes 3848 | tf_op jit(solution)/shard_map/ppermute | solution.py:16
  83.3 12.0 %collective-permute-done.4 = f32[320]{0:T(512)S(1)} collective-permute-done((f32[320]{0:T(512)S(1)}, f32[320]{0:T(512)S(1)}, u32[]{:S(2)}, u32[]{:S(2)}) %collective-permute-start.4) | collective-permute-done | bytes 1312 | tf_op jit(solution)/shard_map/ppermute | solution.py:16
  96.0 4.6 %fusion.25 = (f32[320]{0:T(512)S(1)}, f32[320,1152]{1,0:T(8,128)}) fusion(bf16[320,1152]{1,0:T(8,128)(2,1)S(1)} %copy-done.1, f32[320]{0:T(512)S(1)} %add_rsqrt_fusion.4, bf16[320,1152]{1,0:T(8,128)(2,1)} %collective-permute-done.6, f32[320,1152]{1,0:T(8,128)} %convolution_add_fusion.3, bf16[640,1152]{1,0:T(8,128)(2,1)} %fusion.12), kind=kOutput, calls=%fused_computation.44 | convolution fusion | flops 476528320 | bytes 6640896 | tf_op jit(solution)/shard_map/dot_general | solution.py:65
  100.6 2.9 %fusion.27 = f32[320,1152]{1,0:T(8,128)} fusion(f32[320,1152]{1,0:T(8,128)} %get-tuple-element.20, bf16[320,1152]{1,0:T(8,128)(2,1)S(1)} %copy-done.1, f32[320]{0:T(512)S(1)} %get-tuple-element.19, f32[320]{0:T(512)S(1)} %add_rsqrt_fusion.4), kind=kLoop, calls=%fused_computation.46 | loop fusion | flops 1843200 | bytes 3688960 | tf_op jit(solution)/shard_map/mul | solution.py:31
  104.4 2.2 %fusion.21 = (f32[320]{0:T(512)S(1)}, f32[320,1152]{1,0:T(8,128)S(1)}) fusion(bf16[320,1152]{1,0:T(8,128)(2,1)S(1)} %copy-done, f32[320]{0:T(512)S(1)} %add_rsqrt_fusion.5, bf16[320,1152]{1,0:T(8,128)(2,1)} %copy-done.9, f32[320,1152]{1,0:T(8,128)S(1)} %copy-done.6, f32[320,1152]{1,0:T(8,128)S(1)} %copy-done.2, ...), kind=kOutput, calls=%fused_computation.40 | convolution fusion | flops 240762560 | bytes 7048960 | tf_op jit(solution)/shard_map/dot_general | solution.py:65
  (53 shorter events, 21.4 us)
Async XLA Ops:
  0.6 15.6 %copy-start.1 = (bf16[320,1152]{1,0:T(8,128)(2,1)S(1)}, bf16[320,1152]{1,0:T(8,128)(2,1)}, u32[]{:S(2)}) copy-start(bf16[320,1152]{1,0:T(8,128)(2,1)} %param.3) | copy-start | bytes 2211844
  0.6 15.3 %copy-start = (bf16[320,1152]{1,0:T(8,128)(2,1)S(1)}, bf16[320,1152]{1,0:T(8,128)(2,1)}, u32[]{:S(2)}) copy-start(bf16[320,1152]{1,0:T(8,128)(2,1)} %param.2) | copy-start | bytes 2211844
  0.6 21.2 %collective-permute-start.1 = (bf16[320,1152]{1,0:T(8,128)(2,1)}, bf16[320,1152]{1,0:T(8,128)(2,1)S(1)}, u32[]{:S(2)}, u32[]{:S(2)}) collective-permute-start(bf16[320,1152]{1,0:T(8,128)(2,1)} %param.3), channel_id=1, source_target_pairs={{0,1},{1,0},{2,3},{3,2},{4,5},{5,4},{6,7},{7,6},{8,9},{9,8},{10,11... | collective-permute-start | bytes 2211848 | tf_op jit(solution)/shard_map/ppermute | solution.py:16
  5.2 19.3 %collective-permute-start.2 = (bf16[320,1152]{1,0:T(8,128)(2,1)}, bf16[320,1152]{1,0:T(8,128)(2,1)S(1)}, u32[]{:S(2)}, u32[]{:S(2)}) collective-permute-start(bf16[320,1152]{1,0:T(8,128)(2,1)} %param.2), channel_id=1, source_target_pairs={{0,16},{16,0},{1,17},{17,1},{2,18},{18,2},{3,19},{19,3},{4,20},{20... | collective-permute-start | bytes 2211848 | tf_op jit(solution)/shard_map/ppermute | solution.py:16
  12.4 24.9 %collective-permute-start = (bf16[640,1152]{1,0:T(8,128)(2,1)}, bf16[640,1152]{1,0:T(8,128)(2,1)}, u32[]{:S(2)}, u32[]{:S(2)}) collective-permute-start(bf16[640,1152]{1,0:T(8,128)(2,1)} %pad_maximum_fusion), channel_id=1, source_target_pairs={{0,32},{32,0},{1,33},{33,1},{2,34},{34,2},{3,35},{35,3},{4,36},{36... | collective-permute-start | bytes 4423688 | tf_op jit(solution)/shard_map/ppermute | solution.py:16
  25.7 28.1 %collective-permute-start.3 = (bf16[640,1152]{1,0:T(8,128)(2,1)}, bf16[640,1152]{1,0:T(8,128)(2,1)}, u32[]{:S(2)}, u32[]{:S(2)}) collective-permute-start(bf16[640,1152]{1,0:T(8,128)(2,1)} %pad_maximum_fusion.1), channel_id=1, source_target_pairs={{0,32},{32,0},{1,33},{33,1},{2,34},{34,2},{3,35},{35,3},{4,36},{36... | collective-permute-start | bytes 4423688 | tf_op jit(solution)/shard_map/ppermute | solution.py:16
  40.8 2.5 %copy-start.3 = (bf16[640,1152]{1,0:T(8,128)(2,1)}, bf16[640,1152]{1,0:T(8,128)(2,1)S(1)}, u32[]{:S(2)}) copy-start(bf16[640,1152]{1,0:T(8,128)(2,1)S(1)} %fusion.10) | copy-start | bytes 4423684
  41.6 1.6 %copy-start.8 = (f32[320,1152]{1,0:T(8,128)S(1)}, f32[320,1152]{1,0:T(8,128)}, u32[]{:S(2)}) copy-start(f32[320,1152]{1,0:T(8,128)} %fusion.106) | copy-start | bytes 4423684
  66.3 4.2 %copy-start.7 = (bf16[640,1152]{1,0:T(8,128)(2,1)S(1)}, bf16[640,1152]{1,0:T(8,128)(2,1)}, u32[]{:S(2)}) copy-start(bf16[640,1152]{1,0:T(8,128)(2,1)} %fusion.12) | copy-start | bytes 4423684
  66.3 29.7 %collective-permute-start.6 = (bf16[320,1152]{1,0:T(8,128)(2,1)}, bf16[320,1152]{1,0:T(8,128)(2,1)}, u32[]{:S(2)}, u32[]{:S(2)}) collective-permute-start(bf16[320,1152]{1,0:T(8,128)(2,1)} %fusion.13), channel_id=1, source_target_pairs={{0,1},{1,0},{2,3},{3,2},{4,5},{5,4},{6,7},{7,6},{8,9},{9,8},{10,11... | collective-permute-start | bytes 2211848 | tf_op jit(solution)/shard_map/ppermute | solution.py:16
  70.5 1.4 %copy-start.4 = (bf16[640,1152]{1,0:T(8,128)(2,1)S(1)}, bf16[640,1152]{1,0:T(8,128)(2,1)}, u32[]{:S(2)}) copy-start(bf16[640,1152]{1,0:T(8,128)(2,1)} %copy-done.3) | copy-start | bytes 4423684
  70.5 1.8 %copy-start.5 = (f32[320,1152]{1,0:T(8,128)S(1)}, f32[320,1152]{1,0:T(8,128)}, u32[]{:S(2)}) copy-start(f32[320,1152]{1,0:T(8,128)} %fusion.108) | copy-start | bytes 4423684
  70.5 1.9 %copy-start.10 = (f32[320,320]{0,1:T(8,128)S(1)}, f32[320,320]{0,1:T(8,128)}, u32[]{:S(2)}) copy-start(f32[320,320]{0,1:T(8,128)} %get-tuple-element.6) | copy-start | bytes 1228804
  73.9 29.6 %collective-permute-start.5 = (bf16[320,1152]{1,0:T(8,128)(2,1)}, bf16[320,1152]{1,0:T(8,128)(2,1)S(1)}, u32[]{:S(2)}, u32[]{:S(2)}) collective-permute-start(bf16[320,1152]{1,0:T(8,128)(2,1)} %fusion.14), channel_id=1, source_target_pairs={{0,16},{16,0},{1,17},{17,1},{2,18},{18,2},{3,19},{19,3},{4,20},{20... | collective-permute-start | bytes 2211848 | tf_op jit(solution)/shard_map/ppermute | solution.py:16
  78.6 16.8 %collective-permute-start.4 = (f32[320]{0:T(512)S(1)}, f32[320]{0:T(512)S(1)}, u32[]{:S(2)}, u32[]{:S(2)}) collective-permute-start(f32[320]{0:T(512)S(1)} %add_add_fusion), channel_id=1, source_target_pairs={{0,16},{16,0},{1,17},{17,1},{2,18},{18,2},{3,19},{19,3},{4,20},{20... | collective-permute-start | bytes 3848 | tf_op jit(solution)/shard_map/ppermute | solution.py:16
  100.6 3.8 %copy-start.2 = (f32[320,1152]{1,0:T(8,128)S(1)}, f32[320,1152]{1,0:T(8,128)}, u32[]{:S(2)}) copy-start(f32[320,1152]{1,0:T(8,128)} %convolution_add_fusion.6) | copy-start | bytes 4423684
  100.6 3.8 %copy-start.6 = (f32[320,1152]{1,0:T(8,128)S(1)}, f32[320,1152]{1,0:T(8,128)}, u32[]{:S(2)}) copy-start(f32[320,1152]{1,0:T(8,128)} %fusion.98) | copy-start | bytes 4423684
  103.5 0.9 copy-start.9

commit v2 on v1

v2 whole, which is shorter than its diff:
```python
import jax
import jax.numpy as jnp
from jax import lax
from jax.experimental import pallas as pl
from jax.experimental.pallas import tpu as pltpu
from jax.sharding import Mesh
from jax.sharding import PartitionSpec as P

LOGIT_SCALE = 8.0
LOGIT_BIAS = -4.0
EPSILON = 1e-06
ROW_COL = (((1,), (1,)), ((), ()))
PLAIN = (((1,), (0,)), ((), ()))
SWAP = ((0, 1), (1, 0))
AXES = ("outer", "core", "x_hi", "z_hi", "z_lo")
F32, BF16 = jnp.float32, jnp.bfloat16
MIB = 1024 * 1024


def swap(value, axis):
    return lax.ppermute(value, axis, SWAP)


def call(body, shapes, args, edges=0):
    spec = pl.BlockSpec(memory_space=pltpu.VMEM)
    rows, depth = args[0].shape[-2:]
    nbytes = sum(a.size * a.dtype.itemsize for a in args)
    return pl.pallas_call(
        body,
        out_shape=[jax.ShapeDtypeStruct(s, d) for s, d in shapes],
        in_specs=[spec] * len(args),
        out_specs=[spec] * len(shapes),
        compiler_params=pltpu.CompilerParams(vmem_limit_bytes=40 * MIB),
        cost_estimate=pl.CostEstimate(
            flops=max(1, edges) * 4 * 320 * 320 * depth, bytes_accessed=nbytes, transcendentals=0
        ),
    )(*args)


def normalize_rows(raw_rows):
    widened = raw_rows.astype(F32)
    inverse = lax.rsqrt(jnp.sum(widened * widened, axis=1, keepdims=True) + EPSILON)
    return (widened * inverse, inverse)


def norm_two(first, second, out):
    rows = first.shape[0]
    out[pl.ds(0, rows), :] = normalize_rows(first[...])[0].astype(BF16)
    out[pl.ds(rows, rows), :] = normalize_rows(second[...])[0].astype(BF16)


def eye(rows):
    r = lax.broadcasted_iota(jnp.int32, (rows, rows), 0)
    c = lax.broadcasted_iota(jnp.int32, (rows, rows), 1)
    return r == c


def as_row(column):
    return jnp.sum(jnp.where(eye(column.shape[0]), column, 0.0), axis=0, keepdims=True)


def edge(left, right, positive=False, losses=False):
    logits = lax.dot_general(left, right, ROW_COL, preferred_element_type=F32)
    logits = LOGIT_SCALE * logits + LOGIT_BIAS
    grown = jnp.exp(logits)
    whole = 1.0 + grown
    part = 1.0 / whole
    weights = grown * part
    loss = None
    if losses:
        soft = jnp.log(whole) + (grown - (whole - 1.0)) * part
        if positive:
            soft = jnp.where(eye(left.shape[0]), soft - logits, soft)
        loss = jnp.sum(soft, axis=1, keepdims=True)
    if positive:
        weights = jnp.where(eye(left.shape[0]), weights - 1.0, weights)
    share = lax.dot_general(weights.astype(BF16), right, PLAIN, preferred_element_type=F32)
    return share, loss


def own_body(own, mate, i_out, t_out, loss_out):
    rows = i_out.shape[0]
    image, text = own[pl.ds(0, rows), :], own[pl.ds(rows, rows), :]
    mate_image, mate_text = mate[pl.ds(0, rows), :], mate[pl.ds(rows, rows), :]
    first, loss = edge(image, text, True, True)
    second, more = edge(image, mate_text, False, True)
    i_out[...] = first + second
    loss_out[...] = as_row(loss + more)
    first, _ = edge(text, image, True)
    second, _ = edge(text, mate_image)
    t_out[...] = first + second


def mid_body(own, mate, near, x_out, z_out, loss_out):
    rows = x_out.shape[0]
    image, mate_image, mate_text = own[pl.ds(0, rows), :], mate[pl.ds(0, rows), :], mate[pl.ds(rows, rows), :]
    x_image, z_text = near[pl.ds(0, rows), :], near[pl.ds(rows, rows), :]
    first, loss = edge(x_image, mate_text, False, True)
    second, more = edge(x_image, z_text, False, True)
    x_out[...] = first + second
    loss_out[...] = as_row(loss + more)
    total = edge(z_text, image)[0] + edge(z_text, mate_image)[0] + edge(z_text, x_image)[0]
    z_out[...] = total


def back_body(near, far, x_in, z_in, loss_in, x_out, z_out, loss_out):
    rows = x_out.shape[0]
    x_image, z_text = near[pl.ds(0, rows), :], near[pl.ds(rows, rows), :]
    far_image, far_text = far[pl.ds(0, rows), :], far[pl.ds(rows, rows), :]
    share, loss = edge(x_image, far_text, False, True)
    x_out[...] = (LOGIT_SCALE * (x_in[...] + share)).astype(BF16)
    loss_out[...] = loss_in[...] + as_row(loss)
    share, _ = edge(z_text, far_image)
    z_out[...] = (LOGIT_SCALE * (z_in[...] + share)).astype(BF16)


def rest_body(own, near, far, i_in, t_in, loss_in, i_out, t_out, loss_out):
    rows = i_out.shape[0]
    image, text = own[pl.ds(0, rows), :], own[pl.ds(rows, rows), :]
    z_text = near[pl.ds(rows, rows), :]
    far_image, far_text = far[pl.ds(0, rows), :], far[pl.ds(rows, rows), :]
    first, loss = edge(image, z_text, False, True)
    second, more = edge(image, far_text, False, True)
    i_out[...] = i_in[...] + first + second
    loss_out[...] = loss_in[...] + as_row(loss + more)
    t_out[...] = t_in[...] + edge(text, far_image)[0]


def raw_gradient(raw, total, back):
    unit, inverse = normalize_rows(raw)
    gradient = LOGIT_SCALE * total + back.astype(F32)
    return inverse * (gradient - unit * jnp.sum(unit * gradient, axis=1, keepdims=True))


def last_body(image, text, i_in, t_in, x_back, z_back, loss_in, loss_back, loss_out, i_out, t_out):
    loss_out[...] = (loss_in[...] + loss_back[...]) * (1.0 / image.shape[0])
    i_out[...] = raw_gradient(image[...], i_in[...], x_back[...])
    t_out[...] = raw_gradient(text[...], t_in[...], z_back[...])


def shards(image, text):
    rows, depth = image.shape
    pair, block, line = (2 * rows, depth), (rows, depth), (1, rows)
    x_image = swap(image, "x_hi")
    z_text = swap(text, "z_lo")
    (own,) = call(norm_two, [(pair, BF16)], (image, text))
    mate = swap(own, "core")
    i_total, t_total, i_loss = call(own_body, [(block, F32), (block, F32), (line, F32)], (own, mate), 4)
    (near,) = call(norm_two, [(pair, BF16)], (x_image, z_text))
    far = swap(near, "core")
    x_total, z_total, x_loss = call(
        mid_body, [(block, F32), (block, F32), (line, F32)], (own, mate, near), 5
    )
    x_share, z_share, x_loss = call(
        back_body, [(block, BF16), (block, BF16), (line, F32)], (near, far, x_total, z_total, x_loss), 2
    )
    x_back = swap(x_share, "x_hi")
    z_back = swap(z_share, "z_lo")
    loss_back = swap(x_loss, "x_hi")
    i_total, t_total, i_loss = call(
        rest_body, [(block, F32), (block, F32), (line, F32)], (own, near, far, i_total, t_total, i_loss), 3
    )
    loss, image_grad, text_grad = call(
        last_body,
        [(line, F32), (block, F32), (block, F32)],
        (image, text, i_total, t_total, x_back, z_back, i_loss, loss_back),
    )
    return (loss.reshape(rows), image_grad, text_grad)


def solution(mesh):
    n_row, n_col = mesh.devices.shape
    fine = Mesh(mesh.devices.reshape(n_row // 2, 2, 2, n_col // 4, 2), AXES)
    return jax.shard_map(
        shards,
        mesh=fine,
        in_specs=(P(AXES, None), P(AXES, None)),
        out_specs=(P(AXES), P(AXES, None), P(AXES, None)),
        check_vma=False,
    )
```

time: 109 us -> 62.1 us (0.57)
  matrix products: 45.9 us -> 0 us
  Pallas kernels: 0 us -> 17.5 us
  other arithmetic: 17.7 us -> 0.6 us
  waiting for transfers between devices: 14.5 us -> 12.8 us
    dot_general x21 -> x0, matrix products: 45.9 us -> none  [the longest x14 38 us: group(): total = total + jnp.dot(weights, right, preferred_element_type=jnp.float32)]
    pallas_call x0 -> x7, Pallas kernels: none -> 17.5 us  [call(): pl.pallas_call(body, out_shape=[jax.ShapeDtypeStruct(s, d) for s, d in sh...]
    convert_element_type x2 -> x0, other arithmetic: 4.48 us -> none  [unit(): return normalize_rows(raw)[0].astype(jnp.bfloat16)]
    reduce_sum x6 -> x0, other arithmetic: 4.42 us -> none  [normalize_rows(): jnp.sum(widened * widened, axis=1, keepdims=True) + EPSILON]
    mul x2 -> x0, other arithmetic: 4.37 us -> none  [raw_gradient(): inverse * (gradient - normed * jnp.sum(normed * gradient, axis=1, keepdim...]
    concatenate x2 -> x0, other arithmetic: 3.78 us -> none  [the longest x1 2.56 us: shards(): mate = swap(jnp.concatenate([image, text], axis=0), 'core')]
    ppermute x7, waiting for transfers between devices: 14.5 us -> 12.8 us  [swap(): return lax.ppermute(value, axis, SWAP)]
    unnamed x22 -> x8, local copies, waits for them, and re-layouts: 2.18 us -> 2.24 us
  transfers between devices with their start and end apart: 7 -> 7, of which waited for: 2 -> 4; matrix products, arithmetic and copies ran while one was open for 44% -> 0% of each run, Pallas kernels for 0% -> 21%
where the time goes in v2:
time: 62.1 us; the launch traced here: 61.7 us
  starting transfers between devices  27.8 us (45%)
  Pallas kernels  17.5 us (28%)
  waiting for transfers between devices  12.8 us (21%)
  local copies, waits for them, and re-layouts  2.24 us (4%)
  between operations  0.76 us (1%)
    ppermute x7, starting transfers between devices, swap(): return lax.ppermute(value, axis, SWAP)  27.8 us
    pallas_call x7, Pallas kernels, call(): pl.pallas_call(body, out_shape=[jax.ShapeDtypeStruct(s, d) for s, d in sh...  17.5 us
    ppermute x7, waiting for transfers between devices, swap(): return lax.ppermute(value, axis, SWAP)  12.8 us
    unnamed x8, local copies, waits for them, and re-layouts  2.24 us
  transfers between devices with their start and end apart: 7, of which 4 were waited for; matrix products, arithmetic and copies ran while one was open for 0% of the time, Pallas kernels for 21%

profile of v2, /device:TPU:1, one launch (start us, length us, event | category | flops | bytes accessed | tf_op | source)
XLA Modules:
  0.0 61.7 jit_solution(3391912848436084163)
XLA Ops:
  0.6 5.5 %collective-permute-start = (bf16[320,1152]{1,0:T(8,128)(2,1)}, bf16[320,1152]{1,0:T(8,128)(2,1)S(1)}, u32[]{:S(2)}, u32[]{:S(2)}) collective-permute-start(bf16[320,1152]{1,0:T(8,128)(2,1)} %image.1), channel_id=1, source_target_pairs={{0,16},{16,0},{1,17},{17,1},{2,18},{18,2},{3,19},{19,3},{4,20},{20... | collective-permute-start | bytes 2211848 | tf_op jit(solution)/shard_map/ppermute | solution.py:21
  6.1 3.5 %collective-permute-start.1 = (bf16[320,1152]{1,0:T(8,128)(2,1)}, bf16[320,1152]{1,0:T(8,128)(2,1)S(1)}, u32[]{:S(2)}, u32[]{:S(2)}) collective-permute-start(bf16[320,1152]{1,0:T(8,128)(2,1)} %text.1), channel_id=1, source_target_pairs={{0,1},{1,0},{2,3},{3,2},{4,5},{5,4},{6,7},{7,6},{8,9},{9,8},{10,11... | collective-permute-start | bytes 2211848 | tf_op jit(solution)/shard_map/ppermute | solution.py:21
  9.7 0.0 copy-start
  9.7 1.1 %copy-done = bf16[320,1152]{1,0:T(8,128)(2,1)S(1)} copy-done((bf16[320,1152]{1,0:T(8,128)(2,1)S(1)}, bf16[320,1152]{1,0:T(8,128)(2,1)}, u32[]{:S(2)}) %copy-start) | copy-done | bytes 737304
  10.8 1.1 %copy-done.2 = bf16[320,1152]{1,0:T(8,128)(2,1)S(1)} copy-done((bf16[320,1152]{1,0:T(8,128)(2,1)S(1)}, bf16[320,1152]{1,0:T(8,128)(2,1)}, u32[]{:S(2)}) %copy-start.2) | copy-done | bytes 737304
  11.9 0.5 shard_map.49.own
  12.4 3.6 %collective-permute-start.3 = (bf16[640,1152]{1,0:T(8,128)(2,1)S(1)}, bf16[640,1152]{1,0:T(8,128)(2,1)S(1)}, u32[]{:S(2)}, u32[]{:S(2)}) collective-permute-start(bf16[640,1152]{1,0:T(8,128)(2,1)S(1)} %shard_map.49.own), channel_id=1, source_target_pairs={{0,32},{32,0},{1,33},{33,1},{2,34},{34,2},{3,35},{35,3},{4,36},{36... | collective-permute-start | bytes 4423688 | tf_op jit(solution)/shard_map/ppermute | solution.py:21
  16.0 3.2 %collective-permute-done.first = bf16[320,1152]{1,0:T(8,128)(2,1)S(1)} collective-permute-done((bf16[320,1152]{1,0:T(8,128)(2,1)}, bf16[320,1152]{1,0:T(8,128)(2,1)S(1)}, u32[]{:S(2)}, u32[]{:S(2)}) %collective-permute-start) | collective-permute-done | bytes 737312 | tf_op jit(solution)/shard_map/ppermute | solution.py:21
  19.2 5.2 %collective-permute-done.1.second = bf16[320,1152]{1,0:T(8,128)(2,1)S(1)} collective-permute-done((bf16[320,1152]{1,0:T(8,128)(2,1)}, bf16[320,1152]{1,0:T(8,128)(2,1)S(1)}, u32[]{:S(2)}, u32[]{:S(2)}) %collective-permute-start.1) | collective-permute-done | bytes 737312 | tf_op jit(solution)/shard_map/ppermute | solution.py:21
  24.3 0.5 shard_map.50.near
  24.8 4.9 %collective-permute-start.2 = (bf16[640,1152]{1,0:T(8,128)(2,1)S(1)}, bf16[640,1152]{1,0:T(8,128)(2,1)S(1)}, u32[]{:S(2)}, u32[]{:S(2)}) collective-permute-start(bf16[640,1152]{1,0:T(8,128)(2,1)S(1)} %shard_map.50.near), channel_id=1, source_target_pairs={{0,32},{32,0},{1,33},{33,1},{2,34},{34,2},{3,35},{35,3},{4,36},{36... | collective-permute-start | bytes 4423688 | tf_op jit(solution)/shard_map/ppermute | solution.py:21
  29.7 4.8 %shard_map.53 = (f32[320,1152]{1,0:T(8,128)S(1)}, f32[320,1152]{1,0:T(8,128)S(1)}, f32[1,320]{1,0:T(1,128)S(1)}) custom-call(bf16[640,1152]{1,0:T(8,128)(2,1)S(1)} %shard_map.49.own, bf16[640,1152]{1,0:T(8,128)(2,1)S(1)} %collective-permute-done.3.mate, bf16[640,1152]{1,0:T(8,128)(2,1)S(1)} %shard_map.50.near), custom_call_target="tpu_custom_call" | custom-call | flops 2359296000 | bytes 4423680 | tf_op jit(solution)/shard_map/pallas_call | solution.py:28
  34.5 2.1 %shard_map.54 = (bf16[320,1152]{1,0:T(8,128)(2,1)S(1)}, bf16[320,1152]{1,0:T(8,128)(2,1)S(1)}, f32[1,320]{1,0:T(1,128)S(1)}) custom-call(bf16[640,1152]{1,0:T(8,128)(2,1)S(1)} %shard_map.50.near, bf16[640,1152]{1,0:T(8,128)(2,1)S(1)} %collective-permute-done.2.far, f32[320,1152]{1,0:T(8,128)S(1)} %get-tuple-element.23.x_in, ...), custom_call_target="tpu_custom_call" | custom-call | flops 943718400 | bytes 5899520 | tf_op jit(solution)/shard_map/pallas_call | solution.py:28
  36.6 2.1 %collective-permute-start.4 = (bf16[320,1152]{1,0:T(8,128)(2,1)S(1)}, bf16[320,1152]{1,0:T(8,128)(2,1)S(1)}, u32[]{:S(2)}, u32[]{:S(2)}) collective-permute-start(bf16[320,1152]{1,0:T(8,128)(2,1)S(1)} %get-tuple-element.26), channel_id=1, source_target_pairs={{0,16},{16,0},{1,17},{17,1},{2,18},{18,2},{3,19},{19,3},{4,20},{20... | collective-permute-start | bytes 2211848 | tf_op jit(solution)/shard_map/ppermute | solution.py:21
  38.7 3.4 %collective-permute-start.5 = (bf16[320,1152]{1,0:T(8,128)(2,1)S(1)}, bf16[320,1152]{1,0:T(8,128)(2,1)S(1)}, u32[]{:S(2)}, u32[]{:S(2)}) collective-permute-start(bf16[320,1152]{1,0:T(8,128)(2,1)S(1)} %get-tuple-element.27), channel_id=1, source_target_pairs={{0,1},{1,0},{2,3},{3,2},{4,5},{5,4},{6,7},{7,6},{8,9},{9,8},{10,11... | collective-permute-start | bytes 2211848 | tf_op jit(solution)/shard_map/ppermute | solution.py:21
  42.1 3.9 %shard_map.51 = (f32[320,1152]{1,0:T(8,128)S(1)}, f32[320,1152]{1,0:T(8,128)S(1)}, f32[1,320]{1,0:T(1,128)S(1)}) custom-call(bf16[640,1152]{1,0:T(8,128)(2,1)S(1)} %shard_map.49.own, bf16[640,1152]{1,0:T(8,128)(2,1)S(1)} %collective-permute-done.3.mate), custom_call_target="tpu_custom_call" | custom-call | flops 1887436800 | bytes 2949120 | tf_op jit(solution)/shard_map/pallas_call | solution.py:28
  46.0 4.8 %collective-permute-start.6 = (f32[1,320]{1,0:T(1,128)S(1)}, f32[1,320]{1,0:T(1,128)S(1)}, u32[]{:S(2)}, u32[]{:S(2)}) collective-permute-start(f32[1,320]{1,0:T(1,128)S(1)} %get-tuple-element.29), channel_id=1, source_target_pairs={{0,16},{16,0},{1,17},{17,1},{2,18},{18,2},{3,19},{19,3},{4,20},{20... | collective-permute-start | bytes 3848 | tf_op jit(solution)/shard_map/ppermute | solution.py:21
  50.8 0.0 copy-start.1
  50.8 0.0 copy-start.3
  50.8 3.2 %shard_map.52 = (f32[320,1152]{1,0:T(8,128)S(1)}, f32[320,1152]{1,0:T(8,128)S(1)}, f32[1,320]{1,0:T(1,128)S(1)}) custom-call(bf16[640,1152]{1,0:T(8,128)(2,1)S(1)} %shard_map.49.own, bf16[640,1152]{1,0:T(8,128)(2,1)S(1)} %shard_map.50.near, bf16[640,1152]{1,0:T(8,128)(2,1)S(1)} %collective-permute-done.2.far, f32[320,1152]{1,0:T(8,128)S(1)} %get-tuple-element.18.i_in, ...), custom_call_target="tpu_custom_call" | custom-call | flops 1415577600 | bytes 7374080 | tf_op jit(solution)/shard_map/pallas_call | solution.py:28
  54.0 4.1 %collective-permute-done.6.loss_back = f32[1,320]{1,0:T(1,128)S(1)} collective-permute-done((f32[1,320]{1,0:T(1,128)S(1)}, f32[1,320]{1,0:T(1,128)S(1)}, u32[]{:S(2)}, u32[]{:S(2)}) %collective-permute-start.6) | collective-permute-done | bytes 1312 | tf_op jit(solution)/shard_map/ppermute | solution.py:21
  58.1 0.3 collective-permute-done.5.z_back
  58.4 2.7 %shard_map.55 = (f32[1,320]{1,0:T(1,128)S(1)}, f32[320,1152]{1,0:T(8,128)}, f32[320,1152]{1,0:T(8,128)}) custom-call(bf16[320,1152]{1,0:T(8,128)(2,1)S(1)} %copy-done.1, bf16[320,1152]{1,0:T(8,128)(2,1)S(1)} %copy-done.3, f32[320,1152]{1,0:T(8,128)S(1)} %get-tuple-element.21.i_in, f32[320,1152]{1,0:T(8,128)S(1)} %get-tuple-element.22.t_in, ...), custom_call_target="tpu_custom_call" | custom-call | flops 471859200 | bytes 5900800 | tf_op jit(solution)/shard_map/pallas_call | solution.py:28
  61.1 0.6 reduce
  (6 shorter events, 0.0 us)
Async XLA Ops:
  0.6 18.5 %collective-permute-start = (bf16[320,1152]{1,0:T(8,128)(2,1)}, bf16[320,1152]{1,0:T(8,128)(2,1)S(1)}, u32[]{:S(2)}, u32[]{:S(2)}) collective-permute-start(bf16[320,1152]{1,0:T(8,128)(2,1)} %image.1), channel_id=1, source_target_pairs={{0,16},{16,0},{1,17},{17,1},{2,18},{18,2},{3,19},{19,3},{4,20},{20... | collective-permute-start | bytes 2211848 | tf_op jit(solution)/shard_map/ppermute | solution.py:21
  6.1 18.2 %collective-permute-start.1 = (bf16[320,1152]{1,0:T(8,128)(2,1)}, bf16[320,1152]{1,0:T(8,128)(2,1)S(1)}, u32[]{:S(2)}, u32[]{:S(2)}) collective-permute-start(bf16[320,1152]{1,0:T(8,128)(2,1)} %text.1), channel_id=1, source_target_pairs={{0,1},{1,0},{2,3},{3,2},{4,5},{5,4},{6,7},{7,6},{8,9},{9,8},{10,11... | collective-permute-start | bytes 2211848 | tf_op jit(solution)/shard_map/ppermute | solution.py:21
  9.7 1.1 %copy-start = (bf16[320,1152]{1,0:T(8,128)(2,1)S(1)}, bf16[320,1152]{1,0:T(8,128)(2,1)}, u32[]{:S(2)}) copy-start(bf16[320,1152]{1,0:T(8,128)(2,1)} %image.1) | copy-start | bytes 2211844
  10.8 1.1 %copy-start.2 = (bf16[320,1152]{1,0:T(8,128)(2,1)S(1)}, bf16[320,1152]{1,0:T(8,128)(2,1)}, u32[]{:S(2)}) copy-start(bf16[320,1152]{1,0:T(8,128)(2,1)} %text.1) | copy-start | bytes 2211844
  12.4 17.3 %collective-permute-start.3 = (bf16[640,1152]{1,0:T(8,128)(2,1)S(1)}, bf16[640,1152]{1,0:T(8,128)(2,1)S(1)}, u32[]{:S(2)}, u32[]{:S(2)}) collective-permute-start(bf16[640,1152]{1,0:T(8,128)(2,1)S(1)} %shard_map.49.own), channel_id=1, source_target_pairs={{0,32},{32,0},{1,33},{33,1},{2,34},{34,2},{3,35},{35,3},{4,36},{36... | collective-permute-start | bytes 4423688 | tf_op jit(solution)/shard_map/ppermute | solution.py:21
  24.8 9.7 %collective-permute-start.2 = (bf16[640,1152]{1,0:T(8,128)(2,1)S(1)}, bf16[640,1152]{1,0:T(8,128)(2,1)S(1)}, u32[]{:S(2)}, u32[]{:S(2)}) collective-permute-start(bf16[640,1152]{1,0:T(8,128)(2,1)S(1)} %shard_map.50.near), channel_id=1, source_target_pairs={{0,32},{32,0},{1,33},{33,1},{2,34},{34,2},{3,35},{35,3},{4,36},{36... | collective-permute-start | bytes 4423688 | tf_op jit(solution)/shard_map/ppermute | solution.py:21
  36.6 21.5 %collective-permute-start.4 = (bf16[320,1152]{1,0:T(8,128)(2,1)S(1)}, bf16[320,1152]{1,0:T(8,128)(2,1)S(1)}, u32[]{:S(2)}, u32[]{:S(2)}) collective-permute-start(bf16[320,1152]{1,0:T(8,128)(2,1)S(1)} %get-tuple-element.26), channel_id=1, source_target_pairs={{0,16},{16,0},{1,17},{17,1},{2,18},{18,2},{3,19},{19,3},{4,20},{20... | collective-permute-start | bytes 2211848 | tf_op jit(solution)/shard_map/ppermute | solution.py:21
  38.7 19.7 %collective-permute-start.5 = (bf16[320,1152]{1,0:T(8,128)(2,1)S(1)}, bf16[320,1152]{1,0:T(8,128)(2,1)S(1)}, u32[]{:S(2)}, u32[]{:S(2)}) collective-permute-start(bf16[320,1152]{1,0:T(8,128)(2,1)S(1)} %get-tuple-element.27), channel_id=1, source_target_pairs={{0,1},{1,0},{2,3},{3,2},{4,5},{5,4},{6,7},{7,6},{8,9},{9,8},{10,11... | collective-permute-start | bytes 2211848 | tf_op jit(solution)/shard_map/ppermute | solution.py:21
  46.0 12.1 %collective-permute-start.6 = (f32[1,320]{1,0:T(1,128)S(1)}, f32[1,320]{1,0:T(1,128)S(1)}, u32[]{:S(2)}, u32[]{:S(2)}) collective-permute-start(f32[1,320]{1,0:T(1,128)S(1)} %get-tuple-element.29), channel_id=1, source_target_pairs={{0,16},{16,0},{1,17},{17,1},{2,18},{18,2},{3,19},{19,3},{4,20},{20... | collective-permute-start | bytes 3848 | tf_op jit(solution)/shard_map/ppermute | solution.py:21
  50.8 7.6 %copy-start.1 = (bf16[320,1152]{1,0:T(8,128)(2,1)S(1)}, bf16[320,1152]{1,0:T(8,128)(2,1)}, u32[]{:S(2)}) copy-start(bf16[320,1152]{1,0:T(8,128)(2,1)} %image.1) | copy-start | bytes 2211844
  50.8 7.6 %copy-start.3 = (bf16[320,1152]{1,0:T(8,128)(2,1)S(1)}, bf16[320,1152]{1,0:T(8,128)(2,1)}, u32[]{:S(2)}) copy-start(bf16[320,1152]{1,0:T(8,128)(2,1)} %text.1) | copy-start | bytes 2211844

commit v3 on v1

v3 whole, which is shorter than its diff:
```python
import math
from functools import partial

import jax
import jax.numpy as jnp
from jax import lax
from jax.experimental import pallas as pl
from jax.experimental.pallas import tpu as pltpu
from jax.sharding import Mesh
from jax.sharding import PartitionSpec as P

LOGIT_SCALE = 8.0
LOGIT_BIAS = -4.0
EPSILON = 1e-06
LOG2E = math.log2(math.e)
LANES = 128
ROW_COL = (((1,), (1,)), ((), ()))
PLAIN = (((1,), (0,)), ((), ()))
SWAP = ((0, 1), (1, 0))
AXES = ("outer", "core", "x_hi", "z_hi", "z_lo")
F32, BF16 = jnp.float32, jnp.bfloat16
MIB = 1024 * 1024
TOKEN = ((8, LANES), F32)


def swap(value, axis):
    return lax.ppermute(value, axis, SWAP)


def call(body, shapes, args, far_outs=(), scratch=()):
    vmem, far = pl.BlockSpec(memory_space=pltpu.VMEM), pl.BlockSpec(memory_space=pl.ANY)
    return pl.pallas_call(
        body,
        out_shape=[jax.ShapeDtypeStruct(s, d) for s, d in shapes],
        in_specs=[vmem] * len(args),
        out_specs=[far if n in far_outs else vmem for n in range(len(shapes))],
        scratch_shapes=scratch,
        compiler_params=pltpu.CompilerParams(vmem_limit_bytes=32 * MIB),
        cost_estimate=pl.CostEstimate(flops=1, bytes_accessed=1, transcendentals=0),
    )(*args)


def normalize_rows(raw_rows):
    widened = raw_rows.astype(F32)
    inverse = lax.rsqrt(jnp.sum(widened * widened, axis=1, keepdims=True) + EPSILON)
    return (widened * inverse, inverse)


def norm_body(*refs):
    pieces, out = refs[:-1], refs[-1]
    rows = pieces[0].shape[0]
    for n, piece in enumerate(pieces):
        out[pl.ds(n * rows, rows), :] = normalize_rows(piece[...])[0].astype(BF16)


def as_row(column):
    rows = column.shape[0]
    r = lax.broadcasted_iota(jnp.int32, (rows, rows), 0)
    c = lax.broadcasted_iota(jnp.int32, (rows, rows), 1)
    return jnp.sum(jnp.where(r == c, column, 0.0), axis=0, keepdims=True)


def soft_sum(grown, whole):
    total, groups = 0.0, grown.shape[1] // LANES
    carried = grown[:, :LANES]
    for n in range(1, groups):
        part = slice(n * LANES, (n + 1) * LANES)
        carried = carried * whole[:, part] + grown[:, part]
    total = jnp.sum(jnp.log1p(carried), axis=1, keepdims=True)
    if groups * LANES < grown.shape[1]:
        total = total + jnp.sum(jnp.log1p(grown[:, groups * LANES :]), axis=1, keepdims=True)
    return total


def edges(left, rights, positive=False, losses=False):
    right = jnp.concatenate(rights, axis=0)
    product = lax.dot_general(left, right, ROW_COL, preferred_element_type=F32)
    grown = jnp.exp2(product * (LOGIT_SCALE * LOG2E) + LOGIT_BIAS * LOG2E)
    whole = 1.0 + grown
    weights = grown * pltpu.reciprocal(whole, approx=True)
    if positive:
        r = lax.broadcasted_iota(jnp.int32, product.shape, 0)
        c = lax.broadcasted_iota(jnp.int32, product.shape, 1)
        weights = jnp.where(r == c, weights - 1.0, weights)
    share = lax.dot_general(weights.astype(BF16), right, PLAIN, preferred_element_type=F32)
    if not losses:
        return share
    loss = soft_sum(grown, whole)
    if positive:
        logits = LOGIT_SCALE * product + LOGIT_BIAS
        loss = loss - jnp.sum(jnp.where(r == c, logits, 0.0), axis=1, keepdims=True)
    return share, loss


def halves(ref):
    rows = ref.shape[0] // 2
    return ref[pl.ds(0, rows), :], ref[pl.ds(rows, rows), :]


def z_body(own, mate, x_near, x_far, z_near, share, token):
    image, mate_image = halves(own)[0], halves(mate)[0]
    total = edges(z_near[...], [image, mate_image, x_near[...], x_far[...]])
    share[...] = (LOGIT_SCALE * total).astype(BF16)
    token[...] = jnp.zeros(token.shape, F32)


def x_body(mate, x_near, z_near, z_far, _, share, loss):
    total, loss[...] = edges(x_near[...], [halves(mate)[1], z_near[...], z_far[...]], False, True)
    share[...] = (LOGIT_SCALE * total).astype(BF16)


def own_body(own, mate, x_far, z_near, z_far, x_loss, i_out, t_out, loss_out, x_loss_out):
    x_loss_out[...] = as_row(x_loss[...])
    image, text = halves(own)
    mate_image, mate_text = halves(mate)
    total, loss = edges(image, [text, mate_text, z_near[...], z_far[...]], True, True)
    i_out[...] = LOGIT_SCALE * total
    loss_out[...] = as_row(loss)
    t_out[...] = LOGIT_SCALE * edges(text, [image, mate_image, x_far[...]], True)


def raw_gradient(raw, gradient):
    unit, inverse = normalize_rows(raw)
    return inverse * (gradient - unit * jnp.sum(unit * gradient, axis=1, keepdims=True))


def last_body(raw, total, back, *rest):
    out, held, sems = rest[-3:]
    pieces = sems.shape[0]
    rows = raw.shape[0] // pieces
    copies = []
    for n in range(pieces):
        part = pl.ds(n * rows, rows)
        held[part, :] = raw_gradient(raw[part, :], total[part, :] + back[part, :].astype(F32))
        copies.append(pltpu.make_async_copy(held.at[part, :], out.at[part, :], sems.at[n]))
        copies[-1].start()
    for copy in copies:
        copy.wait()


def last(raw, total, back, *tokens):
    return call(
        last_body,
        [(raw.shape, F32)],
        (raw, total, back) + tokens,
        far_outs=(0,),
        scratch=[pltpu.VMEM(raw.shape, F32), pltpu.SemaphoreType.DMA((4,))],
    )[0]


def shards(image, text):
    rows, depth = image.shape
    block, pair = (rows, depth), (2 * rows, depth)
    x_near, z_near = swap(image, "x_hi"), swap(text, "z_lo")
    (own,) = call(norm_body, [(pair, BF16)], (image, text))
    mate = swap(own, "core")
    (x_near,) = call(norm_body, [(block, BF16)], (x_near,))
    x_far = swap(x_near, "core")
    (z_near,) = call(norm_body, [(block, BF16)], (z_near,))
    z_far = swap(z_near, "core")
    z_share, token = call(z_body, [(block, BF16), TOKEN], (own, mate, x_near, x_far, z_near))
    z_back = swap(z_share, "z_lo")
    x_share, x_loss = call(
        x_body, [(block, BF16), ((rows, 1), F32)], (mate, x_near, z_near, z_far, token)
    )
    x_back = swap(x_share, "x_hi")
    i_total, t_total, i_loss, x_loss = call(
        own_body,
        [(block, F32), (block, F32), ((1, rows), F32), ((1, rows), F32)],
        (own, mate, x_far, z_near, z_far, x_loss),
    )
    loss = ((i_loss + swap(x_loss, "x_hi")) * (1.0 / rows)).reshape(rows)
    text_grad = last(text, t_total, z_back)
    image_grad = last(image, i_total, x_back)
    return (loss, image_grad, text_grad)


def solution(mesh):
    n_row, n_col = mesh.devices.shape
    fine = Mesh(mesh.devices.reshape(n_row // 2, 2, 2, n_col // 4, 2), AXES)
    return jax.shard_map(
        shards,
        mesh=fine,
        in_specs=(P(AXES, None), P(AXES, None)),
        out_specs=(P(AXES), P(AXES, None), P(AXES, None)),
        check_vma=False,
    )
```

time: 109 us -> 59.9 us (0.55)
  matrix products: 45.9 us -> 0 us
  other arithmetic: 17.7 us -> 0.6 us
  Pallas kernels: 0 us -> 13.1 us
  starting transfers between devices: 27.1 us -> 32.6 us
  waiting for transfers between devices: 14.5 us -> 10.2 us
    dot_general x21 -> x0, matrix products: 45.9 us -> none  [the longest x14 38 us: group(): total = total + jnp.dot(weights, right, preferred_element_type=jnp.float32)]
    pallas_call x0 -> x8, Pallas kernels: none -> 13.1 us  [call(): pl.pallas_call(body, out_shape=[jax.ShapeDtypeStruct(s, d) for s, d in sh...]
    ppermute x7 -> x8, starting transfers between devices: 27.1 us -> 32.6 us  [swap(): return lax.ppermute(value, axis, SWAP)]
    convert_element_type x2 -> x0, other arithmetic: 4.48 us -> none  [unit(): return normalize_rows(raw)[0].astype(jnp.bfloat16)]
    reduce_sum x6 -> x0, other arithmetic: 4.42 us -> none  [normalize_rows(): jnp.sum(widened * widened, axis=1, keepdims=True) + EPSILON]
    ppermute x7 -> x8, waiting for transfers between devices: 14.5 us -> 10.2 us  [swap(): return lax.ppermute(value, axis, SWAP)]
    concatenate x2 -> x0, other arithmetic: 3.78 us -> none  [the longest x1 2.56 us: shards(): mate = swap(jnp.concatenate([image, text], axis=0), 'core')]
    mul x2 -> x1, other arithmetic: 4.37 us -> 0.6 us  [shards(): loss = ((i_loss + swap(x_loss, 'x_hi')) * (1.0 / rows)).reshape(rows)]
  transfers between devices with their start and end apart: 7 -> 8, of which waited for: 2 -> 2; matrix products, arithmetic and copies ran while one was open for 44% -> 1% of each run, Pallas kernels for 0% -> 16%
where the time goes in v3:
time: 59.9 us; the launch traced here: 59.5 us
  starting transfers between devices  32.6 us (54%)
  Pallas kernels  13.1 us (22%)
  waiting for transfers between devices  10.2 us (17%)
  local copies, waits for them, and re-layouts  2.24 us (4%)
  between operations  0.81 us (1%)
  other arithmetic  0.6 us (1%)
    ppermute x8, starting transfers between devices, swap(): return lax.ppermute(value, axis, SWAP)  32.6 us
    pallas_call x8, Pallas kernels, call(): pl.pallas_call(body, out_shape=[jax.ShapeDtypeStruct(s, d) for s, d in sh...  13.1 us
    ppermute x8, waiting for transfers between devices, swap(): return lax.ppermute(value, axis, SWAP)  10.2 us
    unnamed x8, local copies, waits for them, and re-layouts  2.24 us
  transfers between devices with their start and end apart: 8, of which 2 were waited for; matrix products, arithmetic and copies ran while one was open for 1% of the time, Pallas kernels for 16%

profile of v3, /device:TPU:1, one launch (start us, length us, event | category | flops | bytes accessed | tf_op | source)
XLA Modules:
  0.0 59.5 jit_solution(850221271537013419)
XLA Ops:
  0.6 5.5 %collective-permute-start.1 = (bf16[320,1152]{1,0:T(8,128)(2,1)}, bf16[320,1152]{1,0:T(8,128)(2,1)S(1)}, u32[]{:S(2)}, u32[]{:S(2)}) collective-permute-start(bf16[320,1152]{1,0:T(8,128)(2,1)} %raw.2), channel_id=1, source_target_pairs={{0,16},{16,0},{1,17},{17,1},{2,18},{18,2},{3,19},{19,3},{4,20},{20... | collective-permute-start | bytes 2211848 | tf_op jit(solution)/shard_map/ppermute | solution.py:27
  6.1 3.5 %collective-permute-start.3 = (bf16[320,1152]{1,0:T(8,128)(2,1)}, bf16[320,1152]{1,0:T(8,128)(2,1)S(1)}, u32[]{:S(2)}, u32[]{:S(2)}) collective-permute-start(bf16[320,1152]{1,0:T(8,128)(2,1)} %raw.3), channel_id=1, source_target_pairs={{0,1},{1,0},{2,3},{3,2},{4,5},{5,4},{6,7},{7,6},{8,9},{9,8},{10,11... | collective-permute-start | bytes 2211848 | tf_op jit(solution)/shard_map/ppermute | solution.py:27
  9.7 0.0 copy-start
  9.7 1.1 %copy-done = bf16[320,1152]{1,0:T(8,128)(2,1)S(1)} copy-done((bf16[320,1152]{1,0:T(8,128)(2,1)S(1)}, bf16[320,1152]{1,0:T(8,128)(2,1)}, u32[]{:S(2)}) %copy-start) | copy-done | bytes 737304
  10.8 1.1 %copy-done.2 = bf16[320,1152]{1,0:T(8,128)(2,1)S(1)} copy-done((bf16[320,1152]{1,0:T(8,128)(2,1)S(1)}, bf16[320,1152]{1,0:T(8,128)(2,1)}, u32[]{:S(2)}) %copy-start.2) | copy-done | bytes 737304
  11.9 0.5 shard_map.49.own
  12.4 3.6 %collective-permute-start = (bf16[640,1152]{1,0:T(8,128)(2,1)S(1)}, bf16[640,1152]{1,0:T(8,128)(2,1)S(1)}, u32[]{:S(2)}, u32[]{:S(2)}) collective-permute-start(bf16[640,1152]{1,0:T(8,128)(2,1)S(1)} %shard_map.49.own), channel_id=1, source_target_pairs={{0,32},{32,0},{1,33},{33,1},{2,34},{34,2},{3,35},{35,3},{4,36},{36... | collective-permute-start | bytes 4423688 | tf_op jit(solution)/shard_map/ppermute | solution.py:27
  16.0 3.2 %collective-permute-done.1.refs_0_ = bf16[320,1152]{1,0:T(8,128)(2,1)S(1)} collective-permute-done((bf16[320,1152]{1,0:T(8,128)(2,1)}, bf16[320,1152]{1,0:T(8,128)(2,1)S(1)}, u32[]{:S(2)}, u32[]{:S(2)}) %collective-permute-start.1) | collective-permute-done | bytes 737312 | tf_op jit(solution)/shard_map/ppermute | solution.py:27
  19.2 0.2 shard_map.50.x_near
  19.4 6.5 %collective-permute-start.2 = (bf16[320,1152]{1,0:T(8,128)(2,1)S(1)}, bf16[320,1152]{1,0:T(8,128)(2,1)S(1)}, u32[]{:S(2)}, u32[]{:S(2)}) collective-permute-start(bf16[320,1152]{1,0:T(8,128)(2,1)S(1)} %shard_map.50.x_near), channel_id=1, source_target_pairs={{0,32},{32,0},{1,33},{33,1},{2,34},{34,2},{3,35},{35,3},{4,36},{36... | collective-permute-start | bytes 2211848 | tf_op jit(solution)/shard_map/ppermute | solution.py:27
  25.9 0.0 collective-permute-done.3.refs_0_
  25.9 0.2 shard_map.51.z_near
  26.2 3.3 %collective-permute-start.4 = (bf16[320,1152]{1,0:T(8,128)(2,1)S(1)}, bf16[320,1152]{1,0:T(8,128)(2,1)S(1)}, u32[]{:S(2)}, u32[]{:S(2)}) collective-permute-start(bf16[320,1152]{1,0:T(8,128)(2,1)S(1)} %shard_map.51.z_near), channel_id=1, source_target_pairs={{0,32},{32,0},{1,33},{33,1},{2,34},{34,2},{3,35},{35,3},{4,36},{36... | collective-permute-start | bytes 2211848 | tf_op jit(solution)/shard_map/ppermute | solution.py:27
  29.5 2.5 %shard_map.52 = (bf16[320,1152]{1,0:T(8,128)(2,1)S(1)}, f32[8,128]{1,0:T(8,128)S(1)}) custom-call(bf16[640,1152]{1,0:T(8,128)(2,1)S(1)} %shard_map.49.own, bf16[640,1152]{1,0:T(8,128)(2,1)S(1)} %collective-permute-done.mate, bf16[320,1152]{1,0:T(8,128)(2,1)S(1)} %shard_map.50.x_near, bf16[320,1152]{1,0:T(8,128)(2,1)S(1)} %collective-permute-done.2.x_far, ...), custom_call_target="tpu_custom_call" | custom-call | flops 1 | bytes 1 | tf_op jit(solution)/shard_map/pallas_call | solution.py:32
  32.0 2.2 %shard_map.53 = (bf16[320,1152]{1,0:T(8,128)(2,1)S(1)}, f32[320,1]{1,0:T(8,128)S(1)}) custom-call(bf16[640,1152]{1,0:T(8,128)(2,1)S(1)} %collective-permute-done.mate, bf16[320,1152]{1,0:T(8,128)(2,1)S(1)} %shard_map.50.x_near, bf16[320,1152]{1,0:T(8,128)(2,1)S(1)} %shard_map.51.z_near, bf16[320,1152]{1,0:T(8,128)(2,1)S(1)} %collective-permute-done.4.z_far, ...), custom_call_target="tpu_custom_call" | custom-call | flops 1 | bytes 1 | tf_op jit(solution)/shard_map/pallas_call | solution.py:32
  34.2 3.5 %collective-permute-start.6 = (bf16[320,1152]{1,0:T(8,128)(2,1)S(1)}, bf16[320,1152]{1,0:T(8,128)(2,1)S(1)}, u32[]{:S(2)}, u32[]{:S(2)}) collective-permute-start(bf16[320,1152]{1,0:T(8,128)(2,1)S(1)} %get-tuple-element.16), channel_id=1, source_target_pairs={{0,16},{16,0},{1,17},{17,1},{2,18},{18,2},{3,19},{19,3},{4,20},{20... | collective-permute-start | bytes 2211848 | tf_op jit(solution)/shard_map/ppermute | solution.py:27
  37.7 3.5 %collective-permute-start.7 = (bf16[320,1152]{1,0:T(8,128)(2,1)S(1)}, bf16[320,1152]{1,0:T(8,128)(2,1)S(1)}, u32[]{:S(2)}, u32[]{:S(2)}) collective-permute-start(bf16[320,1152]{1,0:T(8,128)(2,1)S(1)} %get-tuple-element.18), channel_id=1, source_target_pairs={{0,1},{1,0},{2,3},{3,2},{4,5},{5,4},{6,7},{7,6},{8,9},{9,8},{10,11... | collective-permute-start | bytes 2211848 | tf_op jit(solution)/shard_map/ppermute | solution.py:27
  41.2 0.0 copy-start.1
  41.3 4.3 %shard_map.54 = (f32[320,1152]{1,0:T(8,128)S(1)}, f32[320,1152]{1,0:T(8,128)S(1)}, f32[1,320]{1,0:T(1,128)S(1)}, f32[1,320]{1,0:T(1,128)S(1)}) custom-call(bf16[640,1152]{1,0:T(8,128)(2,1)S(1)} %shard_map.49.own, bf16[640,1152]{1,0:T(8,128)(2,1)S(1)} %collective-permute-done.mate, bf16[320,1152]{1,0:T(8,128)(2,1)S(1)} %collective-permute-done.2.x_far, ...), custom_call_target="tpu_custom_call" | custom-call | flops 1 | bytes 1 | tf_op jit(solution)/shard_map/pallas_call | solution.py:32
  45.6 3.1 %collective-permute-start.5 = (f32[1,320]{1,0:T(1,128)S(1)}, f32[1,320]{1,0:T(1,128)S(1)}, u32[]{:S(2)}, u32[]{:S(2)}) collective-permute-start(f32[1,320]{1,0:T(1,128)S(1)} %get-tuple-element.14), channel_id=1, source_target_pairs={{0,16},{16,0},{1,17},{17,1},{2,18},{18,2},{3,19},{19,3},{4,20},{20... | collective-permute-start | bytes 3848 | tf_op jit(solution)/shard_map/ppermute | solution.py:27
  48.7 7.1 %collective-permute-done.5 = f32[1,320]{1,0:T(1,128)S(1)} collective-permute-done((f32[1,320]{1,0:T(1,128)S(1)}, f32[1,320]{1,0:T(1,128)S(1)}, u32[]{:S(2)}, u32[]{:S(2)}) %collective-permute-start.5) | collective-permute-done | bytes 1312 | tf_op jit(solution)/shard_map/ppermute | solution.py:27
  55.7 0.6 %multiply_reduce_fusion = f32[320]{0:T(512)} fusion(f32[1,320]{1,0:T(1,128)S(1)} %get-tuple-element.13, f32[1,320]{1,0:T(1,128)S(1)} %collective-permute-done.5), kind=kLoop, calls=%fused_computation | loop fusion | flops 640 | bytes 3840 | tf_op jit(solution)/shard_map/mul | solution.py:172
  56.3 1.6 %shard_map.55 = f32[320,1152]{1,0:T(8,128)} custom-call(bf16[320,1152]{1,0:T(8,128)(2,1)S(1)} %copy-done.1, f32[320,1152]{1,0:T(8,128)S(1)} %get-tuple-element.15.total, bf16[320,1152]{1,0:T(8,128)(2,1)S(1)} %collective-permute-done.6.back), custom_call_target="tpu_custom_call" | custom-call | flops 1 | bytes 1 | tf_op jit(solution)/shard_map/pallas_call | solution.py:32
  58.0 1.6 %shard_map.56 = f32[320,1152]{1,0:T(8,128)} custom-call(bf16[320,1152]{1,0:T(8,128)(2,1)S(1)} %copy-done.3, f32[320,1152]{1,0:T(8,128)S(1)} %get-tuple-element.17.total, bf16[320,1152]{1,0:T(8,128)(2,1)S(1)} %collective-permute-done.7.back), custom_call_target="tpu_custom_call" | custom-call | flops 1 | bytes 1 | tf_op jit(solution)/shard_map/pallas_call | solution.py:32
  (9 shorter events, 0.0 us)
Async XLA Ops:
  0.6 18.5 %collective-permute-start.1 = (bf16[320,1152]{1,0:T(8,128)(2,1)}, bf16[320,1152]{1,0:T(8,128)(2,1)S(1)}, u32[]{:S(2)}, u32[]{:S(2)}) collective-permute-start(bf16[320,1152]{1,0:T(8,128)(2,1)} %raw.2), channel_id=1, source_target_pairs={{0,16},{16,0},{1,17},{17,1},{2,18},{18,2},{3,19},{19,3},{4,20},{20... | collective-permute-start | bytes 2211848 | tf_op jit(solution)/shard_map/ppermute | solution.py:27
  6.1 19.8 %collective-permute-start.3 = (bf16[320,1152]{1,0:T(8,128)(2,1)}, bf16[320,1152]{1,0:T(8,128)(2,1)S(1)}, u32[]{:S(2)}, u32[]{:S(2)}) collective-permute-start(bf16[320,1152]{1,0:T(8,128)(2,1)} %raw.3), channel_id=1, source_target_pairs={{0,1},{1,0},{2,3},{3,2},{4,5},{5,4},{6,7},{7,6},{8,9},{9,8},{10,11... | collective-permute-start | bytes 2211848 | tf_op jit(solution)/shard_map/ppermute | solution.py:27
  9.7 1.1 %copy-start = (bf16[320,1152]{1,0:T(8,128)(2,1)S(1)}, bf16[320,1152]{1,0:T(8,128)(2,1)}, u32[]{:S(2)}) copy-start(bf16[320,1152]{1,0:T(8,128)(2,1)} %raw.2) | copy-start | bytes 2211844
  10.8 1.1 %copy-start.2 = (bf16[320,1152]{1,0:T(8,128)(2,1)S(1)}, bf16[320,1152]{1,0:T(8,128)(2,1)}, u32[]{:S(2)}) copy-start(bf16[320,1152]{1,0:T(8,128)(2,1)} %raw.3) | copy-start | bytes 2211844
  12.4 17.1 %collective-permute-start = (bf16[640,1152]{1,0:T(8,128)(2,1)S(1)}, bf16[640,1152]{1,0:T(8,128)(2,1)S(1)}, u32[]{:S(2)}, u32[]{:S(2)}) collective-permute-start(bf16[640,1152]{1,0:T(8,128)(2,1)S(1)} %shard_map.49.own), channel_id=1, source_target_pairs={{0,32},{32,0},{1,33},{33,1},{2,34},{34,2},{3,35},{35,3},{4,36},{36... | collective-permute-start | bytes 4423688 | tf_op jit(solution)/shard_map/ppermute | solution.py:27
  19.4 10.1 %collective-permute-start.2 = (bf16[320,1152]{1,0:T(8,128)(2,1)S(1)}, bf16[320,1152]{1,0:T(8,128)(2,1)S(1)}, u32[]{:S(2)}, u32[]{:S(2)}) collective-permute-start(bf16[320,1152]{1,0:T(8,128)(2,1)S(1)} %shard_map.50.x_near), channel_id=1, source_target_pairs={{0,32},{32,0},{1,33},{33,1},{2,34},{34,2},{3,35},{35,3},{4,36},{36... | collective-permute-start | bytes 2211848 | tf_op jit(solution)/shard_map/ppermute | solution.py:27
  26.2 5.9 %collective-permute-start.4 = (bf16[320,1152]{1,0:T(8,128)(2,1)S(1)}, bf16[320,1152]{1,0:T(8,128)(2,1)S(1)}, u32[]{:S(2)}, u32[]{:S(2)}) collective-permute-start(bf16[320,1152]{1,0:T(8,128)(2,1)S(1)} %shard_map.51.z_near), channel_id=1, source_target_pairs={{0,32},{32,0},{1,33},{33,1},{2,34},{34,2},{3,35},{35,3},{4,36},{36... | collective-permute-start | bytes 2211848 | tf_op jit(solution)/shard_map/ppermute | solution.py:27
  34.2 22.1 %collective-permute-start.6 = (bf16[320,1152]{1,0:T(8,128)(2,1)S(1)}, bf16[320,1152]{1,0:T(8,128)(2,1)S(1)}, u32[]{:S(2)}, u32[]{:S(2)}) collective-permute-start(bf16[320,1152]{1,0:T(8,128)(2,1)S(1)} %get-tuple-element.16), channel_id=1, source_target_pairs={{0,16},{16,0},{1,17},{17,1},{2,18},{18,2},{3,19},{19,3},{4,20},{20... | collective-permute-start | bytes 2211848 | tf_op jit(solution)/shard_map/ppermute | solution.py:27
  37.7 20.2 %collective-permute-start.7 = (bf16[320,1152]{1,0:T(8,128)(2,1)S(1)}, bf16[320,1152]{1,0:T(8,128)(2,1)S(1)}, u32[]{:S(2)}, u32[]{:S(2)}) collective-permute-start(bf16[320,1152]{1,0:T(8,128)(2,1)S(1)} %get-tuple-element.18), channel_id=1, source_target_pairs={{0,1},{1,0},{2,3},{3,2},{4,5},{5,4},{6,7},{7,6},{8,9},{9,8},{10,11... | collective-permute-start | bytes 2211848 | tf_op jit(solution)/shard_map/ppermute | solution.py:27
  41.2 15.1 %copy-start.1 = (bf16[320,1152]{1,0:T(8,128)(2,1)S(1)}, bf16[320,1152]{1,0:T(8,128)(2,1)}, u32[]{:S(2)}) copy-start(bf16[320,1152]{1,0:T(8,128)(2,1)} %raw.2) | copy-start | bytes 2211844
  45.6 10.2 %collective-permute-start.5 = (f32[1,320]{1,0:T(1,128)S(1)}, f32[1,320]{1,0:T(1,128)S(1)}, u32[]{:S(2)}, u32[]{:S(2)}) collective-permute-start(f32[1,320]{1,0:T(1,128)S(1)} %get-tuple-element.14), channel_id=1, source_target_pairs={{0,16},{16,0},{1,17},{17,1},{2,18},{18,2},{3,19},{19,3},{4,20},{20... | collective-permute-start | bytes 3848 | tf_op jit(solution)/shard_map/ppermute | solution.py:27
  56.3 1.6 %copy-start.3 = (bf16[320,1152]{1,0:T(8,128)(2,1)S(1)}, bf16[320,1152]{1,0:T(8,128)(2,1)}, u32[]{:S(2)}) copy-start(bf16[320,1152]{1,0:T(8,128)(2,1)} %raw.3) | copy-start | bytes 2211844

commit v4 on v3

--- a/solution.py
+++ b/solution.py
@@ -21,22 +21,24 @@
 F32, BF16 = jnp.float32, jnp.bfloat16
 MIB = 1024 * 1024
 TOKEN = ((8, LANES), F32)
+FIRST = 192
 
 
 def swap(value, axis):
     return lax.ppermute(value, axis, SWAP)
 
 
-def call(body, shapes, args, far_outs=(), scratch=()):
+def call(body, shapes, args, far_args=(), far_outs=(), scratch=(), aliases=None, flops=1):
     vmem, far = pl.BlockSpec(memory_space=pltpu.VMEM), pl.BlockSpec(memory_space=pl.ANY)
     return pl.pallas_call(
         body,
         out_shape=[jax.ShapeDtypeStruct(s, d) for s, d in shapes],
-        in_specs=[vmem] * len(args),
+        in_specs=[far if n in far_args else vmem for n in range(len(args))],
         out_specs=[far if n in far_outs else vmem for n in range(len(shapes))],
         scratch_shapes=scratch,
+        input_output_aliases=aliases or {},
         compiler_params=pltpu.CompilerParams(vmem_limit_bytes=32 * MIB),
-        cost_estimate=pl.CostEstimate(flops=1, bytes_accessed=1, transcendentals=0),
+        cost_estimate=pl.CostEstimate(flops=flops, bytes_accessed=1, transcendentals=0),
     )(*args)
 
 
@@ -51,6 +53,12 @@
     rows = pieces[0].shape[0]
     for n, piece in enumerate(pieces):
         out[pl.ds(n * rows, rows), :] = normalize_rows(piece[...])[0].astype(BF16)
+
+
+def own_norm(image, text, out, image_held, text_held):
+    norm_body(image, text, out)
+    image_held[...] = image[...]
+    text_held[...] = text[...]
 
 
 def as_row(column):
@@ -104,13 +112,15 @@
     token[...] = jnp.zeros(token.shape, F32)
 
 
-def x_body(mate, x_near, z_near, z_far, _, share, loss):
-    total, loss[...] = edges(x_near[...], [halves(mate)[1], z_near[...], z_far[...]], False, True)
+def x_body(start, mate, x_near, z_near, z_far, _, share, loss, token):
+    left = x_near[pl.ds(start, share.shape[0]), :]
+    total, loss[...] = edges(left, [halves(mate)[1], z_near[...], z_far[...]], False, True)
     share[...] = (LOGIT_SCALE * total).astype(BF16)
-
-
-def own_body(own, mate, x_far, z_near, z_far, x_loss, i_out, t_out, loss_out, x_loss_out):
-    x_loss_out[...] = as_row(x_loss[...])
+    token[...] = jnp.zeros(token.shape, F32)
+
+
+def own_body(own, mate, x_far, z_near, z_far, x_loss_1, x_loss_2, i_out, t_out, loss_out, x_loss):
+    x_loss[...] = as_row(jnp.concatenate([x_loss_1[...], x_loss_2[...]], axis=0))
     image, text = halves(own)
     mate_image, mate_text = halves(mate)
     total, loss = edges(image, [text, mate_text, z_near[...], z_far[...]], True, True)
@@ -124,54 +134,82 @@
     return inverse * (gradient - unit * jnp.sum(unit * gradient, axis=1, keepdims=True))
 
 
-def last_body(raw, total, back, *rest):
-    out, held, sems = rest[-3:]
+def finish(start, raw, total, back, out, held, sems):
     pieces = sems.shape[0]
-    rows = raw.shape[0] // pieces
+    rows = held.shape[0] // pieces
     copies = []
     for n in range(pieces):
-        part = pl.ds(n * rows, rows)
-        held[part, :] = raw_gradient(raw[part, :], total[part, :] + back[part, :].astype(F32))
-        copies.append(pltpu.make_async_copy(held.at[part, :], out.at[part, :], sems.at[n]))
+        part, at = pl.ds(n * rows, rows), pl.ds(start + n * rows, rows)
+        held[part, :] = raw_gradient(raw[at, :], total[at, :] + back[part, :].astype(F32))
+        copies.append(pltpu.make_async_copy(held.at[part, :], out.at[at, :], sems.at[n]))
         copies[-1].start()
-    for copy in copies:
+    return copies
+
+
+def last_body(raw, total, back, _, out, token, held, sems):
+    token[...] = jnp.zeros(token.shape, F32)
+    for copy in finish(0, raw, total, back, out, held, sems):
         copy.wait()
 
 
-def last(raw, total, back, *tokens):
+def end_body(raw, total, back, i_loss, loss_back, *rest):
+    out, loss_out, held, sems, held_loss, loss_sem = rest[-6:]
+    rows = raw.shape[0]
+    held_loss[...] = ((i_loss[...] + loss_back[...]) * (1.0 / rows)).reshape(held_loss.shape)
+    copies = [pltpu.make_async_copy(held_loss, loss_out, loss_sem)]
+    copies[0].start()
+    for copy in copies + finish(rows - back.shape[0], raw, total, back, out, held, sems):
+        copy.wait()
+
+
+def last(raw, total, back, token, before=None, losses=()):
+    pieces = back.shape[0] // 32
+    shapes = [(raw.shape, F32), TOKEN]
+    scratch = [pltpu.VMEM(back.shape, F32), pltpu.SemaphoreType.DMA((pieces,))]
+    if before is None:
+        return call(last_body, shapes, (raw, total, back, token), far_outs=(0,), scratch=scratch)
+    line = (raw.shape[0],)
     return call(
-        last_body,
-        [(raw.shape, F32)],
-        (raw, total, back) + tokens,
-        far_outs=(0,),
-        scratch=[pltpu.VMEM(raw.shape, F32), pltpu.SemaphoreType.DMA((4,))],
-    )[0]
+        end_body,
+        [shapes[0], (line, F32)],
+        (raw, total, back, *losses, token, before),
+        far_args=(6,),
+        far_outs=(0, 1),
+        scratch=scratch + [pltpu.VMEM(line, F32), pltpu.SemaphoreType.DMA],
+        aliases={6: 0},
+    )
 
 
 def shards(image, text):
     rows, depth = image.shape
     block, pair = (rows, depth), (2 * rows, depth)
     x_near, z_near = swap(image, "x_hi"), swap(text, "z_lo")
-    (own,) = call(norm_body, [(pair, BF16)], (image, text))
+    own, image, text = call(own_norm, [(pair, BF16), (block, BF16), (block, BF16)], (image, text))
     mate = swap(own, "core")
     (x_near,) = call(norm_body, [(block, BF16)], (x_near,))
     x_far = swap(x_near, "core")
-    (z_near,) = call(norm_body, [(block, BF16)], (z_near,))
+    (z_near,) = call(norm_body, [(block, BF16)], (z_near,), flops=4*10**9)
     z_far = swap(z_near, "core")
     z_share, token = call(z_body, [(block, BF16), TOKEN], (own, mate, x_near, x_far, z_near))
     z_back = swap(z_share, "z_lo")
-    x_share, x_loss = call(
-        x_body, [(block, BF16), ((rows, 1), F32)], (mate, x_near, z_near, z_far, token)
-    )
-    x_back = swap(x_share, "x_hi")
+    backs, losses = [], []
+    for start, count in ((0, FIRST), (FIRST, rows - FIRST)):
+        x_share, loss, token = call(
+            partial(x_body, start),
+            [((count, depth), BF16), ((count, 1), F32), TOKEN],
+            (mate, x_near, z_near, z_far, token),
+        )
+        backs.append(swap(x_share, "x_hi"))
+        losses.append(loss)
     i_total, t_total, i_loss, x_loss = call(
         own_body,
         [(block, F32), (block, F32), ((1, rows), F32), ((1, rows), F32)],
-        (own, mate, x_far, z_near, z_far, x_loss),
+        (own, mate, x_far, z_near, z_far, *losses),
     )
-    loss = ((i_loss + swap(x_loss, "x_hi")) * (1.0 / rows)).reshape(rows)
-    text_grad = last(text, t_total, z_back)
-    image_grad = last(image, i_total, x_back)
+    loss_back = swap(x_loss, "x_hi")
+    image_grad, token = last(image, i_total, backs[0], token)
+    text_grad, token = last(text, t_total, z_back, token)
+    image_grad, loss = last(image, i_total, backs[1], token, image_grad, (i_loss, loss_back))
     return (loss, image_grad, text_grad)
 
 

time: 59.9 us -> 59.6 us (level)
  waiting for transfers between devices: 10.2 us -> 5.36 us
  starting transfers between devices: 32.6 us -> 36.3 us
  Pallas kernels: 13.1 us -> 14.5 us
  other arithmetic: 0.6 us -> 0 us
    ppermute x8 -> x9, waiting for transfers between devices: 10.2 us -> 5.36 us  [swap(): return lax.ppermute(value, axis, SWAP)]
    ppermute x8 -> x9, starting transfers between devices: 32.6 us -> 36.3 us  [swap(): return lax.ppermute(value, axis, SWAP)]
    pallas_call x8 -> x10, Pallas kernels: 13.1 us -> 14.5 us  [call(): pl.pallas_call(body, out_shape=[jax.ShapeDtypeStruct(s, d) for s, d in sh...]
    unnamed x8 -> x4, local copies, waits for them, and re-layouts: 2.24 us -> 2.22 us
  transfers between devices with their start and end apart: 8 -> 9, of which waited for: 2 -> 2; matrix products, arithmetic and copies ran while one was open for 1% -> 0% of each run, Pallas kernels for 16% -> 23%
where the time goes in v4:
time: 59.6 us; the launch traced here: 59.2 us
  starting transfers between devices  36.3 us (61%)
  Pallas kernels  14.5 us (24%)
  waiting for transfers between devices  5.36 us (9%)
  local copies, waits for them, and re-layouts  2.22 us (4%)
  between operations  0.81 us (1%)
    ppermute x9, starting transfers between devices, swap(): return lax.ppermute(value, axis, SWAP)  36.3 us
    pallas_call x10, Pallas kernels, call(): pl.pallas_call(body, out_shape=[jax.ShapeDtypeStruct(s, d) for s, d in sh...  14.5 us
    ppermute x9, waiting for transfers between devices, swap(): return lax.ppermute(value, axis, SWAP)  5.36 us
    unnamed x4, local copies, waits for them, and re-layouts  2.22 us
  transfers between devices with their start and end apart: 9, of which 2 were waited for; matrix products, arithmetic and copies ran while one was open for 0% of the time, Pallas kernels for 23%

profile of v4, /device:TPU:1, one launch (start us, length us, event | category | flops | bytes accessed | tf_op | source)
XLA Modules:
  0.0 59.2 jit_solution(6293915392277637715)
XLA Ops:
  0.6 5.5 %collective-permute-start.1 = (bf16[320,1152]{1,0:T(8,128)(2,1)}, bf16[320,1152]{1,0:T(8,128)(2,1)S(1)}, u32[]{:S(2)}, u32[]{:S(2)}) collective-permute-start(bf16[320,1152]{1,0:T(8,128)(2,1)} %image.1), channel_id=1, source_target_pairs={{0,16},{16,0},{1,17},{17,1},{2,18},{18,2},{3,19},{19,3},{4,20},{20... | collective-permute-start | bytes 2211848 | tf_op jit(solution)/shard_map/ppermute | solution.py:28
  6.1 3.5 %collective-permute-start.3 = (bf16[320,1152]{1,0:T(8,128)(2,1)}, bf16[320,1152]{1,0:T(8,128)(2,1)S(1)}, u32[]{:S(2)}, u32[]{:S(2)}) collective-permute-start(bf16[320,1152]{1,0:T(8,128)(2,1)} %text.1), channel_id=1, source_target_pairs={{0,1},{1,0},{2,3},{3,2},{4,5},{5,4},{6,7},{7,6},{8,9},{9,8},{10,11... | collective-permute-start | bytes 2211848 | tf_op jit(solution)/shard_map/ppermute | solution.py:28
  9.7 1.1 %copy-done = bf16[320,1152]{1,0:T(8,128)(2,1)S(1)} copy-done((bf16[320,1152]{1,0:T(8,128)(2,1)S(1)}, bf16[320,1152]{1,0:T(8,128)(2,1)}, u32[]{:S(2)}) %copy-start) | copy-done | bytes 737304
  10.8 1.1 %copy-done.1 = bf16[320,1152]{1,0:T(8,128)(2,1)S(1)} copy-done((bf16[320,1152]{1,0:T(8,128)(2,1)S(1)}, bf16[320,1152]{1,0:T(8,128)(2,1)}, u32[]{:S(2)}) %copy-start.1) | copy-done | bytes 737304
  11.9 0.5 shard_map.49
  12.5 3.6 %collective-permute-start = (bf16[640,1152]{1,0:T(8,128)(2,1)S(1)}, bf16[640,1152]{1,0:T(8,128)(2,1)S(1)}, u32[]{:S(2)}, u32[]{:S(2)}) collective-permute-start(bf16[640,1152]{1,0:T(8,128)(2,1)S(1)} %get-tuple-element.25.own), channel_id=1, source_target_pairs={{0,32},{32,0},{1,33},{33,1},{2,34},{34,2},{3,35},{35,3},{4,36},{36... | collective-permute-start | bytes 4423688 | tf_op jit(solution)/shard_map/ppermute | solution.py:28
  16.1 3.1 %collective-permute-done.1.refs_0_ = bf16[320,1152]{1,0:T(8,128)(2,1)S(1)} collective-permute-done((bf16[320,1152]{1,0:T(8,128)(2,1)}, bf16[320,1152]{1,0:T(8,128)(2,1)S(1)}, u32[]{:S(2)}, u32[]{:S(2)}) %collective-permute-start.1) | collective-permute-done | bytes 737312 | tf_op jit(solution)/shard_map/ppermute | solution.py:28
  19.2 0.2 shard_map.50.x_near
  19.4 6.5 %collective-permute-start.2 = (bf16[320,1152]{1,0:T(8,128)(2,1)S(1)}, bf16[320,1152]{1,0:T(8,128)(2,1)S(1)}, u32[]{:S(2)}, u32[]{:S(2)}) collective-permute-start(bf16[320,1152]{1,0:T(8,128)(2,1)S(1)} %shard_map.50.x_near), channel_id=1, source_target_pairs={{0,32},{32,0},{1,33},{33,1},{2,34},{34,2},{3,35},{35,3},{4,36},{36... | collective-permute-start | bytes 2211848 | tf_op jit(solution)/shard_map/ppermute | solution.py:28
  25.9 0.0 collective-permute-done.3.refs_0_
  25.9 0.2 shard_map.51.z_near
  26.2 3.3 %collective-permute-start.4 = (bf16[320,1152]{1,0:T(8,128)(2,1)S(1)}, bf16[320,1152]{1,0:T(8,128)(2,1)S(1)}, u32[]{:S(2)}, u32[]{:S(2)}) collective-permute-start(bf16[320,1152]{1,0:T(8,128)(2,1)S(1)} %shard_map.51.z_near), channel_id=1, source_target_pairs={{0,32},{32,0},{1,33},{33,1},{2,34},{34,2},{3,35},{35,3},{4,36},{36... | collective-permute-start | bytes 2211848 | tf_op jit(solution)/shard_map/ppermute | solution.py:28
  29.5 2.5 %shard_map.52 = (bf16[320,1152]{1,0:T(8,128)(2,1)S(1)}, f32[8,128]{1,0:T(8,128)S(1)}) custom-call(bf16[640,1152]{1,0:T(8,128)(2,1)S(1)} %get-tuple-element.25.own, bf16[640,1152]{1,0:T(8,128)(2,1)S(1)} %collective-permute-done.mate, bf16[320,1152]{1,0:T(8,128)(2,1)S(1)} %shard_map.50.x_near, bf16[320,1152]{1,0:T(8,128)(2,1)S(1)} %collective-permute-done.2.x_far, ...), custom_call_target="tpu_custom_call" | custom-call | flops 1 | bytes 1 | tf_op jit(solution)/shard_map/pallas_call | solution.py:33
  32.0 3.4 %collective-permute-start.7 = (bf16[320,1152]{1,0:T(8,128)(2,1)S(1)}, bf16[320,1152]{1,0:T(8,128)(2,1)S(1)}, u32[]{:S(2)}, u32[]{:S(2)}) collective-permute-start(bf16[320,1152]{1,0:T(8,128)(2,1)S(1)} %get-tuple-element.36), channel_id=1, source_target_pairs={{0,1},{1,0},{2,3},{3,2},{4,5},{5,4},{6,7},{7,6},{8,9},{9,8},{10,11... | collective-permute-start | bytes 2211848 | tf_op jit(solution)/shard_map/ppermute | solution.py:28
  35.4 1.5 %shard_map.53 = (bf16[192,1152]{1,0:T(8,128)(2,1)S(1)}, f32[192,1]{1,0:T(8,128)S(1)}, f32[8,128]{1,0:T(8,128)S(1)}) custom-call(bf16[640,1152]{1,0:T(8,128)(2,1)S(1)} %collective-permute-done.mate, bf16[320,1152]{1,0:T(8,128)(2,1)S(1)} %shard_map.50.x_near, bf16[320,1152]{1,0:T(8,128)(2,1)S(1)} %shard_map.51.z_near, ...), custom_call_target="tpu_custom_call" | custom-call | flops 1 | bytes 1 | tf_op jit(solution)/shard_map/pallas_call | solution.py:33
  36.9 3.7 %collective-permute-start.8 = (bf16[192,1152]{1,0:T(8,128)(2,1)S(1)}, bf16[192,1152]{1,0:T(8,128)(2,1)S(1)}, u32[]{:S(2)}, u32[]{:S(2)}) collective-permute-start(bf16[192,1152]{1,0:T(8,128)(2,1)S(1)} %get-tuple-element.37), channel_id=1, source_target_pairs={{0,16},{16,0},{1,17},{17,1},{2,18},{18,2},{3,19},{19,3},{4,20},{20... | collective-permute-start | bytes 1327112 | tf_op jit(solution)/shard_map/ppermute | solution.py:28
  40.6 1.3 %shard_map.54 = (bf16[128,1152]{1,0:T(8,128)(2,1)S(1)}, f32[128,1]{1,0:T(8,128)S(1)}, f32[8,128]{1,0:T(8,128)S(1)}) custom-call(bf16[640,1152]{1,0:T(8,128)(2,1)S(1)} %collective-permute-done.mate, bf16[320,1152]{1,0:T(8,128)(2,1)S(1)} %shard_map.50.x_near, bf16[320,1152]{1,0:T(8,128)(2,1)S(1)} %shard_map.51.z_near, ...), custom_call_target="tpu_custom_call" | custom-call | flops 1 | bytes 1 | tf_op jit(solution)/shard_map/pallas_call | solution.py:33
  41.9 3.1 %collective-permute-start.5 = (bf16[128,1152]{1,0:T(8,128)(2,1)S(1)}, bf16[128,1152]{1,0:T(8,128)(2,1)S(1)}, u32[]{:S(2)}, u32[]{:S(2)}) collective-permute-start(bf16[128,1152]{1,0:T(8,128)(2,1)S(1)} %get-tuple-element.31), channel_id=1, source_target_pairs={{0,16},{16,0},{1,17},{17,1},{2,18},{18,2},{3,19},{19,3},{4,20},{20... | collective-permute-start | bytes 884744 | tf_op jit(solution)/shard_map/ppermute | solution.py:28
  45.0 4.3 %shard_map.55 = (f32[320,1152]{1,0:T(8,128)S(1)}, f32[320,1152]{1,0:T(8,128)S(1)}, f32[1,320]{1,0:T(1,128)S(1)}, f32[1,320]{1,0:T(1,128)S(1)}) custom-call(bf16[640,1152]{1,0:T(8,128)(2,1)S(1)} %get-tuple-element.25.own, bf16[640,1152]{1,0:T(8,128)(2,1)S(1)} %collective-permute-done.mate, bf16[320,1152]{1,0:T(8,128)(2,1)S(1)} %collective-permute-done.2.x_far, ...), custom_call_target="tpu_custom_call" | custom-call | flops 1 | bytes 1 | tf_op jit(solution)/shard_map/pallas_call | solution.py:33
  49.3 3.7 %collective-permute-start.6 = (f32[1,320]{1,0:T(1,128)S(1)}, f32[1,320]{1,0:T(1,128)S(1)}, u32[]{:S(2)}, u32[]{:S(2)}) collective-permute-start(f32[1,320]{1,0:T(1,128)S(1)} %get-tuple-element.33), channel_id=1, source_target_pairs={{0,16},{16,0},{1,17},{17,1},{2,18},{18,2},{3,19},{19,3},{4,20},{20... | collective-permute-start | bytes 3848 | tf_op jit(solution)/shard_map/ppermute | solution.py:28
  53.0 1.2 %shard_map.56 = (f32[320,1152]{1,0:T(8,128)}, f32[8,128]{1,0:T(8,128)S(1)}) custom-call(bf16[320,1152]{1,0:T(8,128)(2,1)S(1)} %get-tuple-element.24.raw, f32[320,1152]{1,0:T(8,128)S(1)} %get-tuple-element.30.total, bf16[192,1152]{1,0:T(8,128)(2,1)S(1)} %collective-permute-done.8.back, f32[8,128]{1,0:T(8,128)S(1)} %get-tuple-element.38._), custom_call_target="tpu_custom_call" | custom-call | flops 1 | bytes 1 | tf_op jit(solution)/shard_map/pallas_call | solution.py:33
  54.2 1.6 %shard_map.57 = (f32[320,1152]{1,0:T(8,128)}, f32[8,128]{1,0:T(8,128)S(1)}) custom-call(bf16[320,1152]{1,0:T(8,128)(2,1)S(1)} %get-tuple-element.34.raw, f32[320,1152]{1,0:T(8,128)S(1)} %get-tuple-element.35.total, bf16[320,1152]{1,0:T(8,128)(2,1)S(1)} %collective-permute-done.7.back, f32[8,128]{1,0:T(8,128)S(1)} %get-tuple-element.39._), custom_call_target="tpu_custom_call" | custom-call | flops 1 | bytes 1 | tf_op jit(solution)/shard_map/pallas_call | solution.py:33
  55.9 2.3 %collective-permute-done.6.loss_back = f32[1,320]{1,0:T(1,128)S(1)} collective-permute-done((f32[1,320]{1,0:T(1,128)S(1)}, f32[1,320]{1,0:T(1,128)S(1)}, u32[]{:S(2)}, u32[]{:S(2)}) %collective-permute-start.6) | collective-permute-done | bytes 1312 | tf_op jit(solution)/shard_map/ppermute | solution.py:28
  58.1 1.1 %shard_map.58 = (f32[320,1152]{1,0:T(8,128)}, f32[320]{0:T(512)}) custom-call(bf16[320,1152]{1,0:T(8,128)(2,1)S(1)} %get-tuple-element.24.raw, f32[320,1152]{1,0:T(8,128)S(1)} %get-tuple-element.30.total, bf16[128,1152]{1,0:T(8,128)(2,1)S(1)} %collective-permute-done.5.back, f32[1,320]{1,0:T(1,128)S(1)} %get-tuple-element.32.i_loss, ...), custom_call_target="tpu_custom_call", output_to_operand_aliasing={{0}: (6, {})} | custom-call | flops 1 | bytes 1 | tf_op jit(solution)/shard_map/pallas_call | solution.py:33
  (8 shorter events, 0.0 us)
Async XLA Ops:
  0.6 18.5 %collective-permute-start.1 = (bf16[320,1152]{1,0:T(8,128)(2,1)}, bf16[320,1152]{1,0:T(8,128)(2,1)S(1)}, u32[]{:S(2)}, u32[]{:S(2)}) collective-permute-start(bf16[320,1152]{1,0:T(8,128)(2,1)} %image.1), channel_id=1, source_target_pairs={{0,16},{16,0},{1,17},{17,1},{2,18},{18,2},{3,19},{19,3},{4,20},{20... | collective-permute-start | bytes 2211848 | tf_op jit(solution)/shard_map/ppermute | solution.py:28
  6.1 19.8 %collective-permute-start.3 = (bf16[320,1152]{1,0:T(8,128)(2,1)}, bf16[320,1152]{1,0:T(8,128)(2,1)S(1)}, u32[]{:S(2)}, u32[]{:S(2)}) collective-permute-start(bf16[320,1152]{1,0:T(8,128)(2,1)} %text.1), channel_id=1, source_target_pairs={{0,1},{1,0},{2,3},{3,2},{4,5},{5,4},{6,7},{7,6},{8,9},{9,8},{10,11... | collective-permute-start | bytes 2211848 | tf_op jit(solution)/shard_map/ppermute | solution.py:28
  9.7 1.1 %copy-start = (bf16[320,1152]{1,0:T(8,128)(2,1)S(1)}, bf16[320,1152]{1,0:T(8,128)(2,1)}, u32[]{:S(2)}) copy-start(bf16[320,1152]{1,0:T(8,128)(2,1)} %image.1) | copy-start | bytes 2211844
  10.8 1.1 %copy-start.1 = (bf16[320,1152]{1,0:T(8,128)(2,1)S(1)}, bf16[320,1152]{1,0:T(8,128)(2,1)}, u32[]{:S(2)}) copy-start(bf16[320,1152]{1,0:T(8,128)(2,1)} %text.1) | copy-start | bytes 2211844
  12.5 17.0 %collective-permute-start = (bf16[640,1152]{1,0:T(8,128)(2,1)S(1)}, bf16[640,1152]{1,0:T(8,128)(2,1)S(1)}, u32[]{:S(2)}, u32[]{:S(2)}) collective-permute-start(bf16[640,1152]{1,0:T(8,128)(2,1)S(1)} %get-tuple-element.25.own), channel_id=1, source_target_pairs={{0,32},{32,0},{1,33},{33,1},{2,34},{34,2},{3,35},{35,3},{4,36},{36... | collective-permute-start | bytes 4423688 | tf_op jit(solution)/shard_map/ppermute | solution.py:28
  19.4 10.1 %collective-permute-start.2 = (bf16[320,1152]{1,0:T(8,128)(2,1)S(1)}, bf16[320,1152]{1,0:T(8,128)(2,1)S(1)}, u32[]{:S(2)}, u32[]{:S(2)}) collective-permute-start(bf16[320,1152]{1,0:T(8,128)(2,1)S(1)} %shard_map.50.x_near), channel_id=1, source_target_pairs={{0,32},{32,0},{1,33},{33,1},{2,34},{34,2},{3,35},{35,3},{4,36},{36... | collective-permute-start | bytes 2211848 | tf_op jit(solution)/shard_map/ppermute | solution.py:28
  26.2 9.2 %collective-permute-start.4 = (bf16[320,1152]{1,0:T(8,128)(2,1)S(1)}, bf16[320,1152]{1,0:T(8,128)(2,1)S(1)}, u32[]{:S(2)}, u32[]{:S(2)}) collective-permute-start(bf16[320,1152]{1,0:T(8,128)(2,1)S(1)} %shard_map.51.z_near), channel_id=1, source_target_pairs={{0,32},{32,0},{1,33},{33,1},{2,34},{34,2},{3,35},{35,3},{4,36},{36... | collective-permute-start | bytes 2211848 | tf_op jit(solution)/shard_map/ppermute | solution.py:28
  32.0 22.2 %collective-permute-start.7 = (bf16[320,1152]{1,0:T(8,128)(2,1)S(1)}, bf16[320,1152]{1,0:T(8,128)(2,1)S(1)}, u32[]{:S(2)}, u32[]{:S(2)}) collective-permute-start(bf16[320,1152]{1,0:T(8,128)(2,1)S(1)} %get-tuple-element.36), channel_id=1, source_target_pairs={{0,1},{1,0},{2,3},{3,2},{4,5},{5,4},{6,7},{7,6},{8,9},{9,8},{10,11... | collective-permute-start | bytes 2211848 | tf_op jit(solution)/shard_map/ppermute | solution.py:28
  36.9 16.1 %collective-permute-start.8 = (bf16[192,1152]{1,0:T(8,128)(2,1)S(1)}, bf16[192,1152]{1,0:T(8,128)(2,1)S(1)}, u32[]{:S(2)}, u32[]{:S(2)}) collective-permute-start(bf16[192,1152]{1,0:T(8,128)(2,1)S(1)} %get-tuple-element.37), channel_id=1, source_target_pairs={{0,16},{16,0},{1,17},{17,1},{2,18},{18,2},{3,19},{19,3},{4,20},{20... | collective-permute-start | bytes 1327112 | tf_op jit(solution)/shard_map/ppermute | solution.py:28
  41.9 16.2 %collective-permute-start.5 = (bf16[128,1152]{1,0:T(8,128)(2,1)S(1)}, bf16[128,1152]{1,0:T(8,128)(2,1)S(1)}, u32[]{:S(2)}, u32[]{:S(2)}) collective-permute-start(bf16[128,1152]{1,0:T(8,128)(2,1)S(1)} %get-tuple-element.31), channel_id=1, source_target_pairs={{0,16},{16,0},{1,17},{17,1},{2,18},{18,2},{3,19},{19,3},{4,20},{20... | collective-permute-start | bytes 884744 | tf_op jit(solution)/shard_map/ppermute | solution.py:28
  49.3 8.8 %collective-permute-start.6 = (f32[1,320]{1,0:T(1,128)S(1)}, f32[1,320]{1,0:T(1,128)S(1)}, u32[]{:S(2)}, u32[]{:S(2)}) collective-permute-start(f32[1,320]{1,0:T(1,128)S(1)} %get-tuple-element.33), channel_id=1, source_target_pairs={{0,16},{16,0},{1,17},{17,1},{2,18},{18,2},{3,19},{19,3},{4,20},{20... | collective-permute-start | bytes 3848 | tf_op jit(solution)/shard_map/ppermute | solution.py:28

commit v5 on v4

--- a/solution.py
+++ b/solution.py
@@ -22,6 +22,7 @@
 MIB = 1024 * 1024
 TOKEN = ((8, LANES), F32)
 FIRST = 192
+PACK = 16
 
 
 def swap(value, axis):
@@ -53,6 +54,10 @@
     rows = pieces[0].shape[0]
     for n, piece in enumerate(pieces):
         out[pl.ds(n * rows, rows), :] = normalize_rows(piece[...])[0].astype(BF16)
+
+
+def norm_after(raw, _, out):
+    norm_body(raw, out)
 
 
 def own_norm(image, text, out, image_held, text_held):
@@ -105,22 +110,45 @@
     return ref[pl.ds(0, rows), :], ref[pl.ds(rows, rows), :]
 
 
-def z_body(own, mate, x_near, x_far, z_near, share, token):
-    image, mate_image = halves(own)[0], halves(mate)[0]
-    total = edges(z_near[...], [image, mate_image, x_near[...], x_far[...]])
-    share[...] = (LOGIT_SCALE * total).astype(BF16)
-    token[...] = jnp.zeros(token.shape, F32)
-
-
-def x_body(start, mate, x_near, z_near, z_far, _, share, loss, token):
-    left = x_near[pl.ds(start, share.shape[0]), :]
+def in_parts(row):
+    high = row.astype(BF16).astype(F32)
+    middle = (row - high).astype(BF16).astype(F32)
+    r = lax.broadcasted_iota(jnp.int32, (PACK, row.shape[1]), 0)
+    low = jnp.where(r == 2, row - high - middle, 0.0)
+    return jnp.where(r == 0, high, jnp.where(r == 1, middle, low)).astype(BF16)
+
+
+def x_first(mate, x_near, z_near, z_far, share, loss, token):
+    left = x_near[pl.ds(0, share.shape[0]), :]
     total, loss[...] = edges(left, [halves(mate)[1], z_near[...], z_far[...]], False, True)
     share[...] = (LOGIT_SCALE * total).astype(BF16)
     token[...] = jnp.zeros(token.shape, F32)
 
 
-def own_body(own, mate, x_far, z_near, z_far, x_loss_1, x_loss_2, i_out, t_out, loss_out, x_loss):
-    x_loss[...] = as_row(jnp.concatenate([x_loss_1[...], x_loss_2[...]], axis=0))
+def x_second(mate, x_near, z_near, z_far, lost, _, share, token):
+    rows = share.shape[0] - PACK
+    left = x_near[pl.ds(x_near.shape[0] - rows, rows), :]
+    total, loss = edges(left, [halves(mate)[1], z_near[...], z_far[...]], False, True)
+    share[pl.ds(0, rows), :] = (LOGIT_SCALE * total).astype(BF16)
+    share[pl.ds(rows, PACK), :] = jnp.zeros((PACK, share.shape[1]), BF16)
+    row = as_row(jnp.concatenate([lost[...], loss], axis=0))
+    share[pl.ds(rows, PACK), pl.ds(0, row.shape[1])] = in_parts(row)
+    token[...] = jnp.zeros(token.shape, F32)
+
+
+def mid_body(own, z_near, out, token):
+    out[...] = edges(z_near[...], [halves(own)[0]])
+    token[...] = jnp.zeros(token.shape, F32)
+
+
+def z_body(start, mate, x_near, x_far, z_near, begun, _, share, token):
+    part = pl.ds(start, share.shape[0])
+    total = edges(z_near[part, :], [halves(mate)[0], x_near[...], x_far[...]])
+    share[...] = (LOGIT_SCALE * (begun[part, :] + total)).astype(BF16)
+    token[...] = jnp.zeros(token.shape, F32)
+
+
+def own_body(own, mate, x_far, z_near, z_far, _, i_out, t_out, loss_out):
     image, text = halves(own)
     mate_image, mate_text = halves(mate)
     total, loss = edges(image, [text, mate_text, z_near[...], z_far[...]], True, True)
@@ -146,70 +174,99 @@
     return copies
 
 
-def last_body(raw, total, back, _, out, token, held, sems):
-    token[...] = jnp.zeros(token.shape, F32)
-    for copy in finish(0, raw, total, back, out, held, sems):
+def last_body(start, raw, total, back, *rest):
+    token, out, held, sems = rest[-4:]
+    token[...] = jnp.zeros(token.shape, F32)
+    for copy in finish(start, raw, total, back, out, held, sems):
         copy.wait()
 
 
-def end_body(raw, total, back, i_loss, loss_back, *rest):
-    out, loss_out, held, sems, held_loss, loss_sem = rest[-6:]
+def final_body(start, raw, total, back, *rest):
+    out, held, sems = rest[-3:]
+    for copy in finish(start, raw, total, back, out, held, sems):
+        copy.wait()
+
+
+def loss_body(start, raw, total, back, i_loss, *rest):
+    loss_out, token, out, held, sems, held_loss, loss_sem = rest[-7:]
+    token[...] = jnp.zeros(token.shape, F32)
     rows = raw.shape[0]
-    held_loss[...] = ((i_loss[...] + loss_back[...]) * (1.0 / rows)).reshape(held_loss.shape)
+    parts = back[pl.ds(rows - start, PACK), :].astype(F32)[:, :rows]
+    loss = (i_loss[...] + jnp.sum(parts, axis=0, keepdims=True)) * (1.0 / rows)
+    held_loss[...] = loss.reshape(held_loss.shape)
     copies = [pltpu.make_async_copy(held_loss, loss_out, loss_sem)]
     copies[0].start()
-    for copy in copies + finish(rows - back.shape[0], raw, total, back, out, held, sems):
+    for copy in copies + finish(start, raw, total, back, out, held, sems):
         copy.wait()
 
 
-def last(raw, total, back, token, before=None, losses=()):
-    pieces = back.shape[0] // 32
-    shapes = [(raw.shape, F32), TOKEN]
-    scratch = [pltpu.VMEM(back.shape, F32), pltpu.SemaphoreType.DMA((pieces,))]
-    if before is None:
-        return call(last_body, shapes, (raw, total, back, token), far_outs=(0,), scratch=scratch)
-    line = (raw.shape[0],)
+def last(start, count, raw, total, back, token, before=(), i_loss=()):
+    args = (raw, total, back, *i_loss, token, *before)
+    shapes, far_outs = [TOKEN, (raw.shape, F32)], (1,)
+    scratch = [pltpu.VMEM((count, raw.shape[1]), F32), pltpu.SemaphoreType.DMA((count // 32,))]
+    if i_loss:
+        line = (raw.shape[0],)
+        shapes, far_outs = [(line, F32)] + shapes, (0, 2)
+        scratch += [pltpu.VMEM(line, F32), pltpu.SemaphoreType.DMA]
+    body = loss_body if i_loss else last_body
+    if before and not i_loss:
+        body, shapes, far_outs = final_body, shapes[1:], (0,)
     return call(
-        end_body,
-        [shapes[0], (line, F32)],
-        (raw, total, back, *losses, token, before),
-        far_args=(6,),
-        far_outs=(0, 1),
-        scratch=scratch + [pltpu.VMEM(line, F32), pltpu.SemaphoreType.DMA],
-        aliases={6: 0},
+        partial(body, start),
+        shapes,
+        args,
+        far_args=(len(args) - 1,) if before else (),
+        far_outs=far_outs,
+        scratch=scratch,
+        aliases={len(args) - 1: len(shapes) - 1} if before else None,
     )
 
 
 def shards(image, text):
     rows, depth = image.shape
     block, pair = (rows, depth), (2 * rows, depth)
-    x_near, z_near = swap(image, "x_hi"), swap(text, "z_lo")
+    first, second = FIRST, rows - FIRST
+    z_near, x_near = swap(text, "z_lo"), swap(image, "x_hi")
     own, image, text = call(own_norm, [(pair, BF16), (block, BF16), (block, BF16)], (image, text))
     mate = swap(own, "core")
-    (x_near,) = call(norm_body, [(block, BF16)], (x_near,))
+    (z_near,) = call(norm_body, [(block, BF16)], (z_near,))
+    z_far = swap(z_near, "core")
+    begun, token = call(mid_body, [(block, F32), TOKEN], (own, z_near))
+    (x_near,) = call(norm_after, [(block, BF16)], (x_near, token), flops=4 * 10**9)
     x_far = swap(x_near, "core")
-    (z_near,) = call(norm_body, [(block, BF16)], (z_near,), flops=4*10**9)
-    z_far = swap(z_near, "core")
-    z_share, token = call(z_body, [(block, BF16), TOKEN], (own, mate, x_near, x_far, z_near))
-    z_back = swap(z_share, "z_lo")
-    backs, losses = [], []
-    for start, count in ((0, FIRST), (FIRST, rows - FIRST)):
-        x_share, loss, token = call(
-            partial(x_body, start),
-            [((count, depth), BF16), ((count, 1), F32), TOKEN],
-            (mate, x_near, z_near, z_far, token),
-        )
-        backs.append(swap(x_share, "x_hi"))
-        losses.append(loss)
-    i_total, t_total, i_loss, x_loss = call(
+    share, x_loss, token = call(
+        x_first, [((first, depth), BF16), ((first, 1), F32), TOKEN], (mate, x_near, z_near, z_far)
+    )
+    x_1 = swap(share, "x_hi")
+    share, token = call(
+        partial(z_body, 0),
+        [((first, depth), BF16), TOKEN],
+        (mate, x_near, x_far, z_near, begun, token),
+    )
+    z_1 = swap(share, "z_lo")
+    share, token = call(
+        x_second,
+        [((second + PACK, depth), BF16), TOKEN],
+        (mate, x_near, z_near, z_far, x_loss, token),
+    )
+    x_2 = swap(share, "x_hi")
+    share, token = call(
+        partial(z_body, first),
+        [((second, depth), BF16), TOKEN],
+        (mate, x_near, x_far, z_near, begun, token),
+    )
+    z_2 = swap(share, "z_lo")
+    i_total, t_total, i_loss = call(
         own_body,
-        [(block, F32), (block, F32), ((1, rows), F32), ((1, rows), F32)],
-        (own, mate, x_far, z_near, z_far, *losses),
-    )
-    loss_back = swap(x_loss, "x_hi")
-    image_grad, token = last(image, i_total, backs[0], token)
-    text_grad, token = last(text, t_total, z_back, token)
-    image_grad, loss = last(image, i_total, backs[1], token, image_grad, (i_loss, loss_back))
+        [(block, F32), (block, F32), ((1, rows), F32)],
+        (own, mate, x_far, z_near, z_far, token),
+    )
+    token, image_grad = last(0, first, image, i_total, x_1, token)
+    token, text_grad = last(0, first, text, t_total, z_1, token)
+    loss, token, image_grad = last(
+        first, second, image, i_total, x_2, token, (image_grad,), (i_loss,)
+    )
+    (text_grad,) = last(first, second, text, t_total, z_2, token, (text_grad,))
     return (loss, image_grad, text_grad)
 
 

time: 59.6 us -> 58.6 us (0.983)
  waiting for transfers between devices: 5.36 us -> 2.43 us
  Pallas kernels: 14.5 us -> 16.6 us
    ppermute x9, waiting for transfers between devices: 5.36 us -> 2.43 us  [swap(): return lax.ppermute(value, axis, SWAP)]
    pallas_call x10 -> x13, Pallas kernels: 14.5 us -> 16.6 us  [call(): pl.pallas_call(body, out_shape=[jax.ShapeDtypeStruct(s, d) for s, d in sh...]
  transfers between devices with their start and end apart: 9 -> 9, of which waited for: 2 -> 2; matrix products, arithmetic and copies ran while one was open for 0% -> 0% of each run, Pallas kernels for 23% -> 27%
where the time goes in v5:
time: 58.6 us; the launch traced here: 58.2 us
  starting transfers between devices  36 us (61%)
  Pallas kernels  16.6 us (28%)
  waiting for transfers between devices  2.43 us (4%)
  local copies, waits for them, and re-layouts  2.22 us (4%)
  between operations  1 us (2%)
    ppermute x9, starting transfers between devices, swap(): return lax.ppermute(value, axis, SWAP)  36 us
    pallas_call x13, Pallas kernels, call(): pl.pallas_call(body, out_shape=[jax.ShapeDtypeStruct(s, d) for s, d in sh...  16.6 us
    ppermute x9, waiting for transfers between devices, swap(): return lax.ppermute(value, axis, SWAP)  2.43 us
    unnamed x4, local copies, waits for them, and re-layouts  2.22 us
  transfers between devices with their start and end apart: 9, of which 2 were waited for; matrix products, arithmetic and copies ran while one was open for 0% of the time, Pallas kernels for 27%

profile of v5, /device:TPU:1, one launch (start us, length us, event | category | flops | bytes accessed | tf_op | source)
XLA Modules:
  0.0 58.2 jit_solution(18110890828974872239)
XLA Ops:
  0.6 4.4 %collective-permute-start.2 = (bf16[320,1152]{1,0:T(8,128)(2,1)}, bf16[320,1152]{1,0:T(8,128)(2,1)S(1)}, u32[]{:S(2)}, u32[]{:S(2)}) collective-permute-start(bf16[320,1152]{1,0:T(8,128)(2,1)} %text.1), channel_id=1, source_target_pairs={{0,1},{1,0},{2,3},{3,2},{4,5},{5,4},{6,7},{7,6},{8,9},{9,8},{10,11... | collective-permute-start | bytes 2211848 | tf_op jit(solution)/shard_map/ppermute | solution.py:29
  5.0 4.7 %collective-permute-start.1 = (bf16[320,1152]{1,0:T(8,128)(2,1)}, bf16[320,1152]{1,0:T(8,128)(2,1)S(1)}, u32[]{:S(2)}, u32[]{:S(2)}) collective-permute-start(bf16[320,1152]{1,0:T(8,128)(2,1)} %image.1), channel_id=1, source_target_pairs={{0,16},{16,0},{1,17},{17,1},{2,18},{18,2},{3,19},{19,3},{4,20},{20... | collective-permute-start | bytes 2211848 | tf_op jit(solution)/shard_map/ppermute | solution.py:29
  9.7 1.1 %copy-done = bf16[320,1152]{1,0:T(8,128)(2,1)S(1)} copy-done((bf16[320,1152]{1,0:T(8,128)(2,1)S(1)}, bf16[320,1152]{1,0:T(8,128)(2,1)}, u32[]{:S(2)}) %copy-start) | copy-done | bytes 737304
  10.8 1.1 %copy-done.1 = bf16[320,1152]{1,0:T(8,128)(2,1)S(1)} copy-done((bf16[320,1152]{1,0:T(8,128)(2,1)S(1)}, bf16[320,1152]{1,0:T(8,128)(2,1)}, u32[]{:S(2)}) %copy-start.1) | copy-done | bytes 737304
  11.9 0.5 shard_map.49
  12.5 3.6 %collective-permute-start = (bf16[640,1152]{1,0:T(8,128)(2,1)S(1)}, bf16[640,1152]{1,0:T(8,128)(2,1)S(1)}, u32[]{:S(2)}, u32[]{:S(2)}) collective-permute-start(bf16[640,1152]{1,0:T(8,128)(2,1)S(1)} %get-tuple-element.28.own), channel_id=1, source_target_pairs={{0,32},{32,0},{1,33},{33,1},{2,34},{34,2},{3,35},{35,3},{4,36},{36... | collective-permute-start | bytes 4423688 | tf_op jit(solution)/shard_map/ppermute | solution.py:29
  16.1 0.9 %collective-permute-done.2.refs_0_ = bf16[320,1152]{1,0:T(8,128)(2,1)S(1)} collective-permute-done((bf16[320,1152]{1,0:T(8,128)(2,1)}, bf16[320,1152]{1,0:T(8,128)(2,1)S(1)}, u32[]{:S(2)}, u32[]{:S(2)}) %collective-permute-start.2) | collective-permute-done | bytes 737312 | tf_op jit(solution)/shard_map/ppermute | solution.py:29
  17.2 7.6 %collective-permute-start.4 = (bf16[320,1152]{1,0:T(8,128)(2,1)S(1)}, bf16[320,1152]{1,0:T(8,128)(2,1)S(1)}, u32[]{:S(2)}, u32[]{:S(2)}) collective-permute-start(bf16[320,1152]{1,0:T(8,128)(2,1)S(1)} %shard_map.50.z_near), channel_id=1, source_target_pairs={{0,32},{32,0},{1,33},{33,1},{2,34},{34,2},{3,35},{35,3},{4,36},{36... | collective-permute-start | bytes 2211848 | tf_op jit(solution)/shard_map/ppermute | solution.py:29
  24.8 1.1 %shard_map.51 = (f32[320,1152]{1,0:T(8,128)S(1)}, f32[8,128]{1,0:T(8,128)S(1)}) custom-call(bf16[640,1152]{1,0:T(8,128)(2,1)S(1)} %get-tuple-element.28.own, bf16[320,1152]{1,0:T(8,128)(2,1)S(1)} %shard_map.50.z_near), custom_call_target="tpu_custom_call" | custom-call | flops 1 | bytes 1 | tf_op jit(solution)/shard_map/pallas_call | solution.py:34
  26.2 3.5 %collective-permute-start.3 = (bf16[320,1152]{1,0:T(8,128)(2,1)S(1)}, bf16[320,1152]{1,0:T(8,128)(2,1)S(1)}, u32[]{:S(2)}, u32[]{:S(2)}) collective-permute-start(bf16[320,1152]{1,0:T(8,128)(2,1)S(1)} %shard_map.52.x_near), channel_id=1, source_target_pairs={{0,32},{32,0},{1,33},{33,1},{2,34},{34,2},{3,35},{35,3},{4,36},{36... | collective-permute-start | bytes 2211848 | tf_op jit(solution)/shard_map/ppermute | solution.py:29
  29.7 1.5 %shard_map.53 = (bf16[192,1152]{1,0:T(8,128)(2,1)S(1)}, f32[192,1]{1,0:T(8,128)S(1)}, f32[8,128]{1,0:T(8,128)S(1)}) custom-call(bf16[640,1152]{1,0:T(8,128)(2,1)S(1)} %collective-permute-done.mate, bf16[320,1152]{1,0:T(8,128)(2,1)S(1)} %shard_map.52.x_near, bf16[320,1152]{1,0:T(8,128)(2,1)S(1)} %shard_map.50.z_near, ...), custom_call_target="tpu_custom_call" | custom-call | flops 1 | bytes 1 | tf_op jit(solution)/shard_map/pallas_call | solution.py:34
  31.2 4.6 %collective-permute-start.7 = (bf16[192,1152]{1,0:T(8,128)(2,1)S(1)}, bf16[192,1152]{1,0:T(8,128)(2,1)S(1)}, u32[]{:S(2)}, u32[]{:S(2)}) collective-permute-start(bf16[192,1152]{1,0:T(8,128)(2,1)S(1)} %get-tuple-element.42), channel_id=1, source_target_pairs={{0,16},{16,0},{1,17},{17,1},{2,18},{18,2},{3,19},{19,3},{4,20},{20... | collective-permute-start | bytes 1327112 | tf_op jit(solution)/shard_map/ppermute | solution.py:29
  35.9 1.4 %shard_map.54 = (bf16[192,1152]{1,0:T(8,128)(2,1)S(1)}, f32[8,128]{1,0:T(8,128)S(1)}) custom-call(bf16[640,1152]{1,0:T(8,128)(2,1)S(1)} %collective-permute-done.mate, bf16[320,1152]{1,0:T(8,128)(2,1)S(1)} %shard_map.52.x_near, bf16[320,1152]{1,0:T(8,128)(2,1)S(1)} %collective-permute-done.3.x_far, bf16[320,1152]{1,0:T(8,128)(2,1)S(1)} %shard_map.50.z_near, ...), custom_call_target="tpu_custom_call" | custom-call | flops 1 | bytes 1 | tf_op jit(solution)/shard_map/pallas_call | solution.py:34
  37.3 1.9 %collective-permute-start.6 = (bf16[192,1152]{1,0:T(8,128)(2,1)S(1)}, bf16[192,1152]{1,0:T(8,128)(2,1)S(1)}, u32[]{:S(2)}, u32[]{:S(2)}) collective-permute-start(bf16[192,1152]{1,0:T(8,128)(2,1)S(1)} %get-tuple-element.41), channel_id=1, source_target_pairs={{0,1},{1,0},{2,3},{3,2},{4,5},{5,4},{6,7},{7,6},{8,9},{9,8},{10,11... | collective-permute-start | bytes 1327112 | tf_op jit(solution)/shard_map/ppermute | solution.py:29
  39.2 1.3 %shard_map.55 = (bf16[144,1152]{1,0:T(8,128)(2,1)S(1)}, f32[8,128]{1,0:T(8,128)S(1)}) custom-call(bf16[640,1152]{1,0:T(8,128)(2,1)S(1)} %collective-permute-done.mate, bf16[320,1152]{1,0:T(8,128)(2,1)S(1)} %shard_map.52.x_near, bf16[320,1152]{1,0:T(8,128)(2,1)S(1)} %shard_map.50.z_near, bf16[320,1152]{1,0:T(8,128)(2,1)S(1)} %collective-permute-done.4.z_far, ...), custom_call_target="tpu_custom_call" | custom-call | flops 1 | bytes 1 | tf_op jit(solution)/shard_map/pallas_call | solution.py:34
  40.6 2.1 %collective-permute-start.5 = (bf16[144,1152]{1,0:T(8,128)(2,1)S(1)}, bf16[144,1152]{1,0:T(8,128)(2,1)S(1)}, u32[]{:S(2)}, u32[]{:S(2)}) collective-permute-start(bf16[144,1152]{1,0:T(8,128)(2,1)S(1)} %get-tuple-element.37), channel_id=1, source_target_pairs={{0,16},{16,0},{1,17},{17,1},{2,18},{18,2},{3,19},{19,3},{4,20},{20... | collective-permute-start | bytes 995336 | tf_op jit(solution)/shard_map/ppermute | solution.py:29
  42.7 1.3 %shard_map.56 = (bf16[128,1152]{1,0:T(8,128)(2,1)S(1)}, f32[8,128]{1,0:T(8,128)S(1)}) custom-call(bf16[640,1152]{1,0:T(8,128)(2,1)S(1)} %collective-permute-done.mate, bf16[320,1152]{1,0:T(8,128)(2,1)S(1)} %shard_map.52.x_near, bf16[320,1152]{1,0:T(8,128)(2,1)S(1)} %collective-permute-done.3.x_far, bf16[320,1152]{1,0:T(8,128)(2,1)S(1)} %shard_map.50.z_near, ...), custom_call_target="tpu_custom_call" | custom-call | flops 1 | bytes 1 | tf_op jit(solution)/shard_map/pallas_call | solution.py:34
  44.0 3.5 %collective-permute-start.8 = (bf16[128,1152]{1,0:T(8,128)(2,1)S(1)}, bf16[128,1152]{1,0:T(8,128)(2,1)S(1)}, u32[]{:S(2)}, u32[]{:S(2)}) collective-permute-start(bf16[128,1152]{1,0:T(8,128)(2,1)S(1)} %get-tuple-element.48), channel_id=1, source_target_pairs={{0,1},{1,0},{2,3},{3,2},{4,5},{5,4},{6,7},{7,6},{8,9},{9,8},{10,11... | collective-permute-start | bytes 884744 | tf_op jit(solution)/shard_map/ppermute | solution.py:29
  47.6 4.3 %shard_map.57 = (f32[320,1152]{1,0:T(8,128)S(1)}, f32[320,1152]{1,0:T(8,128)S(1)}, f32[1,320]{1,0:T(1,128)S(1)}) custom-call(bf16[640,1152]{1,0:T(8,128)(2,1)S(1)} %get-tuple-element.28.own, bf16[640,1152]{1,0:T(8,128)(2,1)S(1)} %collective-permute-done.mate, bf16[320,1152]{1,0:T(8,128)(2,1)S(1)} %collective-permute-done.3.x_far, ...), custom_call_target="tpu_custom_call" | custom-call | flops 1 | bytes 1 | tf_op jit(solution)/shard_map/pallas_call | solution.py:34
  51.9 1.2 %shard_map.58 = (f32[8,128]{1,0:T(8,128)S(1)}, f32[320,1152]{1,0:T(8,128)}) custom-call(bf16[320,1152]{1,0:T(8,128)(2,1)S(1)} %get-tuple-element.27.raw, f32[320,1152]{1,0:T(8,128)S(1)} %get-tuple-element.36.total, bf16[192,1152]{1,0:T(8,128)(2,1)S(1)} %collective-permute-done.7.back, f32[8,128]{1,0:T(8,128)S(1)} %get-tuple-element.35._.rest_0_), custom_call_target="tpu_custom_call" | custom-call | flops 1 | bytes 1 | tf_op jit(solution)/shard_map/pallas_call | solution.py:34
  53.1 1.2 %shard_map.59 = (f32[8,128]{1,0:T(8,128)S(1)}, f32[320,1152]{1,0:T(8,128)}) custom-call(bf16[320,1152]{1,0:T(8,128)(2,1)S(1)} %get-tuple-element.39.raw, f32[320,1152]{1,0:T(8,128)S(1)} %get-tuple-element.40.total, bf16[192,1152]{1,0:T(8,128)(2,1)S(1)} %collective-permute-done.6.back, f32[8,128]{1,0:T(8,128)S(1)} %get-tuple-element.43.rest_0_), custom_call_target="tpu_custom_call" | custom-call | flops 1 | bytes 1 | tf_op jit(solution)/shard_map/pallas_call | solution.py:34
  54.4 1.1 %shard_map.60 = (f32[320]{0:T(512)}, f32[8,128]{1,0:T(8,128)S(1)}, f32[320,1152]{1,0:T(8,128)}) custom-call(bf16[320,1152]{1,0:T(8,128)(2,1)S(1)} %get-tuple-element.27.raw, f32[320,1152]{1,0:T(8,128)S(1)} %get-tuple-element.36.total, bf16[144,1152]{1,0:T(8,128)(2,1)S(1)} %collective-permute-done.5.back, ...), custom_call_target="tpu_custom_call", output_to_operand_aliasing={{2}: (5, {})} | custom-call | flops 1 | bytes 1 | tf_op jit(solution)/shard_map/pallas_call | solution.py:34
  55.5 1.5 %collective-permute-done.8.back = bf16[128,1152]{1,0:T(8,128)(2,1)S(1)} collective-permute-done((bf16[128,1152]{1,0:T(8,128)(2,1)S(1)}, bf16[128,1152]{1,0:T(8,128)(2,1)S(1)}, u32[]{:S(2)}, u32[]{:S(2)}) %collective-permute-start.8) | collective-permute-done | bytes 294944 | tf_op jit(solution)/shard_map/ppermute | solution.py:29
  57.0 1.0 %shard_map.61 = f32[320,1152]{1,0:T(8,128)} custom-call(bf16[320,1152]{1,0:T(8,128)(2,1)S(1)} %get-tuple-element.39.raw, f32[320,1152]{1,0:T(8,128)S(1)} %get-tuple-element.40.total, bf16[128,1152]{1,0:T(8,128)(2,1)S(1)} %collective-permute-done.8.back, f32[8,128]{1,0:T(8,128)S(1)} %get-tuple-element.49.rest_0_, ...), custom_call_target="tpu_custom_call", output_to_operand_aliasing={{}: (4, {})} | custom-call | flops 1 | bytes 1 | tf_op jit(solution)/shard_map/pallas_call | solution.py:34
  (11 shorter events, 0.5 us)
Async XLA Ops:
  0.6 16.3 %collective-permute-start.2 = (bf16[320,1152]{1,0:T(8,128)(2,1)}, bf16[320,1152]{1,0:T(8,128)(2,1)S(1)}, u32[]{:S(2)}, u32[]{:S(2)}) collective-permute-start(bf16[320,1152]{1,0:T(8,128)(2,1)} %text.1), channel_id=1, source_target_pairs={{0,1},{1,0},{2,3},{3,2},{4,5},{5,4},{6,7},{7,6},{8,9},{9,8},{10,11... | collective-permute-start | bytes 2211848 | tf_op jit(solution)/shard_map/ppermute | solution.py:29
  5.0 21.0 %collective-permute-start.1 = (bf16[320,1152]{1,0:T(8,128)(2,1)}, bf16[320,1152]{1,0:T(8,128)(2,1)S(1)}, u32[]{:S(2)}, u32[]{:S(2)}) collective-permute-start(bf16[320,1152]{1,0:T(8,128)(2,1)} %image.1), channel_id=1, source_target_pairs={{0,16},{16,0},{1,17},{17,1},{2,18},{18,2},{3,19},{19,3},{4,20},{20... | collective-permute-start | bytes 2211848 | tf_op jit(solution)/shard_map/ppermute | solution.py:29
  9.7 1.1 %copy-start = (bf16[320,1152]{1,0:T(8,128)(2,1)S(1)}, bf16[320,1152]{1,0:T(8,128)(2,1)}, u32[]{:S(2)}) copy-start(bf16[320,1152]{1,0:T(8,128)(2,1)} %text.1) | copy-start | bytes 2211844
  10.8 1.1 %copy-start.1 = (bf16[320,1152]{1,0:T(8,128)(2,1)S(1)}, bf16[320,1152]{1,0:T(8,128)(2,1)}, u32[]{:S(2)}) copy-start(bf16[320,1152]{1,0:T(8,128)(2,1)} %image.1) | copy-start | bytes 2211844
  12.5 17.2 %collective-permute-start = (bf16[640,1152]{1,0:T(8,128)(2,1)S(1)}, bf16[640,1152]{1,0:T(8,128)(2,1)S(1)}, u32[]{:S(2)}, u32[]{:S(2)}) collective-permute-start(bf16[640,1152]{1,0:T(8,128)(2,1)S(1)} %get-tuple-element.28.own), channel_id=1, source_target_pairs={{0,32},{32,0},{1,33},{33,1},{2,34},{34,2},{3,35},{35,3},{4,36},{36... | collective-permute-start | bytes 4423688 | tf_op jit(solution)/shard_map/ppermute | solution.py:29
  17.2 12.5 %collective-permute-start.4 = (bf16[320,1152]{1,0:T(8,128)(2,1)S(1)}, bf16[320,1152]{1,0:T(8,128)(2,1)S(1)}, u32[]{:S(2)}, u32[]{:S(2)}) collective-permute-start(bf16[320,1152]{1,0:T(8,128)(2,1)S(1)} %shard_map.50.z_near), channel_id=1, source_target_pairs={{0,32},{32,0},{1,33},{33,1},{2,34},{34,2},{3,35},{35,3},{4,36},{36... | collective-permute-start | bytes 2211848 | tf_op jit(solution)/shard_map/ppermute | solution.py:29
  26.2 9.6 %collective-permute-start.3 = (bf16[320,1152]{1,0:T(8,128)(2,1)S(1)}, bf16[320,1152]{1,0:T(8,128)(2,1)S(1)}, u32[]{:S(2)}, u32[]{:S(2)}) collective-permute-start(bf16[320,1152]{1,0:T(8,128)(2,1)S(1)} %shard_map.52.x_near), channel_id=1, source_target_pairs={{0,32},{32,0},{1,33},{33,1},{2,34},{34,2},{3,35},{35,3},{4,36},{36... | collective-permute-start | bytes 2211848 | tf_op jit(solution)/shard_map/ppermute | solution.py:29
  31.2 20.7 %collective-permute-start.7 = (bf16[192,1152]{1,0:T(8,128)(2,1)S(1)}, bf16[192,1152]{1,0:T(8,128)(2,1)S(1)}, u32[]{:S(2)}, u32[]{:S(2)}) collective-permute-start(bf16[192,1152]{1,0:T(8,128)(2,1)S(1)} %get-tuple-element.42), channel_id=1, source_target_pairs={{0,16},{16,0},{1,17},{17,1},{2,18},{18,2},{3,19},{19,3},{4,20},{20... | collective-permute-start | bytes 1327112 | tf_op jit(solution)/shard_map/ppermute | solution.py:29
  37.3 15.8 %collective-permute-start.6 = (bf16[192,1152]{1,0:T(8,128)(2,1)S(1)}, bf16[192,1152]{1,0:T(8,128)(2,1)S(1)}, u32[]{:S(2)}, u32[]{:S(2)}) collective-permute-start(bf16[192,1152]{1,0:T(8,128)(2,1)S(1)} %get-tuple-element.41), channel_id=1, source_target_pairs={{0,1},{1,0},{2,3},{3,2},{4,5},{5,4},{6,7},{7,6},{8,9},{9,8},{10,11... | collective-permute-start | bytes 1327112 | tf_op jit(solution)/shard_map/ppermute | solution.py:29
  40.6 13.8 %collective-permute-start.5 = (bf16[144,1152]{1,0:T(8,128)(2,1)S(1)}, bf16[144,1152]{1,0:T(8,128)(2,1)S(1)}, u32[]{:S(2)}, u32[]{:S(2)}) collective-permute-start(bf16[144,1152]{1,0:T(8,128)(2,1)S(1)} %get-tuple-element.37), channel_id=1, source_target_pairs={{0,16},{16,0},{1,17},{17,1},{2,18},{18,2},{3,19},{19,3},{4,20},{20... | collective-permute-start | bytes 995336 | tf_op jit(solution)/shard_map/ppermute | solution.py:29
  44.0 13.0 %collective-permute-start.8 = (bf16[128,1152]{1,0:T(8,128)(2,1)S(1)}, bf16[128,1152]{1,0:T(8,128)(2,1)S(1)}, u32[]{:S(2)}, u32[]{:S(2)}) collective-permute-start(bf16[128,1152]{1,0:T(8,128)(2,1)S(1)} %get-tuple-element.48), channel_id=1, source_target_pairs={{0,1},{1,0},{2,3},{3,2},{4,5},{5,4},{6,7},{7,6},{8,9},{9,8},{10,11... | collective-permute-start | bytes 884744 | tf_op jit(solution)/shard_map/ppermute | solution.py:29

commit v6 on v5

--- a/solution.py
+++ b/solution.py
@@ -23,6 +23,7 @@
 TOKEN = ((8, LANES), F32)
 FIRST = 192
 PACK = 16
+PIECES = 2
 
 
 def swap(value, axis):
@@ -60,8 +61,12 @@
     norm_body(raw, out)
 
 
-def own_norm(image, text, out, image_held, text_held):
+def own_norm(image, text, out, image_held, text_held, text_unit, *pieces):
     norm_body(image, text, out)
+    text_unit[...] = halves(out)[1]
+    rows = pieces[0].shape[0]
+    for n, piece in enumerate(pieces):
+        piece[...] = out[pl.ds(n * rows, rows), :]
     image_held[...] = image[...]
     text_held[...] = text[...]
 
@@ -118,17 +123,17 @@
     return jnp.where(r == 0, high, jnp.where(r == 1, middle, low)).astype(BF16)
 
 
-def x_first(mate, x_near, z_near, z_far, share, loss, token):
+def x_first(mate_text, x_near, z_near, z_far, share, loss, token):
     left = x_near[pl.ds(0, share.shape[0]), :]
-    total, loss[...] = edges(left, [halves(mate)[1], z_near[...], z_far[...]], False, True)
+    total, loss[...] = edges(left, [mate_text[...], z_near[...], z_far[...]], False, True)
     share[...] = (LOGIT_SCALE * total).astype(BF16)
     token[...] = jnp.zeros(token.shape, F32)
 
 
-def x_second(mate, x_near, z_near, z_far, lost, _, share, token):
+def x_second(mate_text, x_near, z_near, z_far, lost, _, share, token):
     rows = share.shape[0] - PACK
     left = x_near[pl.ds(x_near.shape[0] - rows, rows), :]
-    total, loss = edges(left, [halves(mate)[1], z_near[...], z_far[...]], False, True)
+    total, loss = edges(left, [mate_text[...], z_near[...], z_far[...]], False, True)
     share[pl.ds(0, rows), :] = (LOGIT_SCALE * total).astype(BF16)
     share[pl.ds(rows, PACK), :] = jnp.zeros((PACK, share.shape[1]), BF16)
     row = as_row(jnp.concatenate([lost[...], loss], axis=0))
@@ -136,25 +141,27 @@
     token[...] = jnp.zeros(token.shape, F32)
 
 
-def mid_body(own, z_near, out, token):
-    out[...] = edges(z_near[...], [halves(own)[0]])
-    token[...] = jnp.zeros(token.shape, F32)
-
-
-def z_body(start, mate, x_near, x_far, z_near, begun, _, share, token):
+def mid_body(own, z_near, *rest):
+    mates, (out, token) = rest[:-2], rest[-2:]
+    out[...] = edges(z_near[...], [halves(own)[0]] + [mate[...] for mate in mates])
+    token[...] = jnp.zeros(token.shape, F32)
+
+
+def z_body(start, x_near, x_far, z_near, begun, _, share, token):
     part = pl.ds(start, share.shape[0])
-    total = edges(z_near[part, :], [halves(mate)[0], x_near[...], x_far[...]])
+    total = edges(z_near[part, :], [x_near[...], x_far[...]])
     share[...] = (LOGIT_SCALE * (begun[part, :] + total)).astype(BF16)
     token[...] = jnp.zeros(token.shape, F32)
 
 
-def own_body(own, mate, x_far, z_near, z_far, _, i_out, t_out, loss_out):
+def own_body(own, mate_text, x_far, z_near, z_far, _, *rest):
+    mates, (i_out, t_out, loss_out) = rest[:-3], rest[-3:]
     image, text = halves(own)
-    mate_image, mate_text = halves(mate)
+    mate_text, mates = mate_text[...], [mate[...] for mate in mates]
     total, loss = edges(image, [text, mate_text, z_near[...], z_far[...]], True, True)
     i_out[...] = LOGIT_SCALE * total
     loss_out[...] = as_row(loss)
-    t_out[...] = LOGIT_SCALE * edges(text, [image, mate_image, x_far[...]], True)
+    t_out[...] = LOGIT_SCALE * edges(text, [image, *mates, x_far[...]], True)
 
 
 def raw_gradient(raw, gradient):
@@ -227,39 +234,43 @@
     block, pair = (rows, depth), (2 * rows, depth)
     first, second = FIRST, rows - FIRST
     z_near, x_near = swap(text, "z_lo"), swap(image, "x_hi")
-    own, image, text = call(own_norm, [(pair, BF16), (block, BF16), (block, BF16)], (image, text))
-    mate = swap(own, "core")
+    piece = ((rows // PIECES, depth), BF16)
+    own, image, text, own_text, *own_image = call(
+        own_norm, [(pair, BF16)] + [(block, BF16)] * 3 + [piece] * PIECES, (image, text)
+    )
+    mate_image = [swap(piece, "core") for piece in own_image]
+    mate_text = swap(own_text, "core")
     (z_near,) = call(norm_body, [(block, BF16)], (z_near,))
     z_far = swap(z_near, "core")
-    begun, token = call(mid_body, [(block, F32), TOKEN], (own, z_near))
+    begun, token = call(mid_body, [(block, F32), TOKEN], (own, z_near, *mate_image))
     (x_near,) = call(norm_after, [(block, BF16)], (x_near, token), flops=4 * 10**9)
     x_far = swap(x_near, "core")
     share, x_loss, token = call(
-        x_first, [((first, depth), BF16), ((first, 1), F32), TOKEN], (mate, x_near, z_near, z_far)
+        x_first, [((first, depth), BF16), ((first, 1), F32), TOKEN], (mate_text, x_near, z_near, z_far)
     )
     x_1 = swap(share, "x_hi")
     share, token = call(
         partial(z_body, 0),
         [((first, depth), BF16), TOKEN],
-        (mate, x_near, x_far, z_near, begun, token),
+        (x_near, x_far, z_near, begun, token),
     )
     z_1 = swap(share, "z_lo")
     share, token = call(
         x_second,
         [((second + PACK, depth), BF16), TOKEN],
-        (mate, x_near, z_near, z_far, x_loss, token),
+        (mate_text, x_near, z_near, z_far, x_loss, token),
     )
     x_2 = swap(share, "x_hi")
     share, token = call(
         partial(z_body, first),
         [((second, depth), BF16), TOKEN],
-        (mate, x_near, x_far, z_near, begun, token),
+        (x_near, x_far, z_near, begun, token),
     )
     z_2 = swap(share, "z_lo")
     i_total, t_total, i_loss = call(
         own_body,
         [(block, F32), (block, F32), ((1, rows), F32)],
-        (own, mate, x_far, z_near, z_far, token),
+        (own, mate_text, x_far, z_near, z_far, token, *mate_image),
     )
     token, image_grad = last(0, first, image, i_total, x_1, token)
     token, text_grad = last(0, first, text, t_total, z_1, token)

time: 58.6 us -> 58.5 us (level)
    ppermute x9 -> x11, waiting for transfers between devices: 2.43 us -> 1.85 us  [swap(): return lax.ppermute(value, axis, SWAP)]
    ppermute x9 -> x11, starting transfers between devices: 36 us -> 36.2 us  [swap(): return lax.ppermute(value, axis, SWAP)]
  transfers between devices with their start and end apart: 9 -> 11, of which waited for: 2 -> 1; matrix products, arithmetic and copies ran while one was open for 0% -> 0% of each run, Pallas kernels for 27% -> 27%
where the time goes in v6:
time: 58.5 us; the launch traced here: 58 us
  starting transfers between devices  36.2 us (62%)
  Pallas kernels  16.7 us (29%)
  local copies, waits for them, and re-layouts  2.22 us (4%)
  waiting for transfers between devices  1.85 us (3%)
  between operations  1.05 us (2%)
    ppermute x11, starting transfers between devices, swap(): return lax.ppermute(value, axis, SWAP)  36.2 us
    pallas_call x13, Pallas kernels, call(): pl.pallas_call(body, out_shape=[jax.ShapeDtypeStruct(s, d) for s, d in sh...  16.7 us
    unnamed x4, local copies, waits for them, and re-layouts  2.22 us
    ppermute x11, waiting for transfers between devices, swap(): return lax.ppermute(value, axis, SWAP)  1.85 us
  transfers between devices with their start and end apart: 11, of which 1 were waited for; matrix products, arithmetic and copies ran while one was open for 0% of the time, Pallas kernels for 27%

profile of v6, /device:TPU:1, one launch (start us, length us, event | category | flops | bytes accessed | tf_op | source)
XLA Modules:
  0.0 58.0 jit_solution(14867096319358263145)
XLA Ops:
  0.6 4.4 %collective-permute-start.2 = (bf16[320,1152]{1,0:T(8,128)(2,1)}, bf16[320,1152]{1,0:T(8,128)(2,1)S(1)}, u32[]{:S(2)}, u32[]{:S(2)}) collective-permute-start(bf16[320,1152]{1,0:T(8,128)(2,1)} %text.1), channel_id=1, source_target_pairs={{0,1},{1,0},{2,3},{3,2},{4,5},{5,4},{6,7},{7,6},{8,9},{9,8},{10,11... | collective-permute-start | bytes 2211848 | tf_op jit(solution)/shard_map/ppermute | solution.py:30
  5.0 4.7 %collective-permute-start.1 = (bf16[320,1152]{1,0:T(8,128)(2,1)}, bf16[320,1152]{1,0:T(8,128)(2,1)S(1)}, u32[]{:S(2)}, u32[]{:S(2)}) collective-permute-start(bf16[320,1152]{1,0:T(8,128)(2,1)} %image.1), channel_id=1, source_target_pairs={{0,16},{16,0},{1,17},{17,1},{2,18},{18,2},{3,19},{19,3},{4,20},{20... | collective-permute-start | bytes 2211848 | tf_op jit(solution)/shard_map/ppermute | solution.py:30
  9.7 1.1 %copy-done = bf16[320,1152]{1,0:T(8,128)(2,1)S(1)} copy-done((bf16[320,1152]{1,0:T(8,128)(2,1)S(1)}, bf16[320,1152]{1,0:T(8,128)(2,1)}, u32[]{:S(2)}) %copy-start) | copy-done | bytes 737304
  10.8 1.1 %copy-done.1 = bf16[320,1152]{1,0:T(8,128)(2,1)S(1)} copy-done((bf16[320,1152]{1,0:T(8,128)(2,1)S(1)}, bf16[320,1152]{1,0:T(8,128)(2,1)}, u32[]{:S(2)}) %copy-start.1) | copy-done | bytes 737304
  12.6 3.6 %collective-permute-start.3 = (bf16[160,1152]{1,0:T(8,128)(2,1)S(1)}, bf16[160,1152]{1,0:T(8,128)(2,1)S(1)}, u32[]{:S(2)}, u32[]{:S(2)}) collective-permute-start(bf16[160,1152]{1,0:T(8,128)(2,1)S(1)} %get-tuple-element.33), channel_id=1, source_target_pairs={{0,32},{32,0},{1,33},{33,1},{2,34},{34,2},{3,35},{35,3},{4,36},{36... | collective-permute-start | bytes 1105928 | tf_op jit(solution)/shard_map/ppermute | solution.py:30
  16.2 1.9 %collective-permute-start.4 = (bf16[160,1152]{1,0:T(8,128)(2,1)S(1)}, bf16[160,1152]{1,0:T(8,128)(2,1)S(1)}, u32[]{:S(2)}, u32[]{:S(2)}) collective-permute-start(bf16[160,1152]{1,0:T(8,128)(2,1)S(1)} %get-tuple-element.34), channel_id=1, source_target_pairs={{0,32},{32,0},{1,33},{33,1},{2,34},{34,2},{3,35},{35,3},{4,36},{36... | collective-permute-start | bytes 1105928 | tf_op jit(solution)/shard_map/ppermute | solution.py:30
  18.1 2.4 %collective-permute-start = (bf16[320,1152]{1,0:T(8,128)(2,1)S(1)}, bf16[320,1152]{1,0:T(8,128)(2,1)S(1)}, u32[]{:S(2)}, u32[]{:S(2)}) collective-permute-start(bf16[320,1152]{1,0:T(8,128)(2,1)S(1)} %get-tuple-element.32), channel_id=1, source_target_pairs={{0,32},{32,0},{1,33},{33,1},{2,34},{34,2},{3,35},{35,3},{4,36},{36... | collective-permute-start | bytes 2211848 | tf_op jit(solution)/shard_map/ppermute | solution.py:30
  20.8 4.0 %collective-permute-start.6 = (bf16[320,1152]{1,0:T(8,128)(2,1)S(1)}, bf16[320,1152]{1,0:T(8,128)(2,1)S(1)}, u32[]{:S(2)}, u32[]{:S(2)}) collective-permute-start(bf16[320,1152]{1,0:T(8,128)(2,1)S(1)} %shard_map.50.z_near), channel_id=1, source_target_pairs={{0,32},{32,0},{1,33},{33,1},{2,34},{34,2},{3,35},{35,3},{4,36},{36... | collective-permute-start | bytes 2211848 | tf_op jit(solution)/shard_map/ppermute | solution.py:30
  24.8 1.6 %shard_map.51 = (f32[320,1152]{1,0:T(8,128)S(1)}, f32[8,128]{1,0:T(8,128)S(1)}) custom-call(bf16[640,1152]{1,0:T(8,128)(2,1)S(1)} %get-tuple-element.31.own, bf16[320,1152]{1,0:T(8,128)(2,1)S(1)} %shard_map.50.z_near, bf16[160,1152]{1,0:T(8,128)(2,1)S(1)} %collective-permute-done.3.rest_0_, bf16[160,1152]{1,0:T(8,128)(2,1)S(1)} %collective-permute-done.4.rest_1_), custom_call_target="tpu_custom_call" | custom-call | flops 1 | bytes 1 | tf_op jit(solution)/shard_map/pallas_call | solution.py:35
  26.7 3.0 %collective-permute-start.5 = (bf16[320,1152]{1,0:T(8,128)(2,1)S(1)}, bf16[320,1152]{1,0:T(8,128)(2,1)S(1)}, u32[]{:S(2)}, u32[]{:S(2)}) collective-permute-start(bf16[320,1152]{1,0:T(8,128)(2,1)S(1)} %shard_map.52.x_near), channel_id=1, source_target_pairs={{0,32},{32,0},{1,33},{33,1},{2,34},{34,2},{3,35},{35,3},{4,36},{36... | collective-permute-start | bytes 2211848 | tf_op jit(solution)/shard_map/ppermute | solution.py:30
  29.7 1.5 %shard_map.53 = (bf16[192,1152]{1,0:T(8,128)(2,1)S(1)}, f32[192,1]{1,0:T(8,128)S(1)}, f32[8,128]{1,0:T(8,128)S(1)}) custom-call(bf16[320,1152]{1,0:T(8,128)(2,1)S(1)} %collective-permute-done.mate_text, bf16[320,1152]{1,0:T(8,128)(2,1)S(1)} %shard_map.52.x_near, bf16[320,1152]{1,0:T(8,128)(2,1)S(1)} %shard_map.50.z_near, ...), custom_call_target="tpu_custom_call" | custom-call | flops 1 | bytes 1 | tf_op jit(solution)/shard_map/pallas_call | solution.py:35
  31.2 4.6 %collective-permute-start.9 = (bf16[192,1152]{1,0:T(8,128)(2,1)S(1)}, bf16[192,1152]{1,0:T(8,128)(2,1)S(1)}, u32[]{:S(2)}, u32[]{:S(2)}) collective-permute-start(bf16[192,1152]{1,0:T(8,128)(2,1)S(1)} %get-tuple-element.48), channel_id=1, source_target_pairs={{0,16},{16,0},{1,17},{17,1},{2,18},{18,2},{3,19},{19,3},{4,20},{20... | collective-permute-start | bytes 1327112 | tf_op jit(solution)/shard_map/ppermute | solution.py:30
  35.9 1.2 %shard_map.54 = (bf16[192,1152]{1,0:T(8,128)(2,1)S(1)}, f32[8,128]{1,0:T(8,128)S(1)}) custom-call(bf16[320,1152]{1,0:T(8,128)(2,1)S(1)} %shard_map.52.x_near, bf16[320,1152]{1,0:T(8,128)(2,1)S(1)} %collective-permute-done.5.x_far, bf16[320,1152]{1,0:T(8,128)(2,1)S(1)} %shard_map.50.z_near, f32[320,1152]{1,0:T(8,128)S(1)} %get-tuple-element.36.begun, ...), custom_call_target="tpu_custom_call" | custom-call | flops 1 | bytes 1 | tf_op jit(solution)/shard_map/pallas_call | solution.py:35
  37.1 2.3 %collective-permute-start.8 = (bf16[192,1152]{1,0:T(8,128)(2,1)S(1)}, bf16[192,1152]{1,0:T(8,128)(2,1)S(1)}, u32[]{:S(2)}, u32[]{:S(2)}) collective-permute-start(bf16[192,1152]{1,0:T(8,128)(2,1)S(1)} %get-tuple-element.47), channel_id=1, source_target_pairs={{0,1},{1,0},{2,3},{3,2},{4,5},{5,4},{6,7},{7,6},{8,9},{9,8},{10,11... | collective-permute-start | bytes 1327112 | tf_op jit(solution)/shard_map/ppermute | solution.py:30
  39.4 1.3 %shard_map.55 = (bf16[144,1152]{1,0:T(8,128)(2,1)S(1)}, f32[8,128]{1,0:T(8,128)S(1)}) custom-call(bf16[320,1152]{1,0:T(8,128)(2,1)S(1)} %collective-permute-done.mate_text, bf16[320,1152]{1,0:T(8,128)(2,1)S(1)} %shard_map.52.x_near, bf16[320,1152]{1,0:T(8,128)(2,1)S(1)} %shard_map.50.z_near, bf16[320,1152]{1,0:T(8,128)(2,1)S(1)} %collective-permute-done.6.z_far, ...), custom_call_target="tpu_custom_call" | custom-call | flops 1 | bytes 1 | tf_op jit(solution)/shard_map/pallas_call | solution.py:35
  40.7 2.1 %collective-permute-start.7 = (bf16[144,1152]{1,0:T(8,128)(2,1)S(1)}, bf16[144,1152]{1,0:T(8,128)(2,1)S(1)}, u32[]{:S(2)}, u32[]{:S(2)}) collective-permute-start(bf16[144,1152]{1,0:T(8,128)(2,1)S(1)} %get-tuple-element.43), channel_id=1, source_target_pairs={{0,16},{16,0},{1,17},{17,1},{2,18},{18,2},{3,19},{19,3},{4,20},{20... | collective-permute-start | bytes 995336 | tf_op jit(solution)/shard_map/ppermute | solution.py:30
  42.9 1.0 %shard_map.56 = (bf16[128,1152]{1,0:T(8,128)(2,1)S(1)}, f32[8,128]{1,0:T(8,128)S(1)}) custom-call(bf16[320,1152]{1,0:T(8,128)(2,1)S(1)} %shard_map.52.x_near, bf16[320,1152]{1,0:T(8,128)(2,1)S(1)} %collective-permute-done.5.x_far, bf16[320,1152]{1,0:T(8,128)(2,1)S(1)} %shard_map.50.z_near, f32[320,1152]{1,0:T(8,128)S(1)} %get-tuple-element.36.begun, ...), custom_call_target="tpu_custom_call" | custom-call | flops 1 | bytes 1 | tf_op jit(solution)/shard_map/pallas_call | solution.py:35
  43.9 3.1 %collective-permute-start.10 = (bf16[128,1152]{1,0:T(8,128)(2,1)S(1)}, bf16[128,1152]{1,0:T(8,128)(2,1)S(1)}, u32[]{:S(2)}, u32[]{:S(2)}) collective-permute-start(bf16[128,1152]{1,0:T(8,128)(2,1)S(1)} %get-tuple-element.54), channel_id=1, source_target_pairs={{0,1},{1,0},{2,3},{3,2},{4,5},{5,4},{6,7},{7,6},{8,9},{9,8},{10,11... | collective-permute-start | bytes 884744 | tf_op jit(solution)/shard_map/ppermute | solution.py:30
  47.0 4.3 %shard_map.57 = (f32[320,1152]{1,0:T(8,128)S(1)}, f32[320,1152]{1,0:T(8,128)S(1)}, f32[1,320]{1,0:T(1,128)S(1)}) custom-call(bf16[640,1152]{1,0:T(8,128)(2,1)S(1)} %get-tuple-element.31.own, bf16[320,1152]{1,0:T(8,128)(2,1)S(1)} %collective-permute-done.mate_text, bf16[320,1152]{1,0:T(8,128)(2,1)S(1)} %collective-permute-done.5.x_far, ...), custom_call_target="tpu_custom_call" | custom-call | flops 1 | bytes 1 | tf_op jit(solution)/shard_map/pallas_call | solution.py:35
  51.4 1.2 %shard_map.58 = (f32[8,128]{1,0:T(8,128)S(1)}, f32[320,1152]{1,0:T(8,128)}) custom-call(bf16[320,1152]{1,0:T(8,128)(2,1)S(1)} %get-tuple-element.30.raw, f32[320,1152]{1,0:T(8,128)S(1)} %get-tuple-element.42.total, bf16[192,1152]{1,0:T(8,128)(2,1)S(1)} %collective-permute-done.9.back, f32[8,128]{1,0:T(8,128)S(1)} %get-tuple-element.41._.rest_0_), custom_call_target="tpu_custom_call" | custom-call | flops 1 | bytes 1 | tf_op jit(solution)/shard_map/pallas_call | solution.py:35
  52.6 1.2 %shard_map.59 = (f32[8,128]{1,0:T(8,128)S(1)}, f32[320,1152]{1,0:T(8,128)}) custom-call(bf16[320,1152]{1,0:T(8,128)(2,1)S(1)} %get-tuple-element.45.raw, f32[320,1152]{1,0:T(8,128)S(1)} %get-tuple-element.46.total, bf16[192,1152]{1,0:T(8,128)(2,1)S(1)} %collective-permute-done.8.back, f32[8,128]{1,0:T(8,128)S(1)} %get-tuple-element.49.rest_0_), custom_call_target="tpu_custom_call" | custom-call | flops 1 | bytes 1 | tf_op jit(solution)/shard_map/pallas_call | solution.py:35
  53.9 1.1 %shard_map.60 = (f32[320]{0:T(512)}, f32[8,128]{1,0:T(8,128)S(1)}, f32[320,1152]{1,0:T(8,128)}) custom-call(bf16[320,1152]{1,0:T(8,128)(2,1)S(1)} %get-tuple-element.30.raw, f32[320,1152]{1,0:T(8,128)S(1)} %get-tuple-element.42.total, bf16[144,1152]{1,0:T(8,128)(2,1)S(1)} %collective-permute-done.7.back, ...), custom_call_target="tpu_custom_call", output_to_operand_aliasing={{2}: (5, {})} | custom-call | flops 1 | bytes 1 | tf_op jit(solution)/shard_map/pallas_call | solution.py:35
  55.0 1.8 %collective-permute-done.10.back = bf16[128,1152]{1,0:T(8,128)(2,1)S(1)} collective-permute-done((bf16[128,1152]{1,0:T(8,128)(2,1)S(1)}, bf16[128,1152]{1,0:T(8,128)(2,1)S(1)}, u32[]{:S(2)}, u32[]{:S(2)}) %collective-permute-start.10) | collective-permute-done | bytes 294944 | tf_op jit(solution)/shard_map/ppermute | solution.py:30
  56.8 1.0 %shard_map.61 = f32[320,1152]{1,0:T(8,128)} custom-call(bf16[320,1152]{1,0:T(8,128)(2,1)S(1)} %get-tuple-element.45.raw, f32[320,1152]{1,0:T(8,128)S(1)} %get-tuple-element.46.total, bf16[128,1152]{1,0:T(8,128)(2,1)S(1)} %collective-permute-done.10.back, f32[8,128]{1,0:T(8,128)S(1)} %get-tuple-element.55.rest_0_, ...), custom_call_target="tpu_custom_call", output_to_operand_aliasing={{}: (4, {})} | custom-call | flops 1 | bytes 1 | tf_op jit(solution)/shard_map/pallas_call | solution.py:35
  (15 shorter events, 1.2 us)
Async XLA Ops:
  0.6 19.9 %collective-permute-start.2 = (bf16[320,1152]{1,0:T(8,128)(2,1)}, bf16[320,1152]{1,0:T(8,128)(2,1)S(1)}, u32[]{:S(2)}, u32[]{:S(2)}) collective-permute-start(bf16[320,1152]{1,0:T(8,128)(2,1)} %text.1), channel_id=1, source_target_pairs={{0,1},{1,0},{2,3},{3,2},{4,5},{5,4},{6,7},{7,6},{8,9},{9,8},{10,11... | collective-permute-start | bytes 2211848 | tf_op jit(solution)/shard_map/ppermute | solution.py:30
  5.0 21.4 %collective-permute-start.1 = (bf16[320,1152]{1,0:T(8,128)(2,1)}, bf16[320,1152]{1,0:T(8,128)(2,1)S(1)}, u32[]{:S(2)}, u32[]{:S(2)}) collective-permute-start(bf16[320,1152]{1,0:T(8,128)(2,1)} %image.1), channel_id=1, source_target_pairs={{0,16},{16,0},{1,17},{17,1},{2,18},{18,2},{3,19},{19,3},{4,20},{20... | collective-permute-start | bytes 2211848 | tf_op jit(solution)/shard_map/ppermute | solution.py:30
  9.7 1.1 %copy-start = (bf16[320,1152]{1,0:T(8,128)(2,1)S(1)}, bf16[320,1152]{1,0:T(8,128)(2,1)}, u32[]{:S(2)}) copy-start(bf16[320,1152]{1,0:T(8,128)(2,1)} %text.1) | copy-start | bytes 2211844
  10.8 1.1 %copy-start.1 = (bf16[320,1152]{1,0:T(8,128)(2,1)S(1)}, bf16[320,1152]{1,0:T(8,128)(2,1)}, u32[]{:S(2)}) copy-start(bf16[320,1152]{1,0:T(8,128)(2,1)} %image.1) | copy-start | bytes 2211844
  12.6 12.2 %collective-permute-start.3 = (bf16[160,1152]{1,0:T(8,128)(2,1)S(1)}, bf16[160,1152]{1,0:T(8,128)(2,1)S(1)}, u32[]{:S(2)}, u32[]{:S(2)}) collective-permute-start(bf16[160,1152]{1,0:T(8,128)(2,1)S(1)} %get-tuple-element.33), channel_id=1, source_target_pairs={{0,32},{32,0},{1,33},{33,1},{2,34},{34,2},{3,35},{35,3},{4,36},{36... | collective-permute-start | bytes 1105928 | tf_op jit(solution)/shard_map/ppermute | solution.py:30
  16.2 8.6 %collective-permute-start.4 = (bf16[160,1152]{1,0:T(8,128)(2,1)S(1)}, bf16[160,1152]{1,0:T(8,128)(2,1)S(1)}, u32[]{:S(2)}, u32[]{:S(2)}) collective-permute-start(bf16[160,1152]{1,0:T(8,128)(2,1)S(1)} %get-tuple-element.34), channel_id=1, source_target_pairs={{0,32},{32,0},{1,33},{33,1},{2,34},{34,2},{3,35},{35,3},{4,36},{36... | collective-permute-start | bytes 1105928 | tf_op jit(solution)/shard_map/ppermute | solution.py:30
  18.1 11.6 %collective-permute-start = (bf16[320,1152]{1,0:T(8,128)(2,1)S(1)}, bf16[320,1152]{1,0:T(8,128)(2,1)S(1)}, u32[]{:S(2)}, u32[]{:S(2)}) collective-permute-start(bf16[320,1152]{1,0:T(8,128)(2,1)S(1)} %get-tuple-element.32), channel_id=1, source_target_pairs={{0,32},{32,0},{1,33},{33,1},{2,34},{34,2},{3,35},{35,3},{4,36},{36... | collective-permute-start | bytes 2211848 | tf_op jit(solution)/shard_map/ppermute | solution.py:30
  20.8 8.9 %collective-permute-start.6 = (bf16[320,1152]{1,0:T(8,128)(2,1)S(1)}, bf16[320,1152]{1,0:T(8,128)(2,1)S(1)}, u32[]{:S(2)}, u32[]{:S(2)}) collective-permute-start(bf16[320,1152]{1,0:T(8,128)(2,1)S(1)} %shard_map.50.z_near), channel_id=1, source_target_pairs={{0,32},{32,0},{1,33},{33,1},{2,34},{34,2},{3,35},{35,3},{4,36},{36... | collective-permute-start | bytes 2211848 | tf_op jit(solution)/shard_map/ppermute | solution.py:30
  26.7 9.2 %collective-permute-start.5 = (bf16[320,1152]{1,0:T(8,128)(2,1)S(1)}, bf16[320,1152]{1,0:T(8,128)(2,1)S(1)}, u32[]{:S(2)}, u32[]{:S(2)}) collective-permute-start(bf16[320,1152]{1,0:T(8,128)(2,1)S(1)} %shard_map.52.x_near), channel_id=1, source_target_pairs={{0,32},{32,0},{1,33},{33,1},{2,34},{34,2},{3,35},{35,3},{4,36},{36... | collective-permute-start | bytes 2211848 | tf_op jit(solution)/shard_map/ppermute | solution.py:30
  31.2 20.2 %collective-permute-start.9 = (bf16[192,1152]{1,0:T(8,128)(2,1)S(1)}, bf16[192,1152]{1,0:T(8,128)(2,1)S(1)}, u32[]{:S(2)}, u32[]{:S(2)}) collective-permute-start(bf16[192,1152]{1,0:T(8,128)(2,1)S(1)} %get-tuple-element.48), channel_id=1, source_target_pairs={{0,16},{16,0},{1,17},{17,1},{2,18},{18,2},{3,19},{19,3},{4,20},{20... | collective-permute-start | bytes 1327112 | tf_op jit(solution)/shard_map/ppermute | solution.py:30
  37.1 15.5 %collective-permute-start.8 = (bf16[192,1152]{1,0:T(8,128)(2,1)S(1)}, bf16[192,1152]{1,0:T(8,128)(2,1)S(1)}, u32[]{:S(2)}, u32[]{:S(2)}) collective-permute-start(bf16[192,1152]{1,0:T(8,128)(2,1)S(1)} %get-tuple-element.47), channel_id=1, source_target_pairs={{0,1},{1,0},{2,3},{3,2},{4,5},{5,4},{6,7},{7,6},{8,9},{9,8},{10,11... | collective-permute-start | bytes 1327112 | tf_op jit(solution)/shard_map/ppermute | solution.py:30
  40.7 13.1 %collective-permute-start.7 = (bf16[144,1152]{1,0:T(8,128)(2,1)S(1)}, bf16[144,1152]{1,0:T(8,128)(2,1)S(1)}, u32[]{:S(2)}, u32[]{:S(2)}) collective-permute-start(bf16[144,1152]{1,0:T(8,128)(2,1)S(1)} %get-tuple-element.43), channel_id=1, source_target_pairs={{0,16},{16,0},{1,17},{17,1},{2,18},{18,2},{3,19},{19,3},{4,20},{20... | collective-permute-start | bytes 995336 | tf_op jit(solution)/shard_map/ppermute | solution.py:30
  43.9 12.9 %collective-permute-start.10 = (bf16[128,1152]{1,0:T(8,128)(2,1)S(1)}, bf16[128,1152]{1,0:T(8,128)(2,1)S(1)}, u32[]{:S(2)}, u32[]{:S(2)}) collective-permute-start(bf16[128,1152]{1,0:T(8,128)(2,1)S(1)} %get-tuple-element.54), channel_id=1, source_target_pairs={{0,1},{1,0},{2,3},{3,2},{4,5},{5,4},{6,7},{7,6},{8,9},{9,8},{10,11... | collective-permute-start | bytes 884744 | tf_op jit(solution)/shard_map/ppermute | solution.py:30

commit v7 on v6

--- a/solution.py
+++ b/solution.py
@@ -23,7 +23,7 @@
 TOKEN = ((8, LANES), F32)
 FIRST = 192
 PACK = 16
-PIECES = 2
+PIECES = 1
 
 
 def swap(value, axis):
@@ -123,7 +123,7 @@
     return jnp.where(r == 0, high, jnp.where(r == 1, middle, low)).astype(BF16)
 
 
-def x_first(mate_text, x_near, z_near, z_far, share, loss, token):
+def x_first(mate_text, x_near, z_near, z_far, _, share, loss, token):
     left = x_near[pl.ds(0, share.shape[0]), :]
     total, loss[...] = edges(left, [mate_text[...], z_near[...], z_far[...]], False, True)
     share[...] = (LOGIT_SCALE * total).astype(BF16)
@@ -141,16 +141,11 @@
     token[...] = jnp.zeros(token.shape, F32)
 
 
-def mid_body(own, z_near, *rest):
-    mates, (out, token) = rest[:-2], rest[-2:]
-    out[...] = edges(z_near[...], [halves(own)[0]] + [mate[...] for mate in mates])
-    token[...] = jnp.zeros(token.shape, F32)
-
-
-def z_body(start, x_near, x_far, z_near, begun, _, share, token):
+def z_body(start, own, x_near, x_far, z_near, *rest):
+    mates, (_, share, token) = rest[:-3], rest[-3:]
     part = pl.ds(start, share.shape[0])
-    total = edges(z_near[part, :], [x_near[...], x_far[...]])
-    share[...] = (LOGIT_SCALE * (begun[part, :] + total)).astype(BF16)
+    images = [halves(own)[0], *[mate[...] for mate in mates], x_near[...], x_far[...]]
+    share[...] = (LOGIT_SCALE * edges(z_near[part, :], images)).astype(BF16)
     token[...] = jnp.zeros(token.shape, F32)
 
 
@@ -233,28 +228,29 @@
     rows, depth = image.shape
     block, pair = (rows, depth), (2 * rows, depth)
     first, second = FIRST, rows - FIRST
-    z_near, x_near = swap(text, "z_lo"), swap(image, "x_hi")
+    x_near, z_near = swap(image, "x_hi"), swap(text, "z_lo")
     piece = ((rows // PIECES, depth), BF16)
     own, image, text, own_text, *own_image = call(
         own_norm, [(pair, BF16)] + [(block, BF16)] * 3 + [piece] * PIECES, (image, text)
     )
     mate_image = [swap(piece, "core") for piece in own_image]
     mate_text = swap(own_text, "core")
-    (z_near,) = call(norm_body, [(block, BF16)], (z_near,))
+    (x_near,) = call(norm_body, [(block, BF16)], (x_near,))
+    x_far = swap(x_near, "core")
+    (z_near,) = call(norm_body, [(block, BF16)], (z_near,), flops=4 * 10**9)
     z_far = swap(z_near, "core")
-    begun, token = call(mid_body, [(block, F32), TOKEN], (own, z_near, *mate_image))
-    (x_near,) = call(norm_after, [(block, BF16)], (x_near, token), flops=4 * 10**9)
-    x_far = swap(x_near, "core")
-    share, x_loss, token = call(
-        x_first, [((first, depth), BF16), ((first, 1), F32), TOKEN], (mate_text, x_near, z_near, z_far)
-    )
-    x_1 = swap(share, "x_hi")
     share, token = call(
         partial(z_body, 0),
         [((first, depth), BF16), TOKEN],
-        (x_near, x_far, z_near, begun, token),
+        (own, x_near, x_far, z_near, *mate_image, z_near),
     )
     z_1 = swap(share, "z_lo")
+    share, x_loss, token = call(
+        x_first,
+        [((first, depth), BF16), ((first, 1), F32), TOKEN],
+        (mate_text, x_near, z_near, z_far, token),
+    )
+    x_1 = swap(share, "x_hi")
     share, token = call(
         x_second,
         [((second + PACK, depth), BF16), TOKEN],
@@ -264,7 +260,7 @@
     share, token = call(
         partial(z_body, first),
         [((second, depth), BF16), TOKEN],
-        (x_near, x_far, z_near, begun, token),
+        (own, x_near, x_far, z_near, *mate_image, token),
     )
     z_2 = swap(share, "z_lo")
     i_total, t_total, i_loss = call(

time: 58.5 us -> 58 us (level)
  waiting for transfers between devices: 1.85 us -> 1.06 us
    ppermute x11 -> x10, waiting for transfers between devices: 1.85 us -> 1.06 us  [swap(): return lax.ppermute(value, axis, SWAP)]
    ppermute x11 -> x10, starting transfers between devices: 36.2 us -> 36.6 us  [swap(): return lax.ppermute(value, axis, SWAP)]
    pallas_call x13 -> x12, Pallas kernels: 16.7 us -> 16.6 us  [call(): pl.pallas_call(body, out_shape=[jax.ShapeDtypeStruct(s, d) for s, d in sh...]
  transfers between devices with their start and end apart: 11 -> 10, of which waited for: 1 -> 1; matrix products, arithmetic and copies ran while one was open for 0% -> 0% of each run, Pallas kernels for 27% -> 24%
where the time goes in v7:
time: 58 us; the launch traced here: 57.5 us
  starting transfers between devices  36.6 us (63%)
  Pallas kernels  16.6 us (29%)
  local copies, waits for them, and re-layouts  2.22 us (4%)
  waiting for transfers between devices  1.06 us (2%)
  between operations  1.02 us (2%)
    ppermute x10, starting transfers between devices, swap(): return lax.ppermute(value, axis, SWAP)  36.6 us
    pallas_call x12, Pallas kernels, call(): pl.pallas_call(body, out_shape=[jax.ShapeDtypeStruct(s, d) for s, d in sh...  16.6 us
    unnamed x4, local copies, waits for them, and re-layouts  2.22 us
  transfers between devices with their start and end apart: 10, of which 1 were waited for; matrix products, arithmetic and copies ran while one was open for 0% of the time, Pallas kernels for 24%

profile of v7, /device:TPU:1, one launch (start us, length us, event | category | flops | bytes accessed | tf_op | source)
XLA Modules:
  0.0 57.5 jit_solution(18230519262059219177)
XLA Ops:
  0.6 5.5 %collective-permute-start.1 = (bf16[320,1152]{1,0:T(8,128)(2,1)}, bf16[320,1152]{1,0:T(8,128)(2,1)S(1)}, u32[]{:S(2)}, u32[]{:S(2)}) collective-permute-start(bf16[320,1152]{1,0:T(8,128)(2,1)} %image.1), channel_id=1, source_target_pairs={{0,16},{16,0},{1,17},{17,1},{2,18},{18,2},{3,19},{19,3},{4,20},{20... | collective-permute-start | bytes 2211848 | tf_op jit(solution)/shard_map/ppermute | solution.py:30
  6.1 3.5 %collective-permute-start.3 = (bf16[320,1152]{1,0:T(8,128)(2,1)}, bf16[320,1152]{1,0:T(8,128)(2,1)S(1)}, u32[]{:S(2)}, u32[]{:S(2)}) collective-permute-start(bf16[320,1152]{1,0:T(8,128)(2,1)} %text.1), channel_id=1, source_target_pairs={{0,1},{1,0},{2,3},{3,2},{4,5},{5,4},{6,7},{7,6},{8,9},{9,8},{10,11... | collective-permute-start | bytes 2211848 | tf_op jit(solution)/shard_map/ppermute | solution.py:30
  9.7 1.1 %copy-done = bf16[320,1152]{1,0:T(8,128)(2,1)S(1)} copy-done((bf16[320,1152]{1,0:T(8,128)(2,1)S(1)}, bf16[320,1152]{1,0:T(8,128)(2,1)}, u32[]{:S(2)}) %copy-start) | copy-done | bytes 737304
  10.8 1.1 %copy-done.1 = bf16[320,1152]{1,0:T(8,128)(2,1)S(1)} copy-done((bf16[320,1152]{1,0:T(8,128)(2,1)S(1)}, bf16[320,1152]{1,0:T(8,128)(2,1)}, u32[]{:S(2)}) %copy-start.1) | copy-done | bytes 737304
  11.9 0.7 %shard_map.49 = (bf16[640,1152]{1,0:T(8,128)(2,1)S(1)}, bf16[320,1152]{1,0:T(8,128)(2,1)S(1)}, bf16[320,1152]{1,0:T(8,128)(2,1)S(1)}, bf16[320,1152]{1,0:T(8,128)(2,1)S(1)}, bf16[320,1152]{1,0:T(8,128)(2,1)S(1)}) custom-call(bf16[320,1152]{1,0:T(8,128)(2,1)S(1)} %copy-done, bf16[320,1152]{1,0:T(8,128)(2,1)S(1)} %copy-done.1), custom_call_target="tpu_custom_call" | custom-call | flops 1 | bytes 1 | tf_op jit(solution)/shard_map/pallas_call | solution.py:35
  12.6 3.6 %collective-permute-start = (bf16[320,1152]{1,0:T(8,128)(2,1)S(1)}, bf16[320,1152]{1,0:T(8,128)(2,1)S(1)}, u32[]{:S(2)}, u32[]{:S(2)}) collective-permute-start(bf16[320,1152]{1,0:T(8,128)(2,1)S(1)} %get-tuple-element.29), channel_id=1, source_target_pairs={{0,32},{32,0},{1,33},{33,1},{2,34},{34,2},{3,35},{35,3},{4,36},{36... | collective-permute-start | bytes 2211848 | tf_op jit(solution)/shard_map/ppermute | solution.py:30
  16.2 1.9 %collective-permute-start.5 = (bf16[320,1152]{1,0:T(8,128)(2,1)S(1)}, bf16[320,1152]{1,0:T(8,128)(2,1)S(1)}, u32[]{:S(2)}, u32[]{:S(2)}) collective-permute-start(bf16[320,1152]{1,0:T(8,128)(2,1)S(1)} %get-tuple-element.30), channel_id=1, source_target_pairs={{0,32},{32,0},{1,33},{33,1},{2,34},{34,2},{3,35},{35,3},{4,36},{36... | collective-permute-start | bytes 2211848 | tf_op jit(solution)/shard_map/ppermute | solution.py:30
  18.1 1.0 %collective-permute-done.1.refs_0_ = bf16[320,1152]{1,0:T(8,128)(2,1)S(1)} collective-permute-done((bf16[320,1152]{1,0:T(8,128)(2,1)}, bf16[320,1152]{1,0:T(8,128)(2,1)S(1)}, u32[]{:S(2)}, u32[]{:S(2)}) %collective-permute-start.1) | collective-permute-done | bytes 737312 | tf_op jit(solution)/shard_map/ppermute | solution.py:30
  19.4 6.5 %collective-permute-start.2 = (bf16[320,1152]{1,0:T(8,128)(2,1)S(1)}, bf16[320,1152]{1,0:T(8,128)(2,1)S(1)}, u32[]{:S(2)}, u32[]{:S(2)}) collective-permute-start(bf16[320,1152]{1,0:T(8,128)(2,1)S(1)} %shard_map.50.x_near), channel_id=1, source_target_pairs={{0,32},{32,0},{1,33},{33,1},{2,34},{34,2},{3,35},{35,3},{4,36},{36... | collective-permute-start | bytes 2211848 | tf_op jit(solution)/shard_map/ppermute | solution.py:30
  25.9 0.2 shard_map.51.z_near.rest_1_
  26.2 3.3 %collective-permute-start.4 = (bf16[320,1152]{1,0:T(8,128)(2,1)S(1)}, bf16[320,1152]{1,0:T(8,128)(2,1)S(1)}, u32[]{:S(2)}, u32[]{:S(2)}) collective-permute-start(bf16[320,1152]{1,0:T(8,128)(2,1)S(1)} %shard_map.51.z_near.rest_1_), channel_id=1, source_target_pairs={{0,32},{32,0},{1,33},{33,1},{2,34},{34,2},{3,35},{35,3},{4,36},{36... | collective-permute-start | bytes 2211848 | tf_op jit(solution)/shard_map/ppermute | solution.py:30
  29.5 2.0 %shard_map.52 = (bf16[192,1152]{1,0:T(8,128)(2,1)S(1)}, f32[8,128]{1,0:T(8,128)S(1)}) custom-call(bf16[640,1152]{1,0:T(8,128)(2,1)S(1)} %get-tuple-element.28.own, bf16[320,1152]{1,0:T(8,128)(2,1)S(1)} %shard_map.50.x_near, bf16[320,1152]{1,0:T(8,128)(2,1)S(1)} %collective-permute-done.2.x_far, bf16[320,1152]{1,0:T(8,128)(2,1)S(1)} %shard_map.51.z_near.rest_1_, ...), custom_call_target="tpu_custom_call" | custom-call | flops 1 | bytes 1 | tf_op jit(solution)/shard_map/pallas_call | solution.py:35
  31.5 1.5 %shard_map.53 = (bf16[192,1152]{1,0:T(8,128)(2,1)S(1)}, f32[192,1]{1,0:T(8,128)S(1)}, f32[8,128]{1,0:T(8,128)S(1)}) custom-call(bf16[320,1152]{1,0:T(8,128)(2,1)S(1)} %collective-permute-done.mate_text, bf16[320,1152]{1,0:T(8,128)(2,1)S(1)} %shard_map.50.x_near, bf16[320,1152]{1,0:T(8,128)(2,1)S(1)} %shard_map.51.z_near.rest_1_, ...), custom_call_target="tpu_custom_call" | custom-call | flops 1 | bytes 1 | tf_op jit(solution)/shard_map/pallas_call | solution.py:35
  33.0 3.6 %collective-permute-start.8 = (bf16[192,1152]{1,0:T(8,128)(2,1)S(1)}, bf16[192,1152]{1,0:T(8,128)(2,1)S(1)}, u32[]{:S(2)}, u32[]{:S(2)}) collective-permute-start(bf16[192,1152]{1,0:T(8,128)(2,1)S(1)} %get-tuple-element.42), channel_id=1, source_target_pairs={{0,16},{16,0},{1,17},{17,1},{2,18},{18,2},{3,19},{19,3},{4,20},{20... | collective-permute-start | bytes 1327112 | tf_op jit(solution)/shard_map/ppermute | solution.py:30
  36.6 3.6 %collective-permute-start.7 = (bf16[192,1152]{1,0:T(8,128)(2,1)S(1)}, bf16[192,1152]{1,0:T(8,128)(2,1)S(1)}, u32[]{:S(2)}, u32[]{:S(2)}) collective-permute-start(bf16[192,1152]{1,0:T(8,128)(2,1)S(1)} %get-tuple-element.41), channel_id=1, source_target_pairs={{0,1},{1,0},{2,3},{3,2},{4,5},{5,4},{6,7},{7,6},{8,9},{9,8},{10,11... | collective-permute-start | bytes 1327112 | tf_op jit(solution)/shard_map/ppermute | solution.py:30
  40.2 1.3 %shard_map.54 = (bf16[144,1152]{1,0:T(8,128)(2,1)S(1)}, f32[8,128]{1,0:T(8,128)S(1)}) custom-call(bf16[320,1152]{1,0:T(8,128)(2,1)S(1)} %collective-permute-done.mate_text, bf16[320,1152]{1,0:T(8,128)(2,1)S(1)} %shard_map.50.x_near, bf16[320,1152]{1,0:T(8,128)(2,1)S(1)} %shard_map.51.z_near.rest_1_, bf16[320,1152]{1,0:T(8,128)(2,1)S(1)} %collective-permute-done.4.z_far, ...), custom_call_target="tpu_custom_call" | custom-call | flops 1 | bytes 1 | tf_op jit(solution)/shard_map/pallas_call | solution.py:35
  41.5 3.0 %collective-permute-start.6 = (bf16[144,1152]{1,0:T(8,128)(2,1)S(1)}, bf16[144,1152]{1,0:T(8,128)(2,1)S(1)}, u32[]{:S(2)}, u32[]{:S(2)}) collective-permute-start(bf16[144,1152]{1,0:T(8,128)(2,1)S(1)} %get-tuple-element.37), channel_id=1, source_target_pairs={{0,16},{16,0},{1,17},{17,1},{2,18},{18,2},{3,19},{19,3},{4,20},{20... | collective-permute-start | bytes 995336 | tf_op jit(solution)/shard_map/ppermute | solution.py:30
  44.5 1.8 %shard_map.55 = (bf16[128,1152]{1,0:T(8,128)(2,1)S(1)}, f32[8,128]{1,0:T(8,128)S(1)}) custom-call(bf16[640,1152]{1,0:T(8,128)(2,1)S(1)} %get-tuple-element.28.own, bf16[320,1152]{1,0:T(8,128)(2,1)S(1)} %shard_map.50.x_near, bf16[320,1152]{1,0:T(8,128)(2,1)S(1)} %collective-permute-done.2.x_far, bf16[320,1152]{1,0:T(8,128)(2,1)S(1)} %shard_map.51.z_near.rest_1_, ...), custom_call_target="tpu_custom_call" | custom-call | flops 1 | bytes 1 | tf_op jit(solution)/shard_map/pallas_call | solution.py:35
  46.3 2.1 %collective-permute-start.9 = (bf16[128,1152]{1,0:T(8,128)(2,1)S(1)}, bf16[128,1152]{1,0:T(8,128)(2,1)S(1)}, u32[]{:S(2)}, u32[]{:S(2)}) collective-permute-start(bf16[128,1152]{1,0:T(8,128)(2,1)S(1)} %get-tuple-element.48), channel_id=1, source_target_pairs={{0,1},{1,0},{2,3},{3,2},{4,5},{5,4},{6,7},{7,6},{8,9},{9,8},{10,11... | collective-permute-start | bytes 884744 | tf_op jit(solution)/shard_map/ppermute | solution.py:30
  48.4 4.3 %shard_map.56 = (f32[320,1152]{1,0:T(8,128)S(1)}, f32[320,1152]{1,0:T(8,128)S(1)}, f32[1,320]{1,0:T(1,128)S(1)}) custom-call(bf16[640,1152]{1,0:T(8,128)(2,1)S(1)} %get-tuple-element.28.own, bf16[320,1152]{1,0:T(8,128)(2,1)S(1)} %collective-permute-done.mate_text, bf16[320,1152]{1,0:T(8,128)(2,1)S(1)} %collective-permute-done.2.x_far, ...), custom_call_target="tpu_custom_call" | custom-call | flops 1 | bytes 1 | tf_op jit(solution)/shard_map/pallas_call | solution.py:35
  52.7 1.2 %shard_map.57 = (f32[8,128]{1,0:T(8,128)S(1)}, f32[320,1152]{1,0:T(8,128)}) custom-call(bf16[320,1152]{1,0:T(8,128)(2,1)S(1)} %get-tuple-element.27.raw, f32[320,1152]{1,0:T(8,128)S(1)} %get-tuple-element.36.total, bf16[192,1152]{1,0:T(8,128)(2,1)S(1)} %collective-permute-done.8.back, f32[8,128]{1,0:T(8,128)S(1)} %get-tuple-element.35._.rest_0_), custom_call_target="tpu_custom_call" | custom-call | flops 1 | bytes 1 | tf_op jit(solution)/shard_map/pallas_call | solution.py:35
  54.0 1.2 %shard_map.58 = (f32[8,128]{1,0:T(8,128)S(1)}, f32[320,1152]{1,0:T(8,128)}) custom-call(bf16[320,1152]{1,0:T(8,128)(2,1)S(1)} %get-tuple-element.39.raw, f32[320,1152]{1,0:T(8,128)S(1)} %get-tuple-element.40.total, bf16[192,1152]{1,0:T(8,128)(2,1)S(1)} %collective-permute-done.7.back, f32[8,128]{1,0:T(8,128)S(1)} %get-tuple-element.43.rest_0_), custom_call_target="tpu_custom_call" | custom-call | flops 1 | bytes 1 | tf_op jit(solution)/shard_map/pallas_call | solution.py:35
  55.2 1.1 %shard_map.59 = (f32[320]{0:T(512)}, f32[8,128]{1,0:T(8,128)S(1)}, f32[320,1152]{1,0:T(8,128)}) custom-call(bf16[320,1152]{1,0:T(8,128)(2,1)S(1)} %get-tuple-element.27.raw, f32[320,1152]{1,0:T(8,128)S(1)} %get-tuple-element.36.total, bf16[144,1152]{1,0:T(8,128)(2,1)S(1)} %collective-permute-done.6.back, ...), custom_call_target="tpu_custom_call", output_to_operand_aliasing={{2}: (5, {})} | custom-call | flops 1 | bytes 1 | tf_op jit(solution)/shard_map/pallas_call | solution.py:35
  56.3 1.1 %shard_map.60 = f32[320,1152]{1,0:T(8,128)} custom-call(bf16[320,1152]{1,0:T(8,128)(2,1)S(1)} %get-tuple-element.39.raw, f32[320,1152]{1,0:T(8,128)S(1)} %get-tuple-element.40.total, bf16[128,1152]{1,0:T(8,128)(2,1)S(1)} %collective-permute-done.9.back, f32[8,128]{1,0:T(8,128)S(1)} %get-tuple-element.49.rest_0_, ...), custom_call_target="tpu_custom_call", output_to_operand_aliasing={{}: (4, {})} | custom-call | flops 1 | bytes 1 | tf_op jit(solution)/shard_map/pallas_call | solution.py:35
  (12 shorter events, 0.3 us)
Async XLA Ops:
  0.6 18.5 %collective-permute-start.1 = (bf16[320,1152]{1,0:T(8,128)(2,1)}, bf16[320,1152]{1,0:T(8,128)(2,1)S(1)}, u32[]{:S(2)}, u32[]{:S(2)}) collective-permute-start(bf16[320,1152]{1,0:T(8,128)(2,1)} %image.1), channel_id=1, source_target_pairs={{0,16},{16,0},{1,17},{17,1},{2,18},{18,2},{3,19},{19,3},{4,20},{20... | collective-permute-start | bytes 2211848 | tf_op jit(solution)/shard_map/ppermute | solution.py:30
  6.1 19.8 %collective-permute-start.3 = (bf16[320,1152]{1,0:T(8,128)(2,1)}, bf16[320,1152]{1,0:T(8,128)(2,1)S(1)}, u32[]{:S(2)}, u32[]{:S(2)}) collective-permute-start(bf16[320,1152]{1,0:T(8,128)(2,1)} %text.1), channel_id=1, source_target_pairs={{0,1},{1,0},{2,3},{3,2},{4,5},{5,4},{6,7},{7,6},{8,9},{9,8},{10,11... | collective-permute-start | bytes 2211848 | tf_op jit(solution)/shard_map/ppermute | solution.py:30
  9.7 1.1 %copy-start = (bf16[320,1152]{1,0:T(8,128)(2,1)S(1)}, bf16[320,1152]{1,0:T(8,128)(2,1)}, u32[]{:S(2)}) copy-start(bf16[320,1152]{1,0:T(8,128)(2,1)} %image.1) | copy-start | bytes 2211844
  10.8 1.1 %copy-start.1 = (bf16[320,1152]{1,0:T(8,128)(2,1)S(1)}, bf16[320,1152]{1,0:T(8,128)(2,1)}, u32[]{:S(2)}) copy-start(bf16[320,1152]{1,0:T(8,128)(2,1)} %text.1) | copy-start | bytes 2211844
  12.6 18.9 %collective-permute-start = (bf16[320,1152]{1,0:T(8,128)(2,1)S(1)}, bf16[320,1152]{1,0:T(8,128)(2,1)S(1)}, u32[]{:S(2)}, u32[]{:S(2)}) collective-permute-start(bf16[320,1152]{1,0:T(8,128)(2,1)S(1)} %get-tuple-element.29), channel_id=1, source_target_pairs={{0,32},{32,0},{1,33},{33,1},{2,34},{34,2},{3,35},{35,3},{4,36},{36... | collective-permute-start | bytes 2211848 | tf_op jit(solution)/shard_map/ppermute | solution.py:30
  16.2 13.3 %collective-permute-start.5 = (bf16[320,1152]{1,0:T(8,128)(2,1)S(1)}, bf16[320,1152]{1,0:T(8,128)(2,1)S(1)}, u32[]{:S(2)}, u32[]{:S(2)}) collective-permute-start(bf16[320,1152]{1,0:T(8,128)(2,1)S(1)} %get-tuple-element.30), channel_id=1, source_target_pairs={{0,32},{32,0},{1,33},{33,1},{2,34},{34,2},{3,35},{35,3},{4,36},{36... | collective-permute-start | bytes 2211848 | tf_op jit(solution)/shard_map/ppermute | solution.py:30
  19.4 10.1 %collective-permute-start.2 = (bf16[320,1152]{1,0:T(8,128)(2,1)S(1)}, bf16[320,1152]{1,0:T(8,128)(2,1)S(1)}, u32[]{:S(2)}, u32[]{:S(2)}) collective-permute-start(bf16[320,1152]{1,0:T(8,128)(2,1)S(1)} %shard_map.50.x_near), channel_id=1, source_target_pairs={{0,32},{32,0},{1,33},{33,1},{2,34},{34,2},{3,35},{35,3},{4,36},{36... | collective-permute-start | bytes 2211848 | tf_op jit(solution)/shard_map/ppermute | solution.py:30
  26.2 5.3 %collective-permute-start.4 = (bf16[320,1152]{1,0:T(8,128)(2,1)S(1)}, bf16[320,1152]{1,0:T(8,128)(2,1)S(1)}, u32[]{:S(2)}, u32[]{:S(2)}) collective-permute-start(bf16[320,1152]{1,0:T(8,128)(2,1)S(1)} %shard_map.51.z_near.rest_1_), channel_id=1, source_target_pairs={{0,32},{32,0},{1,33},{33,1},{2,34},{34,2},{3,35},{35,3},{4,36},{36... | collective-permute-start | bytes 2211848 | tf_op jit(solution)/shard_map/ppermute | solution.py:30
  33.0 19.7 %collective-permute-start.8 = (bf16[192,1152]{1,0:T(8,128)(2,1)S(1)}, bf16[192,1152]{1,0:T(8,128)(2,1)S(1)}, u32[]{:S(2)}, u32[]{:S(2)}) collective-permute-start(bf16[192,1152]{1,0:T(8,128)(2,1)S(1)} %get-tuple-element.42), channel_id=1, source_target_pairs={{0,16},{16,0},{1,17},{17,1},{2,18},{18,2},{3,19},{19,3},{4,20},{20... | collective-permute-start | bytes 1327112 | tf_op jit(solution)/shard_map/ppermute | solution.py:30
  36.6 17.3 %collective-permute-start.7 = (bf16[192,1152]{1,0:T(8,128)(2,1)S(1)}, bf16[192,1152]{1,0:T(8,128)(2,1)S(1)}, u32[]{:S(2)}, u32[]{:S(2)}) collective-permute-start(bf16[192,1152]{1,0:T(8,128)(2,1)S(1)} %get-tuple-element.41), channel_id=1, source_target_pairs={{0,1},{1,0},{2,3},{3,2},{4,5},{5,4},{6,7},{7,6},{8,9},{9,8},{10,11... | collective-permute-start | bytes 1327112 | tf_op jit(solution)/shard_map/ppermute | solution.py:30
  41.5 13.7 %collective-permute-start.6 = (bf16[144,1152]{1,0:T(8,128)(2,1)S(1)}, bf16[144,1152]{1,0:T(8,128)(2,1)S(1)}, u32[]{:S(2)}, u32[]{:S(2)}) collective-permute-start(bf16[144,1152]{1,0:T(8,128)(2,1)S(1)} %get-tuple-element.37), channel_id=1, source_target_pairs={{0,16},{16,0},{1,17},{17,1},{2,18},{18,2},{3,19},{19,3},{4,20},{20... | collective-permute-start | bytes 995336 | tf_op jit(solution)/shard_map/ppermute | solution.py:30
  46.3 10.0 %collective-permute-start.9 = (bf16[128,1152]{1,0:T(8,128)(2,1)S(1)}, bf16[128,1152]{1,0:T(8,128)(2,1)S(1)}, u32[]{:S(2)}, u32[]{:S(2)}) collective-permute-start(bf16[128,1152]{1,0:T(8,128)(2,1)S(1)} %get-tuple-element.48), channel_id=1, source_target_pairs={{0,1},{1,0},{2,3},{3,2},{4,5},{5,4},{6,7},{7,6},{8,9},{9,8},{10,11... | collective-permute-start | bytes 884744 | tf_op jit(solution)/shard_map/ppermute | solution.py:30

commit v8 on v7

--- a/solution.py
+++ b/solution.py
@@ -149,14 +149,22 @@
     token[...] = jnp.zeros(token.shape, F32)
 
 
-def own_body(own, mate_text, x_far, z_near, z_far, _, *rest):
+def pair_body(own, i_out, t_out, loss_out, token):
+    image, text = halves(own)
+    i_out[...], loss = edges(image, [text], True, True)
+    loss_out[...] = as_row(loss)
+    t_out[...] = edges(text, [image], True)
+    token[...] = jnp.zeros(token.shape, F32)
+
+
+def own_body(own, mate_text, x_far, z_near, z_far, _, i_in, t_in, loss_in, *rest):
     mates, (i_out, t_out, loss_out) = rest[:-3], rest[-3:]
     image, text = halves(own)
     mate_text, mates = mate_text[...], [mate[...] for mate in mates]
-    total, loss = edges(image, [text, mate_text, z_near[...], z_far[...]], True, True)
-    i_out[...] = LOGIT_SCALE * total
-    loss_out[...] = as_row(loss)
-    t_out[...] = LOGIT_SCALE * edges(text, [image, *mates, x_far[...]], True)
+    total, loss = edges(image, [mate_text, z_near[...], z_far[...]], False, True)
+    i_out[...] = LOGIT_SCALE * (i_in[...] + total)
+    loss_out[...] = loss_in[...] + as_row(loss)
+    t_out[...] = LOGIT_SCALE * (t_in[...] + edges(text, [*mates, x_far[...]]))
 
 
 def raw_gradient(raw, gradient):
@@ -235,7 +243,10 @@
     )
     mate_image = [swap(piece, "core") for piece in own_image]
     mate_text = swap(own_text, "core")
-    (x_near,) = call(norm_body, [(block, BF16)], (x_near,))
+    *own_parts, token = call(
+        pair_body, [(block, F32), (block, F32), ((1, rows), F32), TOKEN], (own,)
+    )
+    (x_near,) = call(norm_after, [(block, BF16)], (x_near, token))
     x_far = swap(x_near, "core")
     (z_near,) = call(norm_body, [(block, BF16)], (z_near,), flops=4 * 10**9)
     z_far = swap(z_near, "core")
@@ -266,7 +277,7 @@
     i_total, t_total, i_loss = call(
         own_body,
         [(block, F32), (block, F32), ((1, rows), F32)],
-        (own, mate_text, x_far, z_near, z_far, token, *mate_image),
+        (own, mate_text, x_far, z_near, z_far, token, *own_parts, *mate_image),
     )
     token, image_grad = last(0, first, image, i_total, x_1, token)
     token, text_grad = last(0, first, text, t_total, z_1, token)

time: 58 us -> 57.9 us (level)
  Pallas kernels: 16.6 us -> 18 us
  starting transfers between devices: 36.6 us -> 35.6 us
    pallas_call x12 -> x13, Pallas kernels: 16.6 us -> 18 us  [call(): pl.pallas_call(body, out_shape=[jax.ShapeDtypeStruct(s, d) for s, d in sh...]
    ppermute x10, starting transfers between devices: 36.6 us -> 35.6 us  [swap(): return lax.ppermute(value, axis, SWAP)]
  transfers between devices with their start and end apart: 10 -> 10, of which waited for: 1 -> 1; matrix products, arithmetic and copies ran while one was open for 0% -> 0% of each run, Pallas kernels for 24% -> 27%
where the time goes in v8:
time: 57.9 us; the launch traced here: 57.4 us
  starting transfers between devices  35.6 us (61%)
  Pallas kernels  18 us (31%)
  local copies, waits for them, and re-layouts  2.22 us (4%)
  between operations  1.03 us (2%)
  waiting for transfers between devices  0.66 us (1%)
    ppermute x10, starting transfers between devices, swap(): return lax.ppermute(value, axis, SWAP)  35.6 us
    pallas_call x13, Pallas kernels, call(): pl.pallas_call(body, out_shape=[jax.ShapeDtypeStruct(s, d) for s, d in sh...  18 us
    unnamed x4, local copies, waits for them, and re-layouts  2.22 us
  transfers between devices with their start and end apart: 10, of which 1 were waited for; matrix products, arithmetic and copies ran while one was open for 0% of the time, Pallas kernels for 27%

profile of v8, /device:TPU:1, one launch (start us, length us, event | category | flops | bytes accessed | tf_op | source)
XLA Modules:
  0.0 57.4 jit_solution(17876451925557359347)
XLA Ops:
  0.6 5.5 %collective-permute-start.1 = (bf16[320,1152]{1,0:T(8,128)(2,1)}, bf16[320,1152]{1,0:T(8,128)(2,1)S(1)}, u32[]{:S(2)}, u32[]{:S(2)}) collective-permute-start(bf16[320,1152]{1,0:T(8,128)(2,1)} %image.1), channel_id=1, source_target_pairs={{0,16},{16,0},{1,17},{17,1},{2,18},{18,2},{3,19},{19,3},{4,20},{20... | collective-permute-start | bytes 2211848 | tf_op jit(solution)/shard_map/ppermute | solution.py:30
  6.1 3.5 %collective-permute-start.3 = (bf16[320,1152]{1,0:T(8,128)(2,1)}, bf16[320,1152]{1,0:T(8,128)(2,1)S(1)}, u32[]{:S(2)}, u32[]{:S(2)}) collective-permute-start(bf16[320,1152]{1,0:T(8,128)(2,1)} %text.1), channel_id=1, source_target_pairs={{0,1},{1,0},{2,3},{3,2},{4,5},{5,4},{6,7},{7,6},{8,9},{9,8},{10,11... | collective-permute-start | bytes 2211848 | tf_op jit(solution)/shard_map/ppermute | solution.py:30
  9.7 1.1 %copy-done = bf16[320,1152]{1,0:T(8,128)(2,1)S(1)} copy-done((bf16[320,1152]{1,0:T(8,128)(2,1)S(1)}, bf16[320,1152]{1,0:T(8,128)(2,1)}, u32[]{:S(2)}) %copy-start) | copy-done | bytes 737304
  10.8 1.1 %copy-done.1 = bf16[320,1152]{1,0:T(8,128)(2,1)S(1)} copy-done((bf16[320,1152]{1,0:T(8,128)(2,1)S(1)}, bf16[320,1152]{1,0:T(8,128)(2,1)}, u32[]{:S(2)}) %copy-start.1) | copy-done | bytes 737304
  11.9 0.7 %shard_map.49 = (bf16[640,1152]{1,0:T(8,128)(2,1)S(1)}, bf16[320,1152]{1,0:T(8,128)(2,1)S(1)}, bf16[320,1152]{1,0:T(8,128)(2,1)S(1)}, bf16[320,1152]{1,0:T(8,128)(2,1)S(1)}, bf16[320,1152]{1,0:T(8,128)(2,1)S(1)}) custom-call(bf16[320,1152]{1,0:T(8,128)(2,1)S(1)} %copy-done, bf16[320,1152]{1,0:T(8,128)(2,1)S(1)} %copy-done.1), custom_call_target="tpu_custom_call" | custom-call | flops 1 | bytes 1 | tf_op jit(solution)/shard_map/pallas_call | solution.py:35
  12.6 3.6 %collective-permute-start = (bf16[320,1152]{1,0:T(8,128)(2,1)S(1)}, bf16[320,1152]{1,0:T(8,128)(2,1)S(1)}, u32[]{:S(2)}, u32[]{:S(2)}) collective-permute-start(bf16[320,1152]{1,0:T(8,128)(2,1)S(1)} %get-tuple-element.33), channel_id=1, source_target_pairs={{0,32},{32,0},{1,33},{33,1},{2,34},{34,2},{3,35},{35,3},{4,36},{36... | collective-permute-start | bytes 2211848 | tf_op jit(solution)/shard_map/ppermute | solution.py:30
  16.2 1.9 %collective-permute-start.5 = (bf16[320,1152]{1,0:T(8,128)(2,1)S(1)}, bf16[320,1152]{1,0:T(8,128)(2,1)S(1)}, u32[]{:S(2)}, u32[]{:S(2)}) collective-permute-start(bf16[320,1152]{1,0:T(8,128)(2,1)S(1)} %get-tuple-element.35), channel_id=1, source_target_pairs={{0,32},{32,0},{1,33},{33,1},{2,34},{34,2},{3,35},{35,3},{4,36},{36... | collective-permute-start | bytes 2211848 | tf_op jit(solution)/shard_map/ppermute | solution.py:30
  18.1 2.1 %shard_map.50 = (f32[320,1152]{1,0:T(8,128)S(1)}, f32[320,1152]{1,0:T(8,128)S(1)}, f32[1,320]{1,0:T(1,128)S(1)}, f32[8,128]{1,0:T(8,128)S(1)}) custom-call(bf16[640,1152]{1,0:T(8,128)(2,1)S(1)} %get-tuple-element.32.own), custom_call_target="tpu_custom_call" | custom-call | flops 1 | bytes 1 | tf_op jit(solution)/shard_map/pallas_call | solution.py:35
  20.4 5.5 %collective-permute-start.2 = (bf16[320,1152]{1,0:T(8,128)(2,1)S(1)}, bf16[320,1152]{1,0:T(8,128)(2,1)S(1)}, u32[]{:S(2)}, u32[]{:S(2)}) collective-permute-start(bf16[320,1152]{1,0:T(8,128)(2,1)S(1)} %shard_map.51.x_near), channel_id=1, source_target_pairs={{0,32},{32,0},{1,33},{33,1},{2,34},{34,2},{3,35},{35,3},{4,36},{36... | collective-permute-start | bytes 2211848 | tf_op jit(solution)/shard_map/ppermute | solution.py:30
  26.2 3.3 %collective-permute-start.4 = (bf16[320,1152]{1,0:T(8,128)(2,1)S(1)}, bf16[320,1152]{1,0:T(8,128)(2,1)S(1)}, u32[]{:S(2)}, u32[]{:S(2)}) collective-permute-start(bf16[320,1152]{1,0:T(8,128)(2,1)S(1)} %shard_map.52.z_near.rest_1_), channel_id=1, source_target_pairs={{0,32},{32,0},{1,33},{33,1},{2,34},{34,2},{3,35},{35,3},{4,36},{36... | collective-permute-start | bytes 2211848 | tf_op jit(solution)/shard_map/ppermute | solution.py:30
  29.5 2.0 %shard_map.53 = (bf16[192,1152]{1,0:T(8,128)(2,1)S(1)}, f32[8,128]{1,0:T(8,128)S(1)}) custom-call(bf16[640,1152]{1,0:T(8,128)(2,1)S(1)} %get-tuple-element.32.own, bf16[320,1152]{1,0:T(8,128)(2,1)S(1)} %shard_map.51.x_near, bf16[320,1152]{1,0:T(8,128)(2,1)S(1)} %collective-permute-done.2.x_far, bf16[320,1152]{1,0:T(8,128)(2,1)S(1)} %shard_map.52.z_near.rest_1_, ...), custom_call_target="tpu_custom_call" | custom-call | flops 1 | bytes 1 | tf_op jit(solution)/shard_map/pallas_call | solution.py:35
  31.5 1.5 %shard_map.54 = (bf16[192,1152]{1,0:T(8,128)(2,1)S(1)}, f32[192,1]{1,0:T(8,128)S(1)}, f32[8,128]{1,0:T(8,128)S(1)}) custom-call(bf16[320,1152]{1,0:T(8,128)(2,1)S(1)} %collective-permute-done.mate_text, bf16[320,1152]{1,0:T(8,128)(2,1)S(1)} %shard_map.51.x_near, bf16[320,1152]{1,0:T(8,128)(2,1)S(1)} %shard_map.52.z_near.rest_1_, ...), custom_call_target="tpu_custom_call" | custom-call | flops 1 | bytes 1 | tf_op jit(solution)/shard_map/pallas_call | solution.py:35
  33.0 3.6 %collective-permute-start.8 = (bf16[192,1152]{1,0:T(8,128)(2,1)S(1)}, bf16[192,1152]{1,0:T(8,128)(2,1)S(1)}, u32[]{:S(2)}, u32[]{:S(2)}) collective-permute-start(bf16[192,1152]{1,0:T(8,128)(2,1)S(1)} %get-tuple-element.50), channel_id=1, source_target_pairs={{0,16},{16,0},{1,17},{17,1},{2,18},{18,2},{3,19},{19,3},{4,20},{20... | collective-permute-start | bytes 1327112 | tf_op jit(solution)/shard_map/ppermute | solution.py:30
  36.7 3.5 %collective-permute-start.7 = (bf16[192,1152]{1,0:T(8,128)(2,1)S(1)}, bf16[192,1152]{1,0:T(8,128)(2,1)S(1)}, u32[]{:S(2)}, u32[]{:S(2)}) collective-permute-start(bf16[192,1152]{1,0:T(8,128)(2,1)S(1)} %get-tuple-element.49), channel_id=1, source_target_pairs={{0,1},{1,0},{2,3},{3,2},{4,5},{5,4},{6,7},{7,6},{8,9},{9,8},{10,11... | collective-permute-start | bytes 1327112 | tf_op jit(solution)/shard_map/ppermute | solution.py:30
  40.2 1.3 %shard_map.55 = (bf16[144,1152]{1,0:T(8,128)(2,1)S(1)}, f32[8,128]{1,0:T(8,128)S(1)}) custom-call(bf16[320,1152]{1,0:T(8,128)(2,1)S(1)} %collective-permute-done.mate_text, bf16[320,1152]{1,0:T(8,128)(2,1)S(1)} %shard_map.51.x_near, bf16[320,1152]{1,0:T(8,128)(2,1)S(1)} %shard_map.52.z_near.rest_1_, bf16[320,1152]{1,0:T(8,128)(2,1)S(1)} %collective-permute-done.4.z_far, ...), custom_call_target="tpu_custom_call" | custom-call | flops 1 | bytes 1 | tf_op jit(solution)/shard_map/pallas_call | solution.py:35
  41.5 3.0 %collective-permute-start.6 = (bf16[144,1152]{1,0:T(8,128)(2,1)S(1)}, bf16[144,1152]{1,0:T(8,128)(2,1)S(1)}, u32[]{:S(2)}, u32[]{:S(2)}) collective-permute-start(bf16[144,1152]{1,0:T(8,128)(2,1)S(1)} %get-tuple-element.45), channel_id=1, source_target_pairs={{0,16},{16,0},{1,17},{17,1},{2,18},{18,2},{3,19},{19,3},{4,20},{20... | collective-permute-start | bytes 995336 | tf_op jit(solution)/shard_map/ppermute | solution.py:30
  44.5 1.8 %shard_map.56 = (bf16[128,1152]{1,0:T(8,128)(2,1)S(1)}, f32[8,128]{1,0:T(8,128)S(1)}) custom-call(bf16[640,1152]{1,0:T(8,128)(2,1)S(1)} %get-tuple-element.32.own, bf16[320,1152]{1,0:T(8,128)(2,1)S(1)} %shard_map.51.x_near, bf16[320,1152]{1,0:T(8,128)(2,1)S(1)} %collective-permute-done.2.x_far, bf16[320,1152]{1,0:T(8,128)(2,1)S(1)} %shard_map.52.z_near.rest_1_, ...), custom_call_target="tpu_custom_call" | custom-call | flops 1 | bytes 1 | tf_op jit(solution)/shard_map/pallas_call | solution.py:35
  46.3 2.1 %collective-permute-start.9 = (bf16[128,1152]{1,0:T(8,128)(2,1)S(1)}, bf16[128,1152]{1,0:T(8,128)(2,1)S(1)}, u32[]{:S(2)}, u32[]{:S(2)}) collective-permute-start(bf16[128,1152]{1,0:T(8,128)(2,1)S(1)} %get-tuple-element.56), channel_id=1, source_target_pairs={{0,1},{1,0},{2,3},{3,2},{4,5},{5,4},{6,7},{7,6},{8,9},{9,8},{10,11... | collective-permute-start | bytes 884744 | tf_op jit(solution)/shard_map/ppermute | solution.py:30
  48.4 3.6 %shard_map.57 = (f32[320,1152]{1,0:T(8,128)S(1)}, f32[320,1152]{1,0:T(8,128)S(1)}, f32[1,320]{1,0:T(1,128)S(1)}) custom-call(bf16[640,1152]{1,0:T(8,128)(2,1)S(1)} %get-tuple-element.32.own, bf16[320,1152]{1,0:T(8,128)(2,1)S(1)} %collective-permute-done.mate_text, bf16[320,1152]{1,0:T(8,128)(2,1)S(1)} %collective-permute-done.2.x_far, ...), custom_call_target="tpu_custom_call" | custom-call | flops 1 | bytes 1 | tf_op jit(solution)/shard_map/pallas_call | solution.py:35
  52.0 1.2 %shard_map.58 = (f32[8,128]{1,0:T(8,128)S(1)}, f32[320,1152]{1,0:T(8,128)}) custom-call(bf16[320,1152]{1,0:T(8,128)(2,1)S(1)} %get-tuple-element.31.raw, f32[320,1152]{1,0:T(8,128)S(1)} %get-tuple-element.44.total, bf16[192,1152]{1,0:T(8,128)(2,1)S(1)} %collective-permute-done.8.back, f32[8,128]{1,0:T(8,128)S(1)} %get-tuple-element.40._.rest_0_), custom_call_target="tpu_custom_call" | custom-call | flops 1 | bytes 1 | tf_op jit(solution)/shard_map/pallas_call | solution.py:35
  53.3 1.2 %shard_map.59 = (f32[8,128]{1,0:T(8,128)S(1)}, f32[320,1152]{1,0:T(8,128)}) custom-call(bf16[320,1152]{1,0:T(8,128)(2,1)S(1)} %get-tuple-element.47.raw, f32[320,1152]{1,0:T(8,128)S(1)} %get-tuple-element.48.total, bf16[192,1152]{1,0:T(8,128)(2,1)S(1)} %collective-permute-done.7.back, f32[8,128]{1,0:T(8,128)S(1)} %get-tuple-element.51.rest_0_), custom_call_target="tpu_custom_call" | custom-call | flops 1 | bytes 1 | tf_op jit(solution)/shard_map/pallas_call | solution.py:35
  54.5 0.6 %collective-permute-done.6.back = bf16[144,1152]{1,0:T(8,128)(2,1)S(1)} collective-permute-done((bf16[144,1152]{1,0:T(8,128)(2,1)S(1)}, bf16[144,1152]{1,0:T(8,128)(2,1)S(1)}, u32[]{:S(2)}, u32[]{:S(2)}) %collective-permute-start.6) | collective-permute-done | bytes 331808 | tf_op jit(solution)/shard_map/ppermute | solution.py:30
  55.1 1.1 %shard_map.60 = (f32[320]{0:T(512)}, f32[8,128]{1,0:T(8,128)S(1)}, f32[320,1152]{1,0:T(8,128)}) custom-call(bf16[320,1152]{1,0:T(8,128)(2,1)S(1)} %get-tuple-element.31.raw, f32[320,1152]{1,0:T(8,128)S(1)} %get-tuple-element.44.total, bf16[144,1152]{1,0:T(8,128)(2,1)S(1)} %collective-permute-done.6.back, ...), custom_call_target="tpu_custom_call", output_to_operand_aliasing={{2}: (5, {})} | custom-call | flops 1 | bytes 1 | tf_op jit(solution)/shard_map/pallas_call | solution.py:35
  56.2 1.1 %shard_map.61 = f32[320,1152]{1,0:T(8,128)} custom-call(bf16[320,1152]{1,0:T(8,128)(2,1)S(1)} %get-tuple-element.47.raw, f32[320,1152]{1,0:T(8,128)S(1)} %get-tuple-element.48.total, bf16[128,1152]{1,0:T(8,128)(2,1)S(1)} %collective-permute-done.9.back, f32[8,128]{1,0:T(8,128)S(1)} %get-tuple-element.57.rest_0_, ...), custom_call_target="tpu_custom_call", output_to_operand_aliasing={{}: (4, {})} | custom-call | flops 1 | bytes 1 | tf_op jit(solution)/shard_map/pallas_call | solution.py:35
  (13 shorter events, 0.5 us)
Async XLA Ops:
  0.6 19.6 %collective-permute-start.1 = (bf16[320,1152]{1,0:T(8,128)(2,1)}, bf16[320,1152]{1,0:T(8,128)(2,1)S(1)}, u32[]{:S(2)}, u32[]{:S(2)}) collective-permute-start(bf16[320,1152]{1,0:T(8,128)(2,1)} %image.1), channel_id=1, source_target_pairs={{0,16},{16,0},{1,17},{17,1},{2,18},{18,2},{3,19},{19,3},{4,20},{20... | collective-permute-start | bytes 2211848 | tf_op jit(solution)/shard_map/ppermute | solution.py:30
  6.1 19.8 %collective-permute-start.3 = (bf16[320,1152]{1,0:T(8,128)(2,1)}, bf16[320,1152]{1,0:T(8,128)(2,1)S(1)}, u32[]{:S(2)}, u32[]{:S(2)}) collective-permute-start(bf16[320,1152]{1,0:T(8,128)(2,1)} %text.1), channel_id=1, source_target_pairs={{0,1},{1,0},{2,3},{3,2},{4,5},{5,4},{6,7},{7,6},{8,9},{9,8},{10,11... | collective-permute-start | bytes 2211848 | tf_op jit(solution)/shard_map/ppermute | solution.py:30
  9.7 1.1 %copy-start = (bf16[320,1152]{1,0:T(8,128)(2,1)S(1)}, bf16[320,1152]{1,0:T(8,128)(2,1)}, u32[]{:S(2)}) copy-start(bf16[320,1152]{1,0:T(8,128)(2,1)} %image.1) | copy-start | bytes 2211844
  10.8 1.1 %copy-start.1 = (bf16[320,1152]{1,0:T(8,128)(2,1)S(1)}, bf16[320,1152]{1,0:T(8,128)(2,1)}, u32[]{:S(2)}) copy-start(bf16[320,1152]{1,0:T(8,128)(2,1)} %text.1) | copy-start | bytes 2211844
  12.6 18.9 %collective-permute-start = (bf16[320,1152]{1,0:T(8,128)(2,1)S(1)}, bf16[320,1152]{1,0:T(8,128)(2,1)S(1)}, u32[]{:S(2)}, u32[]{:S(2)}) collective-permute-start(bf16[320,1152]{1,0:T(8,128)(2,1)S(1)} %get-tuple-element.33), channel_id=1, source_target_pairs={{0,32},{32,0},{1,33},{33,1},{2,34},{34,2},{3,35},{35,3},{4,36},{36... | collective-permute-start | bytes 2211848 | tf_op jit(solution)/shard_map/ppermute | solution.py:30
  16.2 13.3 %collective-permute-start.5 = (bf16[320,1152]{1,0:T(8,128)(2,1)S(1)}, bf16[320,1152]{1,0:T(8,128)(2,1)S(1)}, u32[]{:S(2)}, u32[]{:S(2)}) collective-permute-start(bf16[320,1152]{1,0:T(8,128)(2,1)S(1)} %get-tuple-element.35), channel_id=1, source_target_pairs={{0,32},{32,0},{1,33},{33,1},{2,34},{34,2},{3,35},{35,3},{4,36},{36... | collective-permute-start | bytes 2211848 | tf_op jit(solution)/shard_map/ppermute | solution.py:30
  20.4 9.0 %collective-permute-start.2 = (bf16[320,1152]{1,0:T(8,128)(2,1)S(1)}, bf16[320,1152]{1,0:T(8,128)(2,1)S(1)}, u32[]{:S(2)}, u32[]{:S(2)}) collective-permute-start(bf16[320,1152]{1,0:T(8,128)(2,1)S(1)} %shard_map.51.x_near), channel_id=1, source_target_pairs={{0,32},{32,0},{1,33},{33,1},{2,34},{34,2},{3,35},{35,3},{4,36},{36... | collective-permute-start | bytes 2211848 | tf_op jit(solution)/shard_map/ppermute | solution.py:30
  26.2 5.3 %collective-permute-start.4 = (bf16[320,1152]{1,0:T(8,128)(2,1)S(1)}, bf16[320,1152]{1,0:T(8,128)(2,1)S(1)}, u32[]{:S(2)}, u32[]{:S(2)}) collective-permute-start(bf16[320,1152]{1,0:T(8,128)(2,1)S(1)} %shard_map.52.z_near.rest_1_), channel_id=1, source_target_pairs={{0,32},{32,0},{1,33},{33,1},{2,34},{34,2},{3,35},{35,3},{4,36},{36... | collective-permute-start | bytes 2211848 | tf_op jit(solution)/shard_map/ppermute | solution.py:30
  33.0 19.0 %collective-permute-start.8 = (bf16[192,1152]{1,0:T(8,128)(2,1)S(1)}, bf16[192,1152]{1,0:T(8,128)(2,1)S(1)}, u32[]{:S(2)}, u32[]{:S(2)}) collective-permute-start(bf16[192,1152]{1,0:T(8,128)(2,1)S(1)} %get-tuple-element.50), channel_id=1, source_target_pairs={{0,16},{16,0},{1,17},{17,1},{2,18},{18,2},{3,19},{19,3},{4,20},{20... | collective-permute-start | bytes 1327112 | tf_op jit(solution)/shard_map/ppermute | solution.py:30
  36.7 16.6 %collective-permute-start.7 = (bf16[192,1152]{1,0:T(8,128)(2,1)S(1)}, bf16[192,1152]{1,0:T(8,128)(2,1)S(1)}, u32[]{:S(2)}, u32[]{:S(2)}) collective-permute-start(bf16[192,1152]{1,0:T(8,128)(2,1)S(1)} %get-tuple-element.49), channel_id=1, source_target_pairs={{0,1},{1,0},{2,3},{3,2},{4,5},{5,4},{6,7},{7,6},{8,9},{9,8},{10,11... | collective-permute-start | bytes 1327112 | tf_op jit(solution)/shard_map/ppermute | solution.py:30
  41.5 13.6 %collective-permute-start.6 = (bf16[144,1152]{1,0:T(8,128)(2,1)S(1)}, bf16[144,1152]{1,0:T(8,128)(2,1)S(1)}, u32[]{:S(2)}, u32[]{:S(2)}) collective-permute-start(bf16[144,1152]{1,0:T(8,128)(2,1)S(1)} %get-tuple-element.45), channel_id=1, source_target_pairs={{0,16},{16,0},{1,17},{17,1},{2,18},{18,2},{3,19},{19,3},{4,20},{20... | collective-permute-start | bytes 995336 | tf_op jit(solution)/shard_map/ppermute | solution.py:30
  46.3 9.9 %collective-permute-start.9 = (bf16[128,1152]{1,0:T(8,128)(2,1)S(1)}, bf16[128,1152]{1,0:T(8,128)(2,1)S(1)}, u32[]{:S(2)}, u32[]{:S(2)}) collective-permute-start(bf16[128,1152]{1,0:T(8,128)(2,1)S(1)} %get-tuple-element.56), channel_id=1, source_target_pairs={{0,1},{1,0},{2,3},{3,2},{4,5},{5,4},{6,7},{7,6},{8,9},{9,8},{10,11... | collective-permute-start | bytes 884744 | tf_op jit(solution)/shard_map/ppermute | solution.py:30

commit v9 on v8

--- a/solution.py
+++ b/solution.py
@@ -21,7 +21,7 @@
 F32, BF16 = jnp.float32, jnp.bfloat16
 MIB = 1024 * 1024
 TOKEN = ((8, LANES), F32)
-FIRST = 192
+FIRST = 224
 PACK = 16
 PIECES = 1
 

time: 57.9 us -> 58 us (level)
  transfers between devices with their start and end apart: 10 -> 10, of which waited for: 1 -> 2; matrix products, arithmetic and copies ran while one was open for 0% -> 0% of each run, Pallas kernels for 27% -> 27%
where the time goes in v9:
time: 58 us; the launch traced here: 57.5 us
  starting transfers between devices  35.6 us (61%)
  Pallas kernels  18 us (31%)
  local copies, waits for them, and re-layouts  2.22 us (4%)
  between operations  1.02 us (2%)
  waiting for transfers between devices  0.74 us (1%)
    ppermute x10, starting transfers between devices, swap(): return lax.ppermute(value, axis, SWAP)  35.6 us
    pallas_call x13, Pallas kernels, call(): pl.pallas_call(body, out_shape=[jax.ShapeDtypeStruct(s, d) for s, d in sh...  18 us
    unnamed x4, local copies, waits for them, and re-layouts  2.22 us
  transfers between devices with their start and end apart: 10, of which 2 were waited for; matrix products, arithmetic and copies ran while one was open for 0% of the time, Pallas kernels for 27%

profile of v9, /device:TPU:1, one launch (start us, length us, event | category | flops | bytes accessed | tf_op | source)
XLA Modules:
  0.0 57.5 jit_solution(5031983868580540251)
XLA Ops:
  0.6 5.5 %collective-permute-start.1 = (bf16[320,1152]{1,0:T(8,128)(2,1)}, bf16[320,1152]{1,0:T(8,128)(2,1)S(1)}, u32[]{:S(2)}, u32[]{:S(2)}) collective-permute-start(bf16[320,1152]{1,0:T(8,128)(2,1)} %image.1), channel_id=1, source_target_pairs={{0,16},{16,0},{1,17},{17,1},{2,18},{18,2},{3,19},{19,3},{4,20},{20... | collective-permute-start | bytes 2211848 | tf_op jit(solution)/shard_map/ppermute | solution.py:30
  6.1 3.5 %collective-permute-start.3 = (bf16[320,1152]{1,0:T(8,128)(2,1)}, bf16[320,1152]{1,0:T(8,128)(2,1)S(1)}, u32[]{:S(2)}, u32[]{:S(2)}) collective-permute-start(bf16[320,1152]{1,0:T(8,128)(2,1)} %text.1), channel_id=1, source_target_pairs={{0,1},{1,0},{2,3},{3,2},{4,5},{5,4},{6,7},{7,6},{8,9},{9,8},{10,11... | collective-permute-start | bytes 2211848 | tf_op jit(solution)/shard_map/ppermute | solution.py:30
  9.7 1.1 %copy-done = bf16[320,1152]{1,0:T(8,128)(2,1)S(1)} copy-done((bf16[320,1152]{1,0:T(8,128)(2,1)S(1)}, bf16[320,1152]{1,0:T(8,128)(2,1)}, u32[]{:S(2)}) %copy-start) | copy-done | bytes 737304
  10.8 1.1 %copy-done.1 = bf16[320,1152]{1,0:T(8,128)(2,1)S(1)} copy-done((bf16[320,1152]{1,0:T(8,128)(2,1)S(1)}, bf16[320,1152]{1,0:T(8,128)(2,1)}, u32[]{:S(2)}) %copy-start.1) | copy-done | bytes 737304
  11.9 0.7 %shard_map.49 = (bf16[640,1152]{1,0:T(8,128)(2,1)S(1)}, bf16[320,1152]{1,0:T(8,128)(2,1)S(1)}, bf16[320,1152]{1,0:T(8,128)(2,1)S(1)}, bf16[320,1152]{1,0:T(8,128)(2,1)S(1)}, bf16[320,1152]{1,0:T(8,128)(2,1)S(1)}) custom-call(bf16[320,1152]{1,0:T(8,128)(2,1)S(1)} %copy-done, bf16[320,1152]{1,0:T(8,128)(2,1)S(1)} %copy-done.1), custom_call_target="tpu_custom_call" | custom-call | flops 1 | bytes 1 | tf_op jit(solution)/shard_map/pallas_call | solution.py:35
  12.6 3.6 %collective-permute-start = (bf16[320,1152]{1,0:T(8,128)(2,1)S(1)}, bf16[320,1152]{1,0:T(8,128)(2,1)S(1)}, u32[]{:S(2)}, u32[]{:S(2)}) collective-permute-start(bf16[320,1152]{1,0:T(8,128)(2,1)S(1)} %get-tuple-element.33), channel_id=1, source_target_pairs={{0,32},{32,0},{1,33},{33,1},{2,34},{34,2},{3,35},{35,3},{4,36},{36... | collective-permute-start | bytes 2211848 | tf_op jit(solution)/shard_map/ppermute | solution.py:30
  16.2 1.9 %collective-permute-start.5 = (bf16[320,1152]{1,0:T(8,128)(2,1)S(1)}, bf16[320,1152]{1,0:T(8,128)(2,1)S(1)}, u32[]{:S(2)}, u32[]{:S(2)}) collective-permute-start(bf16[320,1152]{1,0:T(8,128)(2,1)S(1)} %get-tuple-element.35), channel_id=1, source_target_pairs={{0,32},{32,0},{1,33},{33,1},{2,34},{34,2},{3,35},{35,3},{4,36},{36... | collective-permute-start | bytes 2211848 | tf_op jit(solution)/shard_map/ppermute | solution.py:30
  18.1 2.1 %shard_map.50 = (f32[320,1152]{1,0:T(8,128)S(1)}, f32[320,1152]{1,0:T(8,128)S(1)}, f32[1,320]{1,0:T(1,128)S(1)}, f32[8,128]{1,0:T(8,128)S(1)}) custom-call(bf16[640,1152]{1,0:T(8,128)(2,1)S(1)} %get-tuple-element.32.own), custom_call_target="tpu_custom_call" | custom-call | flops 1 | bytes 1 | tf_op jit(solution)/shard_map/pallas_call | solution.py:35
  20.4 5.5 %collective-permute-start.2 = (bf16[320,1152]{1,0:T(8,128)(2,1)S(1)}, bf16[320,1152]{1,0:T(8,128)(2,1)S(1)}, u32[]{:S(2)}, u32[]{:S(2)}) collective-permute-start(bf16[320,1152]{1,0:T(8,128)(2,1)S(1)} %shard_map.51.x_near), channel_id=1, source_target_pairs={{0,32},{32,0},{1,33},{33,1},{2,34},{34,2},{3,35},{35,3},{4,36},{36... | collective-permute-start | bytes 2211848 | tf_op jit(solution)/shard_map/ppermute | solution.py:30
  26.2 3.3 %collective-permute-start.4 = (bf16[320,1152]{1,0:T(8,128)(2,1)S(1)}, bf16[320,1152]{1,0:T(8,128)(2,1)S(1)}, u32[]{:S(2)}, u32[]{:S(2)}) collective-permute-start(bf16[320,1152]{1,0:T(8,128)(2,1)S(1)} %shard_map.52.z_near.rest_1_), channel_id=1, source_target_pairs={{0,32},{32,0},{1,33},{33,1},{2,34},{34,2},{3,35},{35,3},{4,36},{36... | collective-permute-start | bytes 2211848 | tf_op jit(solution)/shard_map/ppermute | solution.py:30
  29.5 2.0 %shard_map.53 = (bf16[224,1152]{1,0:T(8,128)(2,1)S(1)}, f32[8,128]{1,0:T(8,128)S(1)}) custom-call(bf16[640,1152]{1,0:T(8,128)(2,1)S(1)} %get-tuple-element.32.own, bf16[320,1152]{1,0:T(8,128)(2,1)S(1)} %shard_map.51.x_near, bf16[320,1152]{1,0:T(8,128)(2,1)S(1)} %collective-permute-done.2.x_far, bf16[320,1152]{1,0:T(8,128)(2,1)S(1)} %shard_map.52.z_near.rest_1_, ...), custom_call_target="tpu_custom_call" | custom-call | flops 1 | bytes 1 | tf_op jit(solution)/shard_map/pallas_call | solution.py:35
  31.5 1.6 %shard_map.54 = (bf16[224,1152]{1,0:T(8,128)(2,1)S(1)}, f32[224,1]{1,0:T(8,128)S(1)}, f32[8,128]{1,0:T(8,128)S(1)}) custom-call(bf16[320,1152]{1,0:T(8,128)(2,1)S(1)} %collective-permute-done.mate_text, bf16[320,1152]{1,0:T(8,128)(2,1)S(1)} %shard_map.51.x_near, bf16[320,1152]{1,0:T(8,128)(2,1)S(1)} %shard_map.52.z_near.rest_1_, ...), custom_call_target="tpu_custom_call" | custom-call | flops 1 | bytes 1 | tf_op jit(solution)/shard_map/pallas_call | solution.py:35
  33.1 3.6 %collective-permute-start.8 = (bf16[224,1152]{1,0:T(8,128)(2,1)S(1)}, bf16[224,1152]{1,0:T(8,128)(2,1)S(1)}, u32[]{:S(2)}, u32[]{:S(2)}) collective-permute-start(bf16[224,1152]{1,0:T(8,128)(2,1)S(1)} %get-tuple-element.50), channel_id=1, source_target_pairs={{0,16},{16,0},{1,17},{17,1},{2,18},{18,2},{3,19},{19,3},{4,20},{20... | collective-permute-start | bytes 1548296 | tf_op jit(solution)/shard_map/ppermute | solution.py:30
  36.7 3.5 %collective-permute-start.7 = (bf16[224,1152]{1,0:T(8,128)(2,1)S(1)}, bf16[224,1152]{1,0:T(8,128)(2,1)S(1)}, u32[]{:S(2)}, u32[]{:S(2)}) collective-permute-start(bf16[224,1152]{1,0:T(8,128)(2,1)S(1)} %get-tuple-element.49), channel_id=1, source_target_pairs={{0,1},{1,0},{2,3},{3,2},{4,5},{5,4},{6,7},{7,6},{8,9},{9,8},{10,11... | collective-permute-start | bytes 1548296 | tf_op jit(solution)/shard_map/ppermute | solution.py:30
  40.3 1.3 %shard_map.55 = (bf16[112,1152]{1,0:T(8,128)(2,1)S(1)}, f32[8,128]{1,0:T(8,128)S(1)}) custom-call(bf16[320,1152]{1,0:T(8,128)(2,1)S(1)} %collective-permute-done.mate_text, bf16[320,1152]{1,0:T(8,128)(2,1)S(1)} %shard_map.51.x_near, bf16[320,1152]{1,0:T(8,128)(2,1)S(1)} %shard_map.52.z_near.rest_1_, bf16[320,1152]{1,0:T(8,128)(2,1)S(1)} %collective-permute-done.4.z_far, ...), custom_call_target="tpu_custom_call" | custom-call | flops 1 | bytes 1 | tf_op jit(solution)/shard_map/pallas_call | solution.py:35
  41.6 3.0 %collective-permute-start.6 = (bf16[112,1152]{1,0:T(8,128)(2,1)S(1)}, bf16[112,1152]{1,0:T(8,128)(2,1)S(1)}, u32[]{:S(2)}, u32[]{:S(2)}) collective-permute-start(bf16[112,1152]{1,0:T(8,128)(2,1)S(1)} %get-tuple-element.45), channel_id=1, source_target_pairs={{0,16},{16,0},{1,17},{17,1},{2,18},{18,2},{3,19},{19,3},{4,20},{20... | collective-permute-start | bytes 774152 | tf_op jit(solution)/shard_map/ppermute | solution.py:30
  44.6 1.7 %shard_map.56 = (bf16[96,1152]{1,0:T(8,128)(2,1)S(1)}, f32[8,128]{1,0:T(8,128)S(1)}) custom-call(bf16[640,1152]{1,0:T(8,128)(2,1)S(1)} %get-tuple-element.32.own, bf16[320,1152]{1,0:T(8,128)(2,1)S(1)} %shard_map.51.x_near, bf16[320,1152]{1,0:T(8,128)(2,1)S(1)} %collective-permute-done.2.x_far, bf16[320,1152]{1,0:T(8,128)(2,1)S(1)} %shard_map.52.z_near.rest_1_, ...), custom_call_target="tpu_custom_call" | custom-call | flops 1 | bytes 1 | tf_op jit(solution)/shard_map/pallas_call | solution.py:35
  46.3 2.1 %collective-permute-start.9 = (bf16[96,1152]{1,0:T(8,128)(2,1)S(1)}, bf16[96,1152]{1,0:T(8,128)(2,1)S(1)}, u32[]{:S(2)}, u32[]{:S(2)}) collective-permute-start(bf16[96,1152]{1,0:T(8,128)(2,1)S(1)} %get-tuple-element.56), channel_id=1, source_target_pairs={{0,1},{1,0},{2,3},{3,2},{4,5},{5,4},{6,7},{7,6},{8,9},{9,8},{10,11... | collective-permute-start | bytes 663560 | tf_op jit(solution)/shard_map/ppermute | solution.py:30
  48.4 3.6 %shard_map.57 = (f32[320,1152]{1,0:T(8,128)S(1)}, f32[320,1152]{1,0:T(8,128)S(1)}, f32[1,320]{1,0:T(1,128)S(1)}) custom-call(bf16[640,1152]{1,0:T(8,128)(2,1)S(1)} %get-tuple-element.32.own, bf16[320,1152]{1,0:T(8,128)(2,1)S(1)} %collective-permute-done.mate_text, bf16[320,1152]{1,0:T(8,128)(2,1)S(1)} %collective-permute-done.2.x_far, ...), custom_call_target="tpu_custom_call" | custom-call | flops 1 | bytes 1 | tf_op jit(solution)/shard_map/pallas_call | solution.py:35
  52.0 1.3 %shard_map.58 = (f32[8,128]{1,0:T(8,128)S(1)}, f32[320,1152]{1,0:T(8,128)}) custom-call(bf16[320,1152]{1,0:T(8,128)(2,1)S(1)} %get-tuple-element.31.raw, f32[320,1152]{1,0:T(8,128)S(1)} %get-tuple-element.44.total, bf16[224,1152]{1,0:T(8,128)(2,1)S(1)} %collective-permute-done.8.back, f32[8,128]{1,0:T(8,128)S(1)} %get-tuple-element.40._.rest_0_), custom_call_target="tpu_custom_call" | custom-call | flops 1 | bytes 1 | tf_op jit(solution)/shard_map/pallas_call | solution.py:35
  53.3 1.3 %shard_map.59 = (f32[8,128]{1,0:T(8,128)S(1)}, f32[320,1152]{1,0:T(8,128)}) custom-call(bf16[320,1152]{1,0:T(8,128)(2,1)S(1)} %get-tuple-element.47.raw, f32[320,1152]{1,0:T(8,128)S(1)} %get-tuple-element.48.total, bf16[224,1152]{1,0:T(8,128)(2,1)S(1)} %collective-permute-done.7.back, f32[8,128]{1,0:T(8,128)S(1)} %get-tuple-element.51.rest_0_), custom_call_target="tpu_custom_call" | custom-call | flops 1 | bytes 1 | tf_op jit(solution)/shard_map/pallas_call | solution.py:35
  54.7 0.6 %collective-permute-done.6.back = bf16[112,1152]{1,0:T(8,128)(2,1)S(1)} collective-permute-done((bf16[112,1152]{1,0:T(8,128)(2,1)S(1)}, bf16[112,1152]{1,0:T(8,128)(2,1)S(1)}, u32[]{:S(2)}, u32[]{:S(2)}) %collective-permute-start.6) | collective-permute-done | bytes 258080 | tf_op jit(solution)/shard_map/ppermute | solution.py:30
  55.3 1.0 %shard_map.60 = (f32[320]{0:T(512)}, f32[8,128]{1,0:T(8,128)S(1)}, f32[320,1152]{1,0:T(8,128)}) custom-call(bf16[320,1152]{1,0:T(8,128)(2,1)S(1)} %get-tuple-element.31.raw, f32[320,1152]{1,0:T(8,128)S(1)} %get-tuple-element.44.total, bf16[112,1152]{1,0:T(8,128)(2,1)S(1)} %collective-permute-done.6.back, ...), custom_call_target="tpu_custom_call", output_to_operand_aliasing={{2}: (5, {})} | custom-call | flops 1 | bytes 1 | tf_op jit(solution)/shard_map/pallas_call | solution.py:35
  56.4 1.0 %shard_map.61 = f32[320,1152]{1,0:T(8,128)} custom-call(bf16[320,1152]{1,0:T(8,128)(2,1)S(1)} %get-tuple-element.47.raw, f32[320,1152]{1,0:T(8,128)S(1)} %get-tuple-element.48.total, bf16[96,1152]{1,0:T(8,128)(2,1)S(1)} %collective-permute-done.9.back, f32[8,128]{1,0:T(8,128)S(1)} %get-tuple-element.57.rest_0_, ...), custom_call_target="tpu_custom_call", output_to_operand_aliasing={{}: (4, {})} | custom-call | flops 1 | bytes 1 | tf_op jit(solution)/shard_map/pallas_call | solution.py:35
  (13 shorter events, 0.6 us)
Async XLA Ops:
  0.6 19.6 %collective-permute-start.1 = (bf16[320,1152]{1,0:T(8,128)(2,1)}, bf16[320,1152]{1,0:T(8,128)(2,1)S(1)}, u32[]{:S(2)}, u32[]{:S(2)}) collective-permute-start(bf16[320,1152]{1,0:T(8,128)(2,1)} %image.1), channel_id=1, source_target_pairs={{0,16},{16,0},{1,17},{17,1},{2,18},{18,2},{3,19},{19,3},{4,20},{20... | collective-permute-start | bytes 2211848 | tf_op jit(solution)/shard_map/ppermute | solution.py:30
  6.1 19.8 %collective-permute-start.3 = (bf16[320,1152]{1,0:T(8,128)(2,1)}, bf16[320,1152]{1,0:T(8,128)(2,1)S(1)}, u32[]{:S(2)}, u32[]{:S(2)}) collective-permute-start(bf16[320,1152]{1,0:T(8,128)(2,1)} %text.1), channel_id=1, source_target_pairs={{0,1},{1,0},{2,3},{3,2},{4,5},{5,4},{6,7},{7,6},{8,9},{9,8},{10,11... | collective-permute-start | bytes 2211848 | tf_op jit(solution)/shard_map/ppermute | solution.py:30
  9.7 1.1 %copy-start = (bf16[320,1152]{1,0:T(8,128)(2,1)S(1)}, bf16[320,1152]{1,0:T(8,128)(2,1)}, u32[]{:S(2)}) copy-start(bf16[320,1152]{1,0:T(8,128)(2,1)} %image.1) | copy-start | bytes 2211844
  10.8 1.1 %copy-start.1 = (bf16[320,1152]{1,0:T(8,128)(2,1)S(1)}, bf16[320,1152]{1,0:T(8,128)(2,1)}, u32[]{:S(2)}) copy-start(bf16[320,1152]{1,0:T(8,128)(2,1)} %text.1) | copy-start | bytes 2211844
  12.6 18.9 %collective-permute-start = (bf16[320,1152]{1,0:T(8,128)(2,1)S(1)}, bf16[320,1152]{1,0:T(8,128)(2,1)S(1)}, u32[]{:S(2)}, u32[]{:S(2)}) collective-permute-start(bf16[320,1152]{1,0:T(8,128)(2,1)S(1)} %get-tuple-element.33), channel_id=1, source_target_pairs={{0,32},{32,0},{1,33},{33,1},{2,34},{34,2},{3,35},{35,3},{4,36},{36... | collective-permute-start | bytes 2211848 | tf_op jit(solution)/shard_map/ppermute | solution.py:30
  16.2 13.3 %collective-permute-start.5 = (bf16[320,1152]{1,0:T(8,128)(2,1)S(1)}, bf16[320,1152]{1,0:T(8,128)(2,1)S(1)}, u32[]{:S(2)}, u32[]{:S(2)}) collective-permute-start(bf16[320,1152]{1,0:T(8,128)(2,1)S(1)} %get-tuple-element.35), channel_id=1, source_target_pairs={{0,32},{32,0},{1,33},{33,1},{2,34},{34,2},{3,35},{35,3},{4,36},{36... | collective-permute-start | bytes 2211848 | tf_op jit(solution)/shard_map/ppermute | solution.py:30
  20.4 9.0 %collective-permute-start.2 = (bf16[320,1152]{1,0:T(8,128)(2,1)S(1)}, bf16[320,1152]{1,0:T(8,128)(2,1)S(1)}, u32[]{:S(2)}, u32[]{:S(2)}) collective-permute-start(bf16[320,1152]{1,0:T(8,128)(2,1)S(1)} %shard_map.51.x_near), channel_id=1, source_target_pairs={{0,32},{32,0},{1,33},{33,1},{2,34},{34,2},{3,35},{35,3},{4,36},{36... | collective-permute-start | bytes 2211848 | tf_op jit(solution)/shard_map/ppermute | solution.py:30
  26.2 5.4 %collective-permute-start.4 = (bf16[320,1152]{1,0:T(8,128)(2,1)S(1)}, bf16[320,1152]{1,0:T(8,128)(2,1)S(1)}, u32[]{:S(2)}, u32[]{:S(2)}) collective-permute-start(bf16[320,1152]{1,0:T(8,128)(2,1)S(1)} %shard_map.52.z_near.rest_1_), channel_id=1, source_target_pairs={{0,32},{32,0},{1,33},{33,1},{2,34},{34,2},{3,35},{35,3},{4,36},{36... | collective-permute-start | bytes 2211848 | tf_op jit(solution)/shard_map/ppermute | solution.py:30
  33.1 18.9 %collective-permute-start.8 = (bf16[224,1152]{1,0:T(8,128)(2,1)S(1)}, bf16[224,1152]{1,0:T(8,128)(2,1)S(1)}, u32[]{:S(2)}, u32[]{:S(2)}) collective-permute-start(bf16[224,1152]{1,0:T(8,128)(2,1)S(1)} %get-tuple-element.50), channel_id=1, source_target_pairs={{0,16},{16,0},{1,17},{17,1},{2,18},{18,2},{3,19},{19,3},{4,20},{20... | collective-permute-start | bytes 1548296 | tf_op jit(solution)/shard_map/ppermute | solution.py:30
  36.7 16.6 %collective-permute-start.7 = (bf16[224,1152]{1,0:T(8,128)(2,1)S(1)}, bf16[224,1152]{1,0:T(8,128)(2,1)S(1)}, u32[]{:S(2)}, u32[]{:S(2)}) collective-permute-start(bf16[224,1152]{1,0:T(8,128)(2,1)S(1)} %get-tuple-element.49), channel_id=1, source_target_pairs={{0,1},{1,0},{2,3},{3,2},{4,5},{5,4},{6,7},{7,6},{8,9},{9,8},{10,11... | collective-permute-start | bytes 1548296 | tf_op jit(solution)/shard_map/ppermute | solution.py:30
  41.6 13.7 %collective-permute-start.6 = (bf16[112,1152]{1,0:T(8,128)(2,1)S(1)}, bf16[112,1152]{1,0:T(8,128)(2,1)S(1)}, u32[]{:S(2)}, u32[]{:S(2)}) collective-permute-start(bf16[112,1152]{1,0:T(8,128)(2,1)S(1)} %get-tuple-element.45), channel_id=1, source_target_pairs={{0,16},{16,0},{1,17},{17,1},{2,18},{18,2},{3,19},{19,3},{4,20},{20... | collective-permute-start | bytes 774152 | tf_op jit(solution)/shard_map/ppermute | solution.py:30
  46.3 10.1 %collective-permute-start.9 = (bf16[96,1152]{1,0:T(8,128)(2,1)S(1)}, bf16[96,1152]{1,0:T(8,128)(2,1)S(1)}, u32[]{:S(2)}, u32[]{:S(2)}) collective-permute-start(bf16[96,1152]{1,0:T(8,128)(2,1)S(1)} %get-tuple-element.56), channel_id=1, source_target_pairs={{0,1},{1,0},{2,3},{3,2},{4,5},{5,4},{6,7},{7,6},{8,9},{9,8},{10,11... | collective-permute-start | bytes 663560 | tf_op jit(solution)/shard_map/ppermute | solution.py:30
